TPU v7x, 128 devices: a whole 4x4x4 slice. The times are simulated.
128 devices in a mesh: rep: 16 (over y, x_lo, core), shard: 8 (over x_hi, z).
Axes of the slice: x: 4 (x_hi: 2, x_lo: 2; x = x_hi * 2 + x_lo), y: 4, z: 4, core: 2. Of those that a mesh axis runs over, the one named last changes fastest.
Arguments:
- resid: float32 [32768, 1536], P(('rep', 'shard')), may hold values from -6 to 6
- cotangent: float32 [32768, 1536], P(('rep', 'shard')), may hold values from -6 to 6
- first_length: int32 [16], P('rep'), may hold values from 128 to 1920, as said below
- norm_gain: float32 [1, 1536], replicated, may hold values from 0.5 to 1.5
- in_weight: bfloat16 [1, 1536, 6448], P(None, 'shard'), may hold values from -0.15625 to 0.15625
- conv_weight: float32 [1, 4, 3328], replicated, may hold values from -3 to 3
- conv_bias: float32 [1, 3328], replicated, may hold values from -2 to 2
- dt_bias: float32 [1, 48], replicated, may hold values from -1 to 1
- a_log: float32 [1, 48], replicated, may hold values from -6.2 to -2.8
- skip: float32 [1, 48], replicated, may hold values from 0.5 to 1.5
- gate_gain: float32 [1, 3072], replicated, may hold values from 0.5 to 1.5
- out_weight: bfloat16 [1, 3072, 1536], P(None, 'shard'), may hold values from -0.109375 to 0.109375
Outputs:
- mixed: float32 [32768, 1536], P(('rep', 'shard'))
- resid_grad: float32 [32768, 1536], P(('rep', 'shard'))
- norm_gain_grad: float32 [1, 1536], replicated
- in_weight_grad: float32 [1, 1536, 6448], P(None, 'shard')
- conv_weight_grad: float32 [1, 4, 3328], replicated
- conv_bias_grad: float32 [1, 3328], replicated
- dt_bias_grad: float32 [1, 48], replicated
- a_log_grad: float32 [1, 48], replicated
- skip_grad: float32 [1, 48], replicated
- gate_gain_grad: float32 [1, 3072], replicated
- out_weight_grad: float32 [1, 3072, 1536], P(None, 'shard')
Inputs may be any that keep to these rules, and one draw needn't show every extreme that they name: `first_length`: each group's first sequence is either shorter than 256 tokens or longer than 1792, so one of its two sequences covers every device of the group.
All inputs are finite; a program needn't handle non-finite values.
Results may differ from a plain program's by a relative error of at most 0.0095.
Values may be sent and summed in bfloat16 or wider, within the bound.
A program may use at most 256 MiB of HBM per device.

v0:
```python
import jax
import jax.numpy as jnp
from jax import lax
from jax.sharding import PartitionSpec as P

HEADS = 48
HEAD_DIM = 64
STATE = 128
CONV = 4
INNER = 3072
CONVCH = 3328


epsilon = 1e-05
highest = lax.Precision.HIGHEST


def shifted(value, axis, by):
    devices = lax.axis_size(axis)
    pairs = [(i, i + by) for i in range(devices) if 0 <= i + by < devices]
    return lax.ppermute(value, axis, pairs)


def entering(value, axis, join, neutral, backward):
    count, mine = (lax.axis_size(axis), lax.axis_index(axis))
    pieces = jax.tree.map(lambda part: lax.all_gather(part, axis), value)
    if backward:
        pieces = jax.tree.map(lambda part: part[::-1], pieces)
        mine = count - 1 - mine
    so_far = jax.tree.map(
        lambda part, zero: jnp.full_like(part, 0) + jnp.asarray(zero, part.dtype), value, neutral
    )

    def step(position, so_far):
        longer = join(so_far, jax.tree.map(lambda part: part[position], pieces))
        return jax.tree.map(lambda new, old: jnp.where(position < mine, new, old), longer, so_far)

    return lax.fori_loop(0, count - 1, step, so_far)


def rms_scale(stream, gain_vec):
    inv_scale = lax.rsqrt(jnp.mean(stream * stream, axis=-1, keepdims=True) + epsilon)
    return stream * inv_scale * gain_vec[None, :]


def pre_mix(projected, rim_rows, taps, conv_shift, step_bias, segment, rim_segment):
    length = projected.shape[0]
    gate_part = projected[:, :INNER]
    conv_input = projected[:, INNER : INNER + CONVCH]
    raw_step = projected[:, INNER + CONVCH :]
    padded = jnp.concatenate([rim_rows, conv_input], axis=0)
    all_segments = jnp.concatenate([rim_segment, segment], axis=0)
    convolved = jnp.zeros((length, CONVCH), jnp.float32) + conv_shift[None, :]
    for offset in range(CONV):
        same_seq = (all_segments[offset : offset + length] == segment).astype(jnp.float32)
        convolved = (
            convolved + taps[offset][None, :] * padded[offset : offset + length] * same_seq[:, None]
        )
    activated = jax.nn.silu(convolved)
    head_input = activated[:, :INNER].reshape(length, HEADS, HEAD_DIM)
    b_proj = activated[:, INNER : INNER + STATE]
    c_proj = activated[:, INNER + STATE :]
    step_size = jax.nn.softplus(raw_step + step_bias[None, :])
    return (gate_part, head_input, step_size, b_proj, c_proj)


def block_terms(head_input, step_size, b_proj, c_proj, rate_log, segment, segment_before):
    length = segment.shape[0]
    log_decay = -step_size * jnp.exp(rate_log)[None, :]
    cum_decay = jnp.cumsum(log_decay, axis=0)
    row_index = lax.broadcasted_iota(jnp.int32, (length, length), 0)
    col_index = lax.broadcasted_iota(jnp.int32, (length, length), 1)
    causal_mask = (row_index >= col_index) & (segment[:, None] == segment[None, :])
    decay_rows = cum_decay.T
    gap_decay = decay_rows[:, :, None] - decay_rows[:, None, :]
    weights_in = jnp.where(
        causal_mask[None], jnp.exp(jnp.where(causal_mask[None], gap_decay, 0.0)), 0.0
    )
    intersection = jnp.dot(c_proj, b_proj.T, precision=highest)
    scaled_input = head_input * step_size[:, :, None]
    local_out = jnp.einsum(
        "hij,jhp->ihp", weights_in * intersection[None], scaled_input, precision=highest
    )
    valid = (segment == segment_before).astype(jnp.float32)
    state_weight = jnp.exp(cum_decay) * valid[:, None]
    last_seg = segment[length - 1]
    tail = (
        jnp.exp(cum_decay[length - 1][None, :] - cum_decay)
        * (segment == last_seg).astype(jnp.float32)[:, None]
    )
    end_state = jnp.einsum("jh,jhp,jn->hpn", tail, scaled_input, b_proj, precision=highest)
    decay_total = jnp.exp(cum_decay[length - 1]) * (last_seg == segment_before).astype(jnp.float32)
    return (local_out, state_weight, end_state, decay_total)


def apply_state(local_out, state_weight, c_proj, state_in):
    return local_out + state_weight[:, :, None] * jnp.einsum(
        "hpn,in->ihp", state_in, c_proj, precision=highest
    )


def post_mix(mixer_out, head_input, gate_part, skip_vec, gain_vec):
    length = mixer_out.shape[0]
    with_skip = (mixer_out + skip_vec[None, :, None] * head_input).reshape(length, INNER)
    gated_out = with_skip * jax.nn.silu(gate_part)
    inv_scale = lax.rsqrt(jnp.mean(gated_out * gated_out, axis=1, keepdims=True) + epsilon)
    return gated_out * inv_scale * gain_vec[None, :]


def chain_combine(earlier, later):
    return (later[1][:, None, None] * earlier[0] + later[0], earlier[1] * later[1])


def local(
    resid,
    cotangent,
    first_length,
    norm_gain,
    in_weight,
    conv_weight,
    conv_bias,
    dt_bias,
    a_log,
    skip,
    gate_gain,
    out_weight,
):
    length = resid.shape[0]
    margin = CONV - 1
    begin = lax.axis_index("shard") * length
    positions = begin + lax.iota(jnp.int32, length)
    segment = (positions >= first_length[0]).astype(jnp.int32)
    rim_positions = begin - margin + lax.iota(jnp.int32, margin)
    rim_segment = (rim_positions >= first_length[0]).astype(jnp.int32)
    segment_before = rim_segment[margin - 1]
    layer_count = in_weight.shape[0]
    layer_index = 0
    w_in = lax.all_gather(in_weight[layer_index], "shard", axis=0, tiled=True)
    w_out = lax.all_gather(out_weight[layer_index], "shard", axis=0, tiled=True)
    normed_in = rms_scale(resid, norm_gain[layer_index]).astype(jnp.bfloat16)
    projected = jnp.dot(normed_in, w_in, preferred_element_type=jnp.float32).astype(jnp.bfloat16)
    rim_rows = shifted(projected[length - margin :, INNER : INNER + CONVCH], "shard", 1)
    gate_part, head_input, step_size, b_proj, c_proj = pre_mix(
        projected.astype(jnp.float32),
        rim_rows.astype(jnp.float32),
        conv_weight[layer_index],
        conv_bias[layer_index],
        dt_bias[layer_index],
        segment,
        rim_segment,
    )
    local_out, state_weight, end_state, decay_total = block_terms(
        head_input, step_size, b_proj, c_proj, a_log[layer_index], segment, segment_before
    )
    state_in, decay_before = entering(
        (end_state, decay_total),
        "shard",
        chain_combine,
        (jnp.zeros_like(end_state), jnp.ones_like(decay_total)),
        False,
    )
    mixer_out = apply_state(local_out, state_weight, c_proj, state_in)
    normed_out = post_mix(
        mixer_out, head_input, gate_part, skip[layer_index], gate_gain[layer_index]
    ).astype(jnp.bfloat16)
    stream_next = resid + jnp.dot(normed_out, w_out, preferred_element_type=jnp.float32)
    kept = [(resid, normed_in, projected, rim_rows, state_in, normed_out, w_in, w_out)]
    grad = cotangent
    in_grads = []
    out_grads = []
    small_grads = []
    for layer_index in reversed(range(layer_count)):
        stream_in, normed_in, projected, rim_rows, state_in, normed_out, w_in, w_out = kept[
            layer_index
        ]
        w_in, w_out = (
            lax.all_gather(in_weight[layer_index], "shard", axis=0, tiled=True),
            lax.all_gather(out_weight[layer_index], "shard", axis=0, tiled=True),
        )
        out_low = grad.astype(jnp.bfloat16)
        d_normed = jnp.einsum("td,id->ti", out_low, w_out, preferred_element_type=jnp.float32)

        def front(proj_in, rim_in, taps, conv_shift, step_bias):
            return pre_mix(proj_in, rim_in, taps, conv_shift, step_bias, segment, rim_segment)

        front_out, front_pull = jax.vjp(
            front,
            projected.astype(jnp.float32),
            rim_rows.astype(jnp.float32),
            conv_weight[layer_index],
            conv_bias[layer_index],
            dt_bias[layer_index],
        )
        gate_part, head_input, step_size, b_proj, c_proj = front_out

        def scan_terms(head_in, step_in, b_in, c_in, rate_in):
            return block_terms(head_in, step_in, b_in, c_in, rate_in, segment, segment_before)

        terms, terms_pull = jax.vjp(
            scan_terms, head_input, step_size, b_proj, c_proj, a_log[layer_index]
        )
        local_out, state_weight, end_state, decay_total = terms
        mixer_out, state_pull = jax.vjp(apply_state, local_out, state_weight, c_proj, state_in)
        unused_out, post_pull = jax.vjp(
            post_mix, mixer_out, head_input, gate_part, skip[layer_index], gate_gain[layer_index]
        )
        d_mixer, d_head_first, d_gate, d_skip, d_gate_gain = post_pull(d_normed)
        d_local, d_weight, d_c_first, d_state = state_pull(d_mixer)
        later_state, later_decay = entering(
            (d_state, decay_total),
            "shard",
            chain_combine,
            (jnp.zeros_like(d_state), jnp.ones_like(decay_total)),
            True,
        )
        d_total = jnp.sum(later_state * state_in, axis=(1, 2))
        d_head_second, d_step, d_b, d_c_second, d_rate = terms_pull(
            (d_local, d_weight, later_state, d_total)
        )
        d_proj, d_rim, d_taps, d_shift, d_step_bias = front_pull(
            (d_gate, d_head_first + d_head_second, d_step, d_b, d_c_first + d_c_second)
        )
        from_next = shifted(d_rim.astype(jnp.bfloat16), "shard", -1).astype(d_rim.dtype)
        d_proj = d_proj.at[length - margin :, INNER : INNER + CONVCH].add(from_next)
        proj_low = d_proj.astype(jnp.bfloat16)
        d_normed_in = jnp.einsum("tp,dp->td", proj_low, w_in, preferred_element_type=jnp.float32)
        unused_norm, norm_pull = jax.vjp(rms_scale, stream_in, norm_gain[layer_index])
        d_stream, d_norm_gain = norm_pull(d_normed_in)
        grad = grad + d_stream
        out_weight_part = jnp.einsum(
            "ti,td->id", normed_out, out_low, preferred_element_type=jnp.float32
        )
        in_weight_part = jnp.einsum(
            "td,tp->dp", normed_in, proj_low, preferred_element_type=jnp.float32
        )
        in_share, out_share = (
            lax.psum_scatter(in_weight_part, "shard", scatter_dimension=0, tiled=True),
            lax.psum_scatter(out_weight_part, "shard", scatter_dimension=0, tiled=True),
        )
        in_summed, out_summed = lax.psum((in_share, out_share), "rep")
        in_grads.insert(0, in_summed)
        out_grads.insert(0, out_summed)
        small_grads.insert(
            0, (d_norm_gain, d_taps, d_shift, d_step_bias, d_rate, d_skip, d_gate_gain)
        )
    stacked = tuple(
        (jnp.stack([entry[member] for entry in small_grads], axis=0) for member in range(7))
    )
    g_norm, g_taps, g_shift, g_step, g_rate, g_skip, g_gate = lax.psum(
        (stacked[0], stacked[1], stacked[2], stacked[3], stacked[4], stacked[5], stacked[6]),
        ("rep", "shard"),
    )
    return (
        stream_next,
        grad,
        g_norm,
        jnp.stack(in_grads, axis=0),
        g_taps,
        g_shift,
        g_step,
        g_rate,
        g_skip,
        g_gate,
        jnp.stack(out_grads, axis=0),
    )


def solution(mesh):
    return jax.shard_map(
        local,
        mesh=mesh,
        in_specs=(
            P(("rep", "shard"), None),
            P(("rep", "shard"), None),
            P("rep"),
            P(),
            P(None, "shard", None),
            P(),
            P(),
            P(),
            P(),
            P(),
            P(),
            P(None, "shard", None),
        ),
        out_specs=(
            P(("rep", "shard"), None),
            P(("rep", "shard"), None),
            P(),
            P(None, "shard", None),
            P(),
            P(),
            P(),
            P(),
            P(),
            P(),
            P(None, "shard", None),
        ),
        check_vma=False,
    )
```

profile of v0, /device:TPU:1, one launch (start us, length us, event | category | flops | bytes accessed | tf_op | source)
XLA Modules:
  0.0 1655.1 jit_solution(7300145434445623860)
XLA Ops:
  17.7 207.9 %all-gather.10.cloned.1.call-done = bf16[1,1536,6448]{2,1,0:T(8,128)(2,1)} async-done(((bf16[1,192,6448]{2,1,0:T(8,128)(2,1)}), bf16[1,1536,6448]{2,1,0:T(8,128)(2,1)}) %all-gather.10.cloned.1.call-update) | async-done | bytes 19808272 | tf_op jit(solution)/shard_map/all_gather | solution.py:138
  225.7 14.5 fusion.125
  253.5 10.1 fusion.35
  266.3 3.8 fusion.46
  271.1 14.9 all-gather.4
  287.4 127.4 %all-gather.12.cloned.1.call-done = f32[384,64,128]{2,1,0:T(8,128)} async-done(((f32[48,64,128]{2,1,0:T(8,128)}), f32[384,64,128]{2,1,0:T(8,128)}) %all-gather.12.cloned.1.call-update) | async-done | bytes 12582928 | tf_op jit(solution)/shard_map/all_gather | solution.py:26
  414.8 13.2 while.29
  431.7 14.2 fusion.38
  446.0 5.8 multiply_reduce_fusion.11
  451.8 79.8 %all-gather.14.cloned.1.call-done = bf16[1,3072,1536]{2,1,0:T(8,128)(2,1)} async-done(((bf16[1,384,1536]{2,1,0:T(8,128)(2,1)}), bf16[1,3072,1536]{2,1,0:T(8,128)(2,1)}) %all-gather.14.cloned.1.call-update) | async-done | bytes 9437200 | tf_op jit(solution)/shard_map/all_gather | solution.py:139
  531.6 8.6 multiply_reduce_fusion.6
  540.2 6.1 multiply_reduce_fusion.7
  548.1 3.8 fusion.42
  552.4 12.4 fusion.84
  565.4 21.3 %fusion.20 = (f32[48,256]{1,0:T(8,128)}, f32[48,256]{1,0:T(8,128)}, f32[256,256]{1,0:T(8,128)S(1)}) fusion(f32[256,256]{1,0:T(8,128)} %copy-done.29, f32[48,256]{1,0:T(8,128)} %get-tuple-element.319, pred[256,256]{1,0:T(8,128)(4,1)} %copy-done.41, f32[48,64,256]{2,1,0:T(8,128)} %bitcast.194, f32[256,48,64]{0,2,1:T(8,128)} %bitcast.189, ...), kind=kOutput, calls=%fused_computation.23 | convolution fusion | flops 2451218432 | bytes 7077888 | tf_op jit(solution)/shard_map/transpose(jvp(hij,jhp->ihp))/dot_general | solution.py:81
  593.6 101.4 %all-gather.16.cloned.1.call-done = f32[384,64,128]{2,1,0:T(8,128)} async-done(((f32[48,64,128]{2,1,0:T(8,128)}), f32[384,64,128]{2,1,0:T(8,128)}) %all-gather.16.cloned.1.call-update) | async-done | bytes 12582928 | tf_op jit(solution)/shard_map/all_gather | solution.py:26
  694.9 12.3 rev.7
  707.2 17.4 %while.30 = (s32[]{:T(128)}, f32[48,64,128]{2,1,0:T(8,128)S(1)}, s32[]{:T(128)}, f32[8,48]{1,0:T(8,128)}, f32[8,48,64,128]{3,2,1,0:T(8,128)}, /*index=5*/s32[]{:T(128)}, s32[]{:T(128)}) while((s32[]{:T(128)}, f32[48,64,128]{2,1,0:T(8,128)S(1)}, s32[]{:T(128)}, f32[8,48]{1,0:T(8,128)}, f32[8,48,64,128]{3,2,1,0:T(8,128)}, ...), condition=%wide.region_8.9_spmd.clone, body=%wide.region_7.8_spmd.clone.sunk | while | flops 1572868 | bytes 4719281 | solution.py:38
  724.7 3.7 fusion.88
  731.6 15.2 multiply_reduce_fusion.5
  746.9 11.5 multiply_reduce_fusion.3
  760.9 4.2 pad_add_fusion.1
  778.0 5.0 pad_add_fusion
  787.3 10.8 scatter-add.4
  798.1 19.5 %fusion.62 = f32[1536,6448]{1,0:T(8,128)} fusion(f32[256,6448]{0,1:T(8,128)} %scatter-add.4, f32[256,1536]{1,0:T(8,128)S(1)} %copy-done.7, f32[1536]{0:T(1024)S(1)} %copy-done.32, f32[256]{0:T(256)S(1)} %copy-done.52), kind=kOutput, calls=%fused_computation.94 | convolution fusion | flops 5073743872 | bytes 47799296 | tf_op jit(solution)/shard_map/td,tp->dp/dot_general | solution.py:233
  820.9 12.8 multiply_reduce_fusion.12
  834.4 70.4 %reduce-scatter.5.cloned.1.call-done = f32[384,1536]{1,0:T(8,128)} async-done(((f32[3072,1536]{1,0:T(8,128)}), f32[384,1536]{1,0:T(8,128)}) %reduce-scatter.5.cloned.1.call-update) | async-done | bytes 2359312 | tf_op jit(solution)/shard_map/reduce_scatter | solution.py:238
  904.8 406.5 %reduce-scatter.3.cloned.1.call-done = f32[192,6448]{1,0:T(8,128)} async-done(((f32[1536,6448]{1,0:T(8,128)}), f32[192,6448]{1,0:T(8,128)}) %reduce-scatter.3.cloned.1.call-update) | async-done | bytes 4952080 | tf_op jit(solution)/shard_map/reduce_scatter | solution.py:237
  1313.3 8.1 fusion.48
  1322.9 139.0 %all-reduce.21.cloned.1.call-done = (f32[1,1536]{1,0:T(1,128)}, f32[1,4,3328]{2,1,0:T(4,128)}, f32[1,3328]{1,0:T(1,128)}, f32[1,48]{1,0:T(1,128)}, f32[1,48]{1,0...) async-done(((f32[1,1536]{1,0:T(1,128)}, f32[1,4,3328]{2,1,0:T(4,128)}, f32[1,3328]{1,0:T(1,128)}, f32[1,48]{1,0:T(1,128)}, f32[1,48]{1,0:T(1,128)}, ...) | async-done | bytes 85584 | tf_op jit(solution)/shard_map/psum | solution.py:249
  1461.9 174.6 %all-reduce.23.cloned.1.call-done = (f32[1,192,6448]{2,1,0:T(8,128)}, f32[1,384,1536]{2,1,0:T(8,128)}) async-done(((f32[1,192,6448]{2,1,0:T(8,128)}, f32[1,384,1536]{2,1,0:T(8,128)}), (f32[1,192,6448]{2,1,0:T(8,128)}, f32[1,384,1536]{2,1,0:T(8,128)})) %all-reduce.23.cloned.1.call-update) | async-done | bytes 7311376 | tf_op jit(solution)/shard_map/psum | solution.py:240
  1637.9 5.2 copy.177
  (285 shorter events, 106.2 us)
Async XLA Ops:
  7.2 218.5 %all-gather.10.cloned.1.call-start = ((), (), s32[]{:S(2)}) async-start(), calls=%async_computation.4 | async-start | bytes 22560768 | tf_op jit(solution)/shard_map/all_gather | solution.py:138
  7.9 406.8 %all-gather.12.cloned.1.call-start = ((), (), s32[]{:S(2)}) async-start(), calls=%async_computation.5 | async-start | bytes 14155776 | tf_op jit(solution)/shard_map/all_gather | solution.py:26
  9.3 230.8 %copy-start.31 = (f32[1536]{0:T(1024)}, f32[1536]{0:T(1024)S(1)}, u32[]{:S(2)}) copy-start(f32[1536]{0:T(1024)S(1)} %reduce.7) | copy-start | bytes 18436
  14.6 233.5 %copy-start.55 = (f32[256]{0:T(256)}, f32[256]{0:T(256)S(1)}, u32[]{:S(2)}) copy-start(f32[256]{0:T(256)S(1)} %get-tuple-element.328) | copy-start | bytes 3076
  14.6 233.5 %copy-start.64 = (f32[256]{0:T(256)}, f32[256]{0:T(256)S(1)}, u32[]{:S(2)}) copy-start(f32[256]{0:T(256)S(1)} %get-tuple-element.329) | copy-start | bytes 3076
  17.1 227.8 %copy-start.71 = (f32[48]{0:T(128)}, f32[48]{0:T(128)S(1)}, u32[]{:S(2)}) copy-start(f32[48]{0:T(128)S(1)} %exponential_bitcast_fusion) | copy-start | bytes 580
  17.1 223.0 %copy-start.51 = (f32[256]{0:T(256)}, f32[256]{0:T(256)S(1)}, u32[]{:S(2)}) copy-start(f32[256]{0:T(256)S(1)} %fusion.116) | copy-start | bytes 3076
  17.7 227.2 %copy-start.70 = (f32[1,48]{1,0:T(1,128)S(1)}, f32[1,48]{1,0:T(1,128)}, u32[]{:S(2)}) copy-start(f32[1,48]{1,0:T(1,128)} %param.25) | copy-start | bytes 580
  242.5 8.6 collective-permute-start
  270.1 261.5 %all-gather.14.cloned.1.call-start = ((), (), s32[]{:S(2)}) async-start(), calls=%async_computation.6 | async-start | bytes 10616832 | tf_op jit(solution)/shard_map/all_gather | solution.py:139
  270.9 424.1 %all-gather.16.cloned.1.call-start = ((), (), s32[]{:S(2)}) async-start(), calls=%async_computation.7 | async-start | bytes 14155776 | tf_op jit(solution)/shard_map/all_gather | solution.py:26
  271.0 160.6 %copy-start.41 = (pred[256,256]{1,0:T(8,128)(4,1)}, pred[256,256]{1,0:T(8,128)(4,1)S(1)}, u32[]{:S(2)}) copy-start(pred[256,256]{1,0:T(8,128)(4,1)S(1)} %fusion.87) | copy-start | bytes 196612
  287.3 144.3 %copy-start.29 = (f32[256,256]{1,0:T(8,128)}, f32[256,256]{1,0:T(8,128)S(1)}, u32[]{:S(2)}) copy-start(f32[256,256]{1,0:T(8,128)S(1)} %fusion.97) | copy-start | bytes 786436
  431.7 14.3 copy-start.19
  446.0 85.6 %copy-start.17 = (f32[256,1536]{1,0:T(8,128)S(1)}, f32[256,1536]{1,0:T(8,128)}, u32[]{:S(2)}) copy-start(f32[256,1536]{1,0:T(8,128)} %param.19) | copy-start | bytes 4718596
  446.0 85.6 %copy-start.27 = (f32[1,3072]{1,0:T(1,128)S(1)}, f32[1,3072]{1,0:T(1,128)}, u32[]{:S(2)}) copy-start(f32[1,3072]{1,0:T(1,128)} %param.28) | copy-start | bytes 36868
  451.8 100.5 %copy-start.49 = (f32[256]{0:T(256)}, f32[256]{0:T(256)S(1)}, u32[]{:S(2)}) copy-start(f32[256]{0:T(256)S(1)} %fusion.117) | copy-start | bytes 3076
  551.9 352.9 %reduce-scatter.5.cloned.1.call-start = ((), (), s32[]{:S(2)}) async-start(), calls=%async_computation.3 | async-start | bytes 21233664 | tf_op jit(solution)/shard_map/reduce_scatter | solution.py:238
  564.8 746.6 %reduce-scatter.3.cloned.1.call-start = ((), (), s32[]{:S(2)}) async-start(), calls=%async_computation.2 | async-start | bytes 45121536 | tf_op jit(solution)/shard_map/reduce_scatter | solution.py:237
  565.4 23.2 %copy-start.13 = (f32[256,3072]{0,1:T(8,128)S(1)}, f32[256,3072]{0,1:T(8,128)}, u32[]{:S(2)}) copy-start(f32[256,3072]{0,1:T(8,128)} %copy-done.12) | copy-start | bytes 9437188
  565.4 23.2 %copy-start.26 = (f32[256,48]{0,1:T(8,128)S(1)}, f32[256,48]{0,1:T(8,128)}, u32[]{:S(2)}) copy-start(f32[256,48]{0,1:T(8,128)} %get-tuple-element.317) | copy-start | bytes 147460
  731.5 15.3 copy-start.5
  731.6 15.3 copy-start.23
  731.6 15.3 copy-start.59
  731.6 15.3 copy-start.60
  731.6 15.3 copy-start.61
  746.8 22.0 %copy-start.35 = (f32[256,48]{0,1:T(8,128)}, f32[256,48]{0,1:T(8,128)S(1)}, u32[]{:S(2)}) copy-start(f32[256,48]{0,1:T(8,128)S(1)} %get-tuple-element.261) | copy-start | bytes 147460
  775.2 7.9 collective-permute-start.1
  784.6 13.5 copy-start.32
  784.6 13.5 copy-start.52
  817.6 644.3 %all-reduce.21.cloned.1.call-start = ((), (), s32[]{:S(2)}) async-start(), calls=%async_computation.8 | async-start | bytes 173056 | tf_op jit(solution)/shard_map/psum | solution.py:249
  834.3 802.2 %all-reduce.23.cloned.1.call-start = ((), (), s32[]{:S(2)}) async-start(), calls=%async_computation.9 | async-start | bytes 14745600 | tf_op jit(solution)/shard_map/psum | solution.py:240
  (58 other events, 298.4 us)
Sparse Core Ops, SparseCore 0:
  10.3 215.2 all-gather.9
  270.2 144.4 all-gather.11
  417.1 114.4 all-gather.13
  552.0 142.8 all-gather.15
  698.7 205.9 reduce-scatter.4
  908.7 402.5 reduce-scatter.2
  1319.6 142.2 all-reduce.20
  1464.5 171.9 all-reduce.22
where the time goes:
time: 1670 us; the launch traced here: 1660 us
  waiting for transfers between devices  1310 us (78%)
  matrix products  153 us (9%)
  other arithmetic  90.3 us (5%)
  local copies, waits for them, and re-layouts  66.2 us (4%)
  between operations  17.5 us (1%)
    reduce_scatter x1, waiting for transfers between devices, local(): lax.psum_scatter(in_weight_part, 'shard', scatter_dimension=0, tiled=True)  407 us
    all_gather x2, waiting for transfers between devices, entering(): pieces = jax.tree.map(lambda part: lax.all_gather(part, axis), value)  229 us
    all_gather x1, waiting for transfers between devices, local(): w_in = lax.all_gather(in_weight[layer_index], 'shard', axis=0, tiled=True)  208 us
    psum x1, waiting for transfers between devices, local(): in_summed, out_summed = lax.psum((in_share, out_share), 'rep')  175 us
    psum x1, waiting for transfers between devices, local(): lax.psum((stacked[0], stacked[1], stacked[2], stacked[3], stacked[4], sta...  139 us
    all_gather x1, waiting for transfers between devices, local(): w_out = lax.all_gather(out_weight[layer_index], 'shard', axis=0, tiled=True)  79.8 us
    reduce_scatter x1, waiting for transfers between devices, local(): lax.psum_scatter(out_weight_part, 'shard', scatter_dimension=0, tiled=True)  70.4 us
    dot_general x3, matrix products, block_terms(): jnp.einsum('hij,jhp->ihp', weights_in * intersection[None], scaled_input,...  50.8 us
  transfers between devices with their start and end apart: 10, of which 8 were waited for; matrix products, arithmetic and copies ran while one was open for 14% of the time, Pallas kernels for 0%

commit v1 on v0

v1 whole, which is shorter than its diff:
```python
import jax
import jax.numpy as jnp
from jax import lax
from jax.experimental import pallas as pl
from jax.experimental.pallas import tpu as pltpu
from jax.sharding import PartitionSpec as P

HEADS = 48
HEAD_DIM = 64
STATE = 128
CONV = 4
INNER = 3072
CONVCH = 3328
MODEL = 1536
SHARDS = 8
OWN = HEADS // SHARDS
CH = OWN * HEAD_DIM
XBC = CH + 2 * STATE
COLS = 2 * CH + 2 * STATE + 128
TOK = 256
GROUP = TOK * SHARDS
L = 128
NB = GROUP // L
HALO = 16
RESET = -200.0

epsilon = 1e-05
F32 = jnp.float32
BF = jnp.bfloat16


def mm(a, b, dims=((1,), (0,))):
    return lax.dot_general(a, b, (dims, ((), ())), preferred_element_type=F32)


def split(v, parts):
    out = []
    for _ in range(parts):
        piece = v.astype(BF)
        out.append(piece)
        v = v - piece.astype(F32)
    return out


def mm_left(ones, v, parts):
    return sum(mm(ones, piece) for piece in split(v, parts))


def mm_right(v, ones, parts):
    return sum(mm(piece, ones) for piece in split(v, parts))


def iota2(shape, dim):
    return lax.broadcasted_iota(jnp.int32, shape, dim)


def head_columns():
    return (iota2((CH, 128), 0) // HEAD_DIM == iota2((CH, 128), 1)).astype(BF)


def spread(per_head):
    lane = iota2((per_head.shape[0], 128), 1)
    tiles = []
    for pair in range(OWN // 2):
        left = per_head[:, 2 * pair : 2 * pair + 1]
        right = per_head[:, 2 * pair + 1 : 2 * pair + 2]
        tiles.append(jnp.where(lane < HEAD_DIM, left, right))
    return jnp.concatenate(tiles, axis=1)


def head_rows(cum_rows, at):
    pieces = [
        jnp.broadcast_to(cum_rows[h : h + 1, at : at + 1], (HEAD_DIM, 1)) for h in range(OWN)
    ]
    return jnp.exp(jnp.concatenate(pieces, axis=0))


def tap_mask(row, first_len, back):
    past = row - first_len
    return jnp.where((past >= 0) & (past < back), 0.0, 1.0)


def block_front(rows, r0, first_len, taps, shift, step_bias, rate_log):
    xbc = rows[:, CH : CH + XBC].astype(F32)
    row = r0 + iota2((L, 1), 0)
    conv = jnp.broadcast_to(shift, (L, XBC))
    for k in range(CONV):
        back = CONV - 1 - k
        term = taps[k : k + 1] * xbc[HALO - back : HALO - back + L]
        if back:
            term = term * tap_mask(row, first_len, back)
        conv = conv + term
    gate = rows[HALO:, :CH].astype(F32)
    raw = rows[HALO:, CH + XBC :].astype(F32) + step_bias
    step = jnp.maximum(raw, 0.0) + jnp.log1p(jnp.exp(-jnp.abs(raw)))
    log_decay = -step * jnp.exp(rate_log)
    with_reset = log_decay + jnp.where(row == first_len, RESET, 0.0)
    lower = (iota2((L, L), 0) >= iota2((L, L), 1)).astype(BF)
    cum = mm_left(lower, with_reset, 3)
    return gate, xbc, conv, raw, step, log_decay, cum


def sigmoid(v):
    return 1.0 / (1.0 + jnp.exp(-v))


def pair_mix(weights, value, dims=((1,), (0,))):
    lane = iota2((L, 128), 1)
    tiles = []
    for pair in range(OWN // 2):
        part = value[:, 128 * pair : 128 * pair + 128]
        tiles.append(
            jnp.where(
                lane < HEAD_DIM,
                mm(weights[2 * pair], part, dims),
                mm(weights[2 * pair + 1], part, dims),
            )
        )
    return jnp.concatenate(tiles, axis=1)


def decay_weights(cum, cum_rows):
    causal = iota2((L, L), 0) >= iota2((L, L), 1)
    out = []
    for h in range(OWN):
        gap = cum[:, h : h + 1] - cum_rows[h : h + 1, :]
        out.append(jnp.exp(jnp.where(causal, gap, -1e30)))
    return out


def to_row(column):
    return jnp.transpose(jnp.broadcast_to(column, (L, L)))[0:1]


def to_column(row):
    return jnp.transpose(jnp.broadcast_to(row, (L, L)))


def forward_kernel(
    first_ref, proj, d_normed, taps, shift, step_bias, rate_log, skip, gain, y_out, states, sums, carry
):
    first_len = first_ref[0]
    carry[...] = jnp.zeros_like(carry)

    def block(b, unused):
        r0 = pl.multiple_of(b * L, L)
        rows = proj[pl.ds(r0, HALO + L), :]
        gate, xbc, conv, raw, step, log_decay, cum = block_front(
            rows, r0, first_len, taps[...], shift[...], step_bias[...], rate_log[...]
        )
        act = conv * sigmoid(conv)
        x = act[:, :CH]
        b_low = act[:, CH : CH + STATE].astype(BF)
        c_low = act[:, CH + STATE :].astype(BF)
        cum_rows = jnp.transpose(cum)
        scores = mm(c_low, b_low, ((1,), (1,)))
        scaled = x * spread(step)
        scaled_low = scaled.astype(BF)
        weights = [(w * scores).astype(BF) for w in decay_weights(cum, cum_rows)]
        state = carry[...]
        states[b] = state
        y = pair_mix(weights, scaled_low)
        y = y + jnp.exp(spread(cum)) * mm(c_low, state.astype(BF), ((1,), (1,)))
        tail = jnp.exp(spread(cum[L - 1 : L] - cum))
        carry[...] = head_rows(cum_rows, L - 1) * state + mm(
            (tail * scaled).astype(BF), b_low, ((0,), (0,))
        )
        y = y + skip[...] * x
        y_out[pl.ds(r0, L), :] = y
        gated = y * (gate * sigmoid(gate))
        normed = gain[...] * d_normed[pl.ds(r0, L), :]
        sums[0, pl.ds(b, 1), :] = to_row(jnp.sum(gated * gated, axis=1, keepdims=True))
        sums[1, pl.ds(b, 1), :] = to_row(jnp.sum(gated * normed, axis=1, keepdims=True))
        return unused

    lax.fori_loop(0, NB, block, 0)
    states[NB] = carry[...]


def backward_kernel(
    first_ref,
    proj,
    d_normed,
    taps,
    shift,
    step_bias,
    rate_log,
    skip,
    gain,
    y_in,
    states,
    sums,
    d_proj,
    small,
    heads,
    carry,
    late,
):
    first_len = first_ref[0]
    carry[...] = jnp.zeros_like(carry)
    late[...] = jnp.zeros_like(late)
    small[...] = jnp.zeros_like(small)
    heads[...] = jnp.zeros_like(heads)
    upper = (iota2((L, L), 1) >= iota2((L, L), 0)).astype(BF)
    columns = head_columns()

    def block(at, unused):
        b = NB - 1 - at
        r0 = pl.multiple_of(b * L, L)
        rows = proj[pl.ds(r0, HALO + L), :]
        gate, xbc, conv, raw, step, log_decay, cum = block_front(
            rows, r0, first_len, taps[...], shift[...], step_bias[...], rate_log[...]
        )
        sig = sigmoid(conv)
        act = conv * sig
        x = act[:, :CH]
        b_low = act[:, CH : CH + STATE].astype(BF)
        c_low = act[:, CH + STATE :].astype(BF)
        cum_rows = jnp.transpose(cum)
        scores = mm(c_low, b_low, ((1,), (1,)))
        step_wide = spread(step)
        scaled = x * step_wide
        scaled_low = scaled.astype(BF)
        decays = decay_weights(cum, cum_rows)

        y = y_in[pl.ds(r0, L), :]
        sig_gate = sigmoid(gate)
        silu_gate = gate * sig_gate
        gated = y * silu_gate
        inv = lax.rsqrt(sums[0, pl.ds(b, 1), :] * (1.0 / INNER) + epsilon)
        back = inv * inv * inv * sums[1, pl.ds(b, 1), :] * (1.0 / INNER)
        inv = jnp.concatenate([to_column(inv)] * (CH // 128), axis=1)
        back = jnp.concatenate([to_column(back)] * (CH // 128), axis=1)
        dn = d_normed[pl.ds(r0, L), :]
        d_gated = inv * gain[...] * dn - gated * back
        dy = d_gated * silu_gate
        d_gate = d_gated * y * (sig_gate + silu_gate * (1.0 - sig_gate))
        dy_low = dy.astype(BF)

        state = states[b]
        end_state = states[b + 1]
        d_state = carry[...]
        state_low = state.astype(BF)
        d_state_low = d_state.astype(BF)
        enter = jnp.exp(spread(cum))
        tail = jnp.exp(spread(cum[L - 1 : L] - cum))
        lane = iota2((L, 128), 1)
        d_scores = jnp.zeros((L, L), F32)
        weights = []
        for h in range(OWN):
            part = slice(128 * (h // 2), 128 * (h // 2) + 128)
            mine = (lane < HEAD_DIM) if h % 2 == 0 else (lane >= HEAD_DIM)
            d_weight = mm(
                dy_low[:, part],
                jnp.where(mine, scaled[:, part], 0.0).astype(BF),
                ((1,), (1,)),
            )
            d_scores = d_scores + d_weight * decays[h]
            weights.append((decays[h] * scores).astype(BF))
        d_scores_low = d_scores.astype(BF)
        d_scaled = pair_mix(weights, dy_low, ((0,), (0,)))
        d_scaled = d_scaled + tail * mm(b_low, d_state_low, ((1,), (1,)))
        enter_dy = (enter * dy).astype(BF)
        d_c = mm(d_scores_low, b_low) + mm(enter_dy, state_low)
        d_b = mm(d_scores_low, c_low, ((0,), (0,))) + mm((tail * scaled).astype(BF), d_state_low)

        ssm = y - skip[...] * x
        d_cum = mm_right(
            dy_low.astype(F32) * ssm - scaled_low.astype(F32) * d_scaled, columns, 3
        )
        through = jnp.zeros((1, 128), F32)
        for piece in split(end_state * d_state, 3):
            through = through + jnp.sum(
                mm(piece, columns, ((0,), (0,))), axis=0, keepdims=True
            )
        d_cum = d_cum + jnp.where(iota2((L, 1), 0) == L - 1, through, 0.0)
        d_log = mm_left(upper, d_cum, 3)
        rate = jnp.exp(rate_log[...])
        d_step = mm_right(d_scaled * x, columns, 3) - rate * d_log
        d_raw = d_step * sigmoid(raw)
        d_x = d_scaled * step_wide + skip[...] * dy

        carry[...] = head_rows(cum_rows, L - 1) * d_state + mm(enter_dy, c_low, ((0,), (0,)))

        d_act = jnp.concatenate([d_x, d_b, d_c], axis=1)
        d_conv = d_act * (sig + act * (1.0 - sig))
        row = r0 + iota2((L + 8, 1), 0)
        longer = jnp.concatenate([d_conv, late[...]], axis=0)
        late[...] = d_conv[:8]
        d_xbc = jnp.zeros((L, XBC), F32)
        for k in range(CONV):
            ahead = CONV - 1 - k
            masked = longer
            if ahead:
                masked = longer * tap_mask(row, first_len, ahead)
            d_xbc = d_xbc + taps[k : k + 1, :] * masked[ahead : ahead + L]
            small[k : k + 1, :] += jnp.sum(
                masked[:L] * xbc[HALO - ahead : HALO - ahead + L], axis=0, keepdims=True
            )
        small[4:5, :] += jnp.sum(d_conv, axis=0, keepdims=True)
        small[5:6, :CH] += jnp.sum(dy * x, axis=0, keepdims=True)
        small[6:7, :CH] += jnp.sum(dn * gated * inv, axis=0, keepdims=True)
        heads[0:1, :] += jnp.sum(d_raw, axis=0, keepdims=True)
        heads[1:2, :] += jnp.sum(d_log * log_decay, axis=0, keepdims=True)
        d_proj[pl.ds(r0, L), :] = jnp.concatenate([d_gate, d_xbc, d_raw], axis=1).astype(BF)
        return unused

    lax.fori_loop(0, NB, block, 0)


VM = pl.BlockSpec(memory_space=pltpu.VMEM)
SM = pl.BlockSpec(memory_space=pltpu.SMEM)
LIMIT = 56 << 20


def rms_scale(stream, gain_vec):
    inv_scale = lax.rsqrt(jnp.mean(stream * stream, axis=-1, keepdims=True) + epsilon)
    return stream * inv_scale * gain_vec[None, :]


def own_lanes(vector, begin, count, width):
    part = lax.dynamic_slice(vector, (begin,), (count,))
    return jnp.pad(part, (0, width - count))[None]


def local(
    resid,
    cotangent,
    first_length,
    norm_gain,
    in_weight,
    conv_weight,
    conv_bias,
    dt_bias,
    a_log,
    skip,
    gate_gain,
    out_weight,
):
    me = lax.axis_index("shard")
    w = in_weight[0]
    rows = w.shape[0]
    normed_in = rms_scale(resid, norm_gain[0]).astype(BF)
    out_low = cotangent.astype(BF)
    wide = jnp.concatenate(
        [w[:, :INNER].reshape(rows, SHARDS, CH), w[:, INNER : 2 * INNER].reshape(rows, SHARDS, CH)],
        axis=2,
    ).transpose(1, 0, 2)
    wide = lax.all_to_all(wide, "shard", 0, 0).reshape(MODEL, 2 * CH)
    narrow = lax.all_gather(w[:, 2 * INNER :], "shard", axis=0, tiled=True)
    w_step = lax.dynamic_slice(narrow, (0, 2 * STATE + me * OWN), (MODEL, OWN))
    w_in = jnp.concatenate(
        [wide, narrow[:, : 2 * STATE], jnp.pad(w_step, ((0, 0), (0, 128 - OWN)))], axis=1
    )
    w_out = out_weight[0]
    all_in = lax.all_gather(normed_in, "shard", axis=0, tiled=True)
    all_low = lax.all_gather(out_low, "shard", axis=0, tiled=True)
    proj = jnp.dot(all_in, w_in, preferred_element_type=F32).astype(BF)
    proj = jnp.pad(proj, ((HALO, 0), (0, 0)))
    d_normed = mm(all_low, w_out, ((1,), (1,)))

    taps = jnp.concatenate(
        [lax.dynamic_slice(conv_weight[0], (0, me * CH), (CONV, CH)), conv_weight[0][:, INNER:]],
        axis=1,
    )
    shift = jnp.concatenate(
        [lax.dynamic_slice(conv_bias[0], (me * CH,), (CH,)), conv_bias[0][INNER:]]
    )[None]
    step_bias = own_lanes(dt_bias[0], me * OWN, OWN, 128)
    rate_log = own_lanes(a_log[0], me * OWN, OWN, 128)
    skip_wide = jnp.repeat(lax.dynamic_slice(skip[0], (me * OWN,), (OWN,)), HEAD_DIM)[None]
    gain = lax.dynamic_slice(gate_gain[0], (me * CH,), (CH,))[None]
    params = (taps, shift, step_bias, rate_log, skip_wide, gain)

    y, states, sums = pl.pallas_call(
        forward_kernel,
        out_shape=(
            jax.ShapeDtypeStruct((GROUP, CH), F32),
            jax.ShapeDtypeStruct((NB + 1, CH, STATE), F32),
            jax.ShapeDtypeStruct((2, NB, L), F32),
        ),
        in_specs=[SM] + [VM] * 8,
        out_specs=(VM,) * 3,
        scratch_shapes=[pltpu.VMEM((CH, STATE), F32)],
        compiler_params=pltpu.CompilerParams(vmem_limit_bytes=LIMIT),
    )(first_length, proj, d_normed, *params)
    sums = lax.psum(sums, "shard")

    inv = lax.rsqrt(sums[0].reshape(GROUP, 1) * (1.0 / INNER) + epsilon)
    normed_out = (y * jax.nn.silu(proj[HALO:, :CH].astype(F32)) * inv * gain).astype(BF)
    mixed_part = mm(normed_out, w_out).astype(BF)
    mixed = resid + lax.psum_scatter(mixed_part, "shard", scatter_dimension=0, tiled=True).astype(F32)
    out_part = mm(normed_out, all_low, ((0,), (0,)))

    d_proj, small, heads = pl.pallas_call(
        backward_kernel,
        out_shape=(
            jax.ShapeDtypeStruct((GROUP, COLS), BF),
            jax.ShapeDtypeStruct((8, XBC), F32),
            jax.ShapeDtypeStruct((8, 128), F32),
        ),
        in_specs=[SM] + [VM] * 11,
        out_specs=(VM,) * 3,
        scratch_shapes=[pltpu.VMEM((CH, STATE), F32), pltpu.VMEM((8, XBC), F32)],
        compiler_params=pltpu.CompilerParams(vmem_limit_bytes=LIMIT),
    )(first_length, proj, d_normed, *params, y, states, sums)

    in_part = mm(all_in, d_proj, ((0,), (0,)))
    d_in_part = mm(d_proj, w_in, ((1,), (1,))).astype(BF)
    d_in = lax.psum_scatter(d_in_part, "shard", scatter_dimension=0, tiled=True).astype(F32)
    unused, norm_pull = jax.vjp(rms_scale, resid, norm_gain[0])
    d_stream, d_norm_gain = norm_pull(d_in)
    grad = cotangent + d_stream

    wide_part = in_part[:, : 2 * CH].astype(BF).reshape(SHARDS, rows, 2 * CH)
    wide_sum = lax.all_to_all(wide_part, "shard", 0, 0).transpose(1, 0, 2)
    narrow_part = jnp.zeros((MODEL, 2 * STATE + HEADS), F32)
    narrow_part = narrow_part.at[:, : 2 * STATE].set(in_part[:, 2 * CH : 2 * CH + 2 * STATE])
    narrow_part = lax.dynamic_update_slice(
        narrow_part, in_part[:, 2 * CH + 2 * STATE :][:, :OWN], (0, 2 * STATE + me * OWN)
    ).astype(BF)
    narrow_sum = lax.psum_scatter(narrow_part, "shard", scatter_dimension=0, tiled=True)
    in_share = jnp.concatenate(
        [wide_sum[:, :, :CH].reshape(rows, INNER), wide_sum[:, :, CH:].reshape(rows, INNER), narrow_sum],
        axis=1,
    )
    in_grad, out_grad = lax.psum((in_share, out_part.astype(BF)), "rep")

    def place(own, rest, total):
        full = jnp.zeros((own.shape[0], total), F32)
        full = lax.dynamic_update_slice(full, own, (0, me * own.shape[1]))
        return full if rest is None else full.at[:, total - rest.shape[1] :].set(rest)

    conv_parts = place(small[:5, :CH], small[:5, CH:], CONVCH)
    skip_part = jnp.sum(small[5, :CH].reshape(OWN, HEAD_DIM), axis=1)[None]
    per_head = place(jnp.concatenate([heads[:2, :OWN], skip_part], axis=0), None, HEADS)
    gain_part = place(small[6:7, :CH], None, INNER)
    g_conv, g_head, g_gain, g_norm = lax.psum(
        (conv_parts, per_head, gain_part, d_norm_gain[None]), ("rep", "shard")
    )
    return (
        mixed,
        grad,
        g_norm,
        in_grad.astype(F32)[None],
        g_conv[:CONV][None],
        g_conv[4:5],
        g_head[0:1],
        g_head[1:2],
        g_head[2:3],
        g_gain,
        out_grad.astype(F32)[None],
    )


def solution(mesh):
    rows = P(("rep", "shard"), None)
    weight = P(None, "shard", None)
    return jax.shard_map(
        local,
        mesh=mesh,
        in_specs=(rows, rows, P("rep"), P(), weight, P(), P(), P(), P(), P(), P(), weight),
        out_specs=(rows, rows, P(), weight, P(), P(), P(), P(), P(), P(), weight),
        check_vma=False,
    )
```

time: 1670 us -> 923 us (0.55)
  waiting for transfers between devices: 1310 us -> 538 us
  blocking collectives: 14.9 us -> 171 us
  matrix products: 153 us -> 59.6 us
  Pallas kernels: 0 us -> 67.3 us
  other arithmetic: 90.3 us -> 24.6 us
  local copies, waits for them, and re-layouts: 66.2 us -> 32.9 us
    all_gather x4 -> x2, waiting for transfers between devices: 516 us -> 106 us  [the longest x1 73.9 us: local(): all_low = lax.all_gather(out_low, 'shard', axis=0, tiled=True)]
    reduce_scatter x2 -> x3, waiting for transfers between devices: 477 us -> 176 us  [the longest x1 96.8 us: local(): lax.psum_scatter(d_in_part, 'shard', scatter_dimension=0, tiled=True)]
    psum x0 -> x2, blocking collectives: none -> 104 us  [the longest x1 73.3 us: local(): lax.psum((conv_parts, per_head, gain_part, d_norm_gain[None]), ('rep', 's...]
    dot_general x18 -> x6, matrix products: 153 us -> 59.6 us  [the longest x5 48.5 us: mm(): return lax.dot_general(a, b, (dims, ((), ())), preferred_element_type=F32)]
    psum x2, waiting for transfers between devices: 314 us -> 245 us  [the longest x1 129 us: local(): in_grad, out_grad = lax.psum((in_share, out_part.astype(BF)), 'rep')]
    pallas_call x0 -> x2, Pallas kernels: none -> 67.3 us  [the longest x1 44.1 us: local(): pl.pallas_call(backward_kernel, out_shape=(jax.ShapeDtypeStruct((GROUP, C...]
    all_gather x1, blocking collectives: 14.9 us -> 66.7 us  [local(): narrow = lax.all_gather(w[:, 2 * INNER:], 'shard', axis=0, tiled=True)]
    select_n x14 -> x0, other arithmetic: 25.1 us -> none  [step(): jnp.where(position < mine, new, old)]
  transfers between devices with their start and end apart: 10 -> 9, of which waited for: 8 -> 8; matrix products, arithmetic and copies ran while one was open for 14% -> 9% of each run, Pallas kernels for 0% -> 0%
where the time goes in v1:
time: 923 us; the launch traced here: 922 us
  waiting for transfers between devices  538 us (58%)
  blocking collectives  171 us (19%)
  Pallas kernels  67.3 us (7%)
  matrix products  59.6 us (6%)
  local copies, waits for them, and re-layouts  32.9 us (4%)
  other arithmetic  24.6 us (3%)
  between operations  15.1 us (2%)
  starting transfers between devices  13.7 us (1%)
    psum x1, waiting for transfers between devices, local(): in_grad, out_grad = lax.psum((in_share, out_part.astype(BF)), 'rep')  129 us
    psum x1, waiting for transfers between devices, local(): lax.psum((conv_parts, per_head, gain_part, d_norm_gain[None]), ('rep', 's...  116 us
    reduce_scatter x1, waiting for transfers between devices, local(): lax.psum_scatter(d_in_part, 'shard', scatter_dimension=0, tiled=True)  96.8 us
    all_gather x1, waiting for transfers between devices, local(): all_low = lax.all_gather(out_low, 'shard', axis=0, tiled=True)  73.9 us
    psum x1, blocking collectives, local(): lax.psum((conv_parts, per_head, gain_part, d_norm_gain[None]), ('rep', 's...  73.3 us
    all_gather x1, blocking collectives, local(): narrow = lax.all_gather(w[:, 2 * INNER:], 'shard', axis=0, tiled=True)  66.7 us
    reduce_scatter x1, waiting for transfers between devices, local(): lax.psum_scatter(narrow_part, 'shard', scatter_dimension=0, tiled=True)  53.1 us
    dot_general x5, matrix products, mm(): return lax.dot_general(a, b, (dims, ((), ())), preferred_element_type=F32)  48.5 us
  transfers between devices with their start and end apart: 9, of which 8 were waited for; matrix products, arithmetic and copies ran while one was open for 9% of the time, Pallas kernels for 0%

profile of v1, /device:TPU:1, one launch (start us, length us, event | category | flops | bytes accessed | tf_op | source)
XLA Modules:
  0.0 921.5 jit_solution(10512975754343859283)
XLA Ops:
  7.2 1.7 multiply_reduce_fusion
  9.7 2.5 multiply_convert_fusion
  13.3 1.8 fusion.37
  17.0 8.5 all-to-all-start
  26.5 66.7 %all_gather.10 = bf16[1536,304]{1,0:T(8,128)(2,1)S(1)} all-gather(bf16[192,304]{1,0:T(8,128)(2,1)S(1)} %slice.135), channel_id=1, replica_groups=mesh['rep'=16,'shard'=8] {'shard'}, dimensions={0}, use_global_device_ids=true | all-gather | bytes 1050624 | tf_op jit(solution)/shard_map/all_gather | solution.py:350
  97.9 1.9 fusion.36
  101.2 31.9 %all-gather.3.cloned.1.call-done = bf16[2048,1536]{1,0:T(8,128)(2,1)} async-done(((bf16[256,1536]{1,0:T(8,128)(2,1)}), bf16[2048,1536]{1,0:T(8,128)(2,1)}) %all-gather.3.cloned.1.call-update) | async-done | bytes 6291472 | tf_op jit(solution)/shard_map/all_gather | solution.py:356
  133.1 11.1 %convolution_convert_fusion.2 = bf16[2048,1152]{1,0:T(8,128)(2,1)S(1)} fusion(bf16[2048,1536]{1,0:T(8,128)(2,1)} %all-gather.3.cloned.1.call-done, bf16[1536,6]{1,0:T(8,128)(2,1)S(1)} %constant_dynamic-slice_fusion.5, bf16[1536,256]{1,0:T(8,128)(2,1)S(1)} %slice.136, bf16[1536,768]{1,0:T(8,128)(2,1)} %bitcast.2), kind=kOutput, calls=%fused_computation.2 | convolution fusion | flops 7264272384 | bytes 14174208 | tf_op jit(solution)/shard_map/dot_general | solution.py:358
  144.2 2.1 copy-done.4
  146.3 2.6 pad.21.proj
  148.9 73.9 %all-gather.5.cloned.1.call-done = bf16[2048,1536]{1,0:T(8,128)(2,1)} async-done(((bf16[256,1536]{1,0:T(8,128)(2,1)}), bf16[2048,1536]{1,0:T(8,128)(2,1)}) %all-gather.5.cloned.1.call-update) | async-done | bytes 6291472 | tf_op jit(solution)/shard_map/all_gather | solution.py:357
  222.8 7.9 fusion.16.d_normed
  230.8 23.2 %shard_map.203 = (f32[2048,384]{1,0:T(8,128)}, f32[17,384,128]{2,1,0:T(8,128)}, f32[2,16,128]{2,1,0:T(8,128)}) custom-call(s32[1]{0:T(128)S(6)} %copy.58.first_ref, bf16[2064,1152]{1,0:T(8,128)(2,1)} %pad.21.proj, f32[2048,384]{1,0:T(8,128)} %fusion.16.d_normed, f32[4,640]{1,0:T(4,128)} %pad_maximum_fusion.taps, f32[1,640]{1,0:T(1,128)} %broadcast_in_dim.47.shift, ...), custom_call_target="tpu_custom_call" | custom-call | tf_op jit(solution)/shard_map/pallas_call | solution.py:375
  253.9 30.6 %psum.49.sums = f32[2,16,128]{2,1,0:T(8,128)} all-reduce(f32[2,16,128]{2,1,0:T(8,128)} %get-tuple-element.42), channel_id=1, replica_groups=mesh['rep'=16,'shard'=8] {'shard'}, use_global_device_ids=true, to_apply=%region_1.2 | all-reduce | flops 4096 | bytes 32768 | tf_op jit(solution)/shard_map/psum | solution.py:387
  284.6 44.1 %shard_map.204 = (bf16[2048,1152]{1,0:T(8,128)(2,1)}, f32[8,640]{1,0:T(8,128)}, f32[8,128]{1,0:T(8,128)}) custom-call(s32[1]{0:T(128)S(6)} %copy.58.first_ref, bf16[2064,1152]{1,0:T(8,128)(2,1)} %pad.21.proj, f32[2048,384]{1,0:T(8,128)} %fusion.16.d_normed, f32[4,640]{1,0:T(4,128)} %pad_maximum_fusion.taps, f32[1,640]{1,0:T(1,128)} %broadcast_in_dim.47.shift, ...), custom_call_target="tpu_custom_call" | custom-call | tf_op jit(solution)/shard_map/pallas_call | solution.py:395
  328.7 10.3 %fusion.39 = bf16[1536,1152]{0,1:T(8,128)(2,1)S(1)} fusion(bf16[2048,1536]{1,0:T(8,128)(2,1)S(1)} %bitcast.65, bf16[2048,1152]{1,0:T(8,128)(2,1)} %get-tuple-element.44), kind=kOutput, calls=%fused_computation.77 | convolution fusion | flops 7247757312 | bytes 14548992 | tf_op jit(solution)/shard_map/dot_general | solution.py:33
  338.9 1.8 copy-done.2
  344.9 2.4 copy.38
  347.3 4.7 all-to-all-start.1
  356.7 8.2 fusion.9
  364.9 10.8 %all-to-all-done.1 = bf16[8,192,768]{2,1,0:T(8,128)(2,1)S(1)} async-done(((bf16[8,192,768]{2,1,0:T(8,128)(2,1)}), bf16[8,192,768]{2,1,0:T(8,128)(2,1)S(1)}, u32[]{:S(2)}, u32[]{:S(2)}) %all-to-all-start.1) | async-done | bytes 2359328 | tf_op jit(solution)/shard_map/all_to_all | solution.py:416
  376.5 53.1 %reduce-scatter.10.cloned.1.call-done = bf16[192,304]{1,0:T(8,128)(2,1)} async-done(((bf16[1536,304]{1,0:T(8,128)(2,1)}), bf16[192,304]{1,0:T(8,128)(2,1)}) %reduce-scatter.10.cloned.1.call-update) | async-done | bytes 116752 | tf_op jit(solution)/shard_map/reduce_scatter | solution.py:422
  429.6 2.5 maximum_bitcast_fusion
  433.4 13.1 %convolution_convert_fusion = bf16[2048,1536]{1,0:T(8,128)(2,1)} fusion(bf16[2048,1152]{1,0:T(8,128)(2,1)} %get-tuple-element.44, bf16[1536,6]{1,0:T(8,128)(2,1)S(1)} %copy-done.9, bf16[1536,256]{1,0:T(8,128)(2,1)S(1)} %copy-done.7, bf16[1536,768]{1,0:T(8,128)(2,1)} %bitcast.2), kind=kOutput, calls=%fused_computation | convolution fusion | flops 7265058816 | bytes 14174208 | tf_op jit(solution)/shard_map/dot_general | solution.py:33
  447.2 9.0 convolution_convert_fusion.1
  458.1 116.4 %all-reduce.10.cloned.1.call-done = f32[5,3328]{1,0:T(8,128)} async-done(((f32[5,3328]{1,0:T(8,128)}), f32[5,3328]{1,0:T(8,128)}) %all-reduce.10.cloned.1.call-update) | async-done | bytes 66576 | tf_op jit(solution)/shard_map/psum | solution.py:438
  577.5 128.6 %all-reduce.12.cloned.1.call-done = (bf16[1,192,6448]{2,1,0:T(8,128)(2,1)}, bf16[1,384,1536]{2,1,0:T(8,128)(2,1)}) async-done(((bf16[1,192,6448]{2,1,0:T(8,128)(2,1)}, bf16[1,384,1536]{2,1,0:T(8,128)(2,1)}), (bf16[1,192,6448]{2,1,0:T(8,128)(2,1)}, bf16[1,384,1536]{2,1,0:T(8,128)(2,1)})) %all-reduce.12.cloned.1.call-update) | async-done | bytes 3655696 | tf_op jit(solution)/shard_map/psum | solution.py:427
  706.1 4.4 broadcast_in_dim.53
  712.2 96.8 %reduce-scatter.8.cloned.1.call-done = bf16[256,1536]{1,0:T(8,128)(2,1)} async-done(((bf16[2048,1536]{1,0:T(8,128)(2,1)}), bf16[256,1536]{1,0:T(8,128)(2,1)}) %reduce-scatter.8.cloned.1.call-update) | async-done | bytes 786448 | tf_op jit(solution)/shard_map/reduce_scatter | solution.py:410
  810.6 73.3 %all-reduce.5 = (f32[1,1536]{1,0:T(1,128)}, f32[3,48]{1,0:T(4,128)S(1)}, f32[1,3072]{1,0:T(1,128)}) all-reduce(f32[1,1536]{1,0:T(1,128)S(1)} %reshape.137, f32[3,48]{1,0:T(4,128)S(1)} %dynamic_update_slice.14, f32[1,3072]{1,0:T(1,128)S(1)} %get-tuple-element.62), channel_id=1, replica_groups=mesh['rep'=16,'shard'=8] {'rep','shard'}, use_global_device_ids=true, to_apply=%region_6.7 | all-reduce | flops 4752 | bytes 38016 | tf_op jit(solution)/shard_map/psum | solution.py:438
  884.5 26.2 %reduce-scatter.6.cloned.1.call-done = bf16[256,1536]{1,0:T(8,128)(2,1)} async-done(((bf16[2048,1536]{1,0:T(8,128)(2,1)}), bf16[256,1536]{1,0:T(8,128)(2,1)}) %reduce-scatter.6.cloned.1.call-update) | async-done | bytes 786448 | tf_op jit(solution)/shard_map/reduce_scatter | solution.py:392
  910.7 4.0 fusion.14
  (104 shorter events, 30.5 us)
Async XLA Ops:
  7.2 215.6 %copy-start = (bf16[1,384,1536]{2,1,0:T(8,128)(2,1)S(1)}, bf16[1,384,1536]{2,1,0:T(8,128)(2,1)}, u32[]{:S(2)}) copy-start(bf16[1,384,1536]{2,1,0:T(8,128)(2,1)} %param.27) | copy-start | bytes 3538948
  7.2 5.1 copy-start.3
  7.2 125.9 %all-gather.3.cloned.1.call-start = ((), (), s32[]{:S(2)}) async-start(), calls=%async_computation.5 | async-start | bytes 7077888 | tf_op jit(solution)/shard_map/all_gather | solution.py:356
  12.2 210.6 %all-gather.5.cloned.1.call-start = ((), (), s32[]{:S(2)}) async-start(), calls=%async_computation.6 | async-start | bytes 7077888 | tf_op jit(solution)/shard_map/all_gather | solution.py:357
  17.0 77.0 %copy-start.12 = (f32[1,3328]{1,0:T(1,128)S(1)}, f32[1,3328]{1,0:T(1,128)}, u32[]{:S(2)}) copy-start(f32[1,3328]{1,0:T(1,128)} %param.22) | copy-start | bytes 39940
  17.0 77.0 %slice-start.1 = ((f32[1,3328]{1,0:T(1,128)}), f32[1,256]{1,0:T(1,128)S(1)}, s32[]{:S(2)}) async-start(f32[1,3328]{1,0:T(1,128)} %param.22), calls=%async_computation.13 | async-start | bytes 2048 | tf_op jit(solution)/shard_map/slice | solution.py:367
  17.0 77.6 %copy-start.16 = (f32[1,48]{1,0:T(1,128)S(1)}, f32[1,48]{1,0:T(1,128)}, u32[]{:S(2)}) copy-start(f32[1,48]{1,0:T(1,128)} %param.25) | copy-start | bytes 580
  17.0 79.7 %copy-start.14 = (f32[1,48]{1,0:T(1,128)S(1)}, f32[1,48]{1,0:T(1,128)}, u32[]{:S(2)}) copy-start(f32[1,48]{1,0:T(1,128)} %param.23) | copy-start | bytes 580
  17.0 79.7 %copy-start.15 = (f32[1,48]{1,0:T(1,128)S(1)}, f32[1,48]{1,0:T(1,128)}, u32[]{:S(2)}) copy-start(f32[1,48]{1,0:T(1,128)} %param.24) | copy-start | bytes 580
  17.0 84.2 %all-to-all-start = ((bf16[8,192,768]{2,1,0:T(8,128)(2,1)}), bf16[8,192,768]{2,1,0:T(8,128)(2,1)}, u32[]{:S(2)}, u32[]{:S(2)}) async-start(bf16[8,192,768]{2,1,0:T(8,128)(2,1)} %maximum_bitcast_fusion.1), calls=%async_computation | async-start | bytes 4718592 | tf_op jit(solution)/shard_map/all_to_all | solution.py:349
  25.5 404.1 %reduce-scatter.10.cloned.1.call-start = ((), (), s32[]{:S(2)}) async-start(), calls=%async_computation.10 | async-start | bytes 1327104 | tf_op jit(solution)/shard_map/reduce_scatter | solution.py:422
  93.3 50.9 %copy-start.6 = (bf16[1536,256]{1,0:T(8,128)(2,1)}, bf16[1536,256]{1,0:T(8,128)(2,1)S(1)}, u32[]{:S(2)}) copy-start(bf16[1536,256]{1,0:T(8,128)(2,1)S(1)} %slice.136) | copy-start | bytes 2359300
  101.2 43.0 %copy-start.8 = (bf16[1536,6]{1,0:T(8,128)(2,1)}, bf16[1536,6]{1,0:T(8,128)(2,1)S(1)}, u32[]{:S(2)}) copy-start(bf16[1536,6]{1,0:T(8,128)(2,1)S(1)} %constant_dynamic-slice_fusion.5) | copy-start | bytes 55300
  144.2 2.1 copy-start.4
  230.8 97.9 %slice-start.2 = ((s8[6291456]{0:T(1024)(128)(4,1)}), s8[2097152]{0:T(1024)(128)(4,1)S(1)}, s32[]{:S(2)}) async-start(s8[6291456]{0:T(1024)(128)(4,1)} %bitcast.64), calls=%async_computation.14 | async-start | bytes 4194304
  284.5 44.1 %slice-start.3 = ((s8[6291456]{0:T(1024)(128)(4,1)}), s8[4194304]{0:T(1024)(128)(4,1)S(1)}, s32[]{:S(2)}) async-start(s8[6291456]{0:T(1024)(128)(4,1)} %bitcast.64), calls=%async_computation.15 | async-start | bytes 8388608
  338.9 1.8 copy-start.2
  343.2 1.7 slice-start
  347.3 28.4 %all-to-all-start.1 = ((bf16[8,192,768]{2,1,0:T(8,128)(2,1)}), bf16[8,192,768]{2,1,0:T(8,128)(2,1)S(1)}, u32[]{:S(2)}, u32[]{:S(2)}) async-start(bf16[8,192,768]{2,1,0:T(8,128)(2,1)} %bitcast.54), calls=%async_computation.3 | async-start | bytes 4718592 | tf_op jit(solution)/shard_map/all_to_all | solution.py:416
  352.0 222.5 %all-reduce.10.cloned.1.call-start = ((), (), s32[]{:S(2)}) async-start(), calls=%async_computation.9 | async-start | bytes 212992 | tf_op jit(solution)/shard_map/psum | solution.py:438
  355.3 350.8 %all-reduce.12.cloned.1.call-start = ((), (), s32[]{:S(2)}) async-start(), calls=%async_computation.11 | async-start | bytes 7372800 | tf_op jit(solution)/shard_map/psum | solution.py:427
  356.1 0.6 copy-start.10
  432.1 1.1 copy-start.7
  432.1 1.2 copy-start.9
  432.2 376.8 %reduce-scatter.8.cloned.1.call-start = ((), (), s32[]{:S(2)}) async-start(), calls=%async_computation.8 | async-start | bytes 7077888 | tf_op jit(solution)/shard_map/reduce_scatter | solution.py:410
  446.5 0.7 copy-start.11
  446.5 0.7 copy-start.13
  446.5 464.2 %reduce-scatter.6.cloned.1.call-start = ((), (), s32[]{:S(2)}) async-start(), calls=%async_computation.7 | async-start | bytes 7077888 | tf_op jit(solution)/shard_map/reduce_scatter | solution.py:392
  706.1 4.4 copy-start.5
  710.5 98.5 %copy-start.1 = (f32[256,1536]{1,0:T(8,128)S(1)}, f32[256,1536]{1,0:T(8,128)}, u32[]{:S(2)}) copy-start(f32[256,1536]{1,0:T(8,128)} %param.16) | copy-start | bytes 4718596
Sparse Core Ops, SparseCore 0:
  12.4 120.7 all-gather.2
  136.0 86.7 all-gather.4
  343.4 86.1 reduce-scatter.9
  434.2 140.2 all-reduce.9
  577.7 128.3 all-reduce.11
  709.8 99.1 reduce-scatter.7
  812.8 97.8 reduce-scatter.5

commit v2 on v1

--- a/solution.py
+++ b/solution.py
@@ -16,12 +16,16 @@
 OWN = HEADS // SHARDS
 CH = OWN * HEAD_DIM
 XBC = CH + 2 * STATE
+HALF = 640
 COLS = 2 * CH + 2 * STATE + 128
+BC = 2 * STATE
 TOK = 256
 GROUP = TOK * SHARDS
 L = 128
 NB = GROUP // L
 HALO = 16
+PIECE = 48
+MESH = pl.DeviceIdType.MESH
 RESET = -200.0
 
 epsilon = 1e-05
@@ -136,45 +140,326 @@
     return jnp.transpose(jnp.broadcast_to(row, (L, L)))
 
 
-def forward_kernel(
-    first_ref, proj, d_normed, taps, shift, step_bias, rate_log, skip, gain, y_out, states, sums, carry
+def forward_block(b, first_len, proj, taps, shift, step_bias, rate_log, skip, y_out, states, sums, carry):
+    r0 = pl.multiple_of(b * L, L)
+    rows = proj[pl.ds(r0, HALO + L), :]
+    gate, xbc, conv, raw, step, log_decay, cum = block_front(
+        rows, r0, first_len, taps, shift, step_bias, rate_log
+    )
+    act = conv * sigmoid(conv)
+    x = act[:, BC:]
+    b_low = act[:, :STATE].astype(BF)
+    c_low = act[:, STATE:BC].astype(BF)
+    cum_rows = jnp.transpose(cum)
+    scores = mm(c_low, b_low, ((1,), (1,)))
+    scaled = x * spread(step)
+    scaled_low = scaled.astype(BF)
+    weights = [(w * scores).astype(BF) for w in decay_weights(cum, cum_rows)]
+    state = carry[...]
+    states[b] = state
+    y = pair_mix(weights, scaled_low)
+    y = y + jnp.exp(spread(cum)) * mm(c_low, state.astype(BF), ((1,), (1,)))
+    tail = jnp.exp(spread(cum[L - 1 : L] - cum))
+    carry[...] = head_rows(cum_rows, L - 1) * state + mm(
+        (tail * scaled).astype(BF), b_low, ((0,), (0,))
+    )
+    y = y + skip * x
+    y_out[pl.ds(r0, L), :] = y
+    gated = y * (gate * sigmoid(gate))
+    sums[pl.ds(b, 1), :] = to_row(jnp.sum(gated * gated, axis=1, keepdims=True))
+
+
+def place_of():
+    rep, me = lax.axis_index("rep"), lax.axis_index("shard")
+    hi, z = me // 4, lax.rem(me, 4)
+    left = hi * 4 + lax.rem(z + 3, 4)
+    right = hi * 4 + lax.rem(z + 1, 4)
+    far = hi * 4 + lax.rem(z + 2, 4)
+    across = lax.rem(me + 4, 8)
+    return rep, me, left, right, far, across
+
+
+def other_side(block):
+    return lax.rem(block + 4, 8)
+
+
+def enter(rep, me):
+    barrier = pltpu.get_barrier_semaphore()
+    peers = [(rep, lax.rem(me + o, SHARDS)) for o in range(1, SHARDS)]
+    peers += [(lax.rem(rep + 4 * o, 16), me) for o in range(1, 4)]
+    peers.append((rep + 1 - 2 * lax.rem(rep, 2), me))
+    for peer in peers:
+        pl.semaphore_signal(barrier, inc=1, device_id=peer, device_id_type=MESH)
+    pl.semaphore_wait(barrier, len(peers))
+
+
+class Gather:
+    def __init__(self, blocks, send, recv):
+        self.blocks, self.send, self.recv = blocks, send, recv
+        self.rep, self.me, self.left, self.right, self.far, self.across = place_of()
+
+    def move(self, channel, block, to, rows=None):
+        ref = self.blocks.at[block] if rows is None else self.blocks.at[block, pl.ds(rows, TOK // 2)]
+        return pltpu.make_async_remote_copy(
+            src_ref=ref,
+            dst_ref=ref,
+            send_sem=self.send.at[channel],
+            recv_sem=self.recv.at[channel],
+            device_id=(self.rep, to),
+            device_id_type=MESH,
+        )
+
+    def outgoing(self, channel):
+        me, left, right, across = self.me, self.left, self.right, self.across
+        return (
+            lambda: self.move(0, me, right),
+            lambda: self.move(1, me, left),
+            lambda: self.move(2, me, across),
+            lambda: self.move(3, left, right, 0),
+            lambda: self.move(4, right, left, TOK // 2),
+            lambda: self.move(5, across, right),
+            lambda: self.move(6, across, left),
+            lambda: self.move(7, self.far, across, 0),
+            lambda: self.move(8, self.far, across, TOK // 2),
+        )[channel]()
+
+    def incoming(self, channel):
+        left, right, far, across = self.left, self.right, self.far, self.across
+        return (
+            lambda: self.move(0, left, left),
+            lambda: self.move(1, right, right),
+            lambda: self.move(2, across, across),
+            lambda: self.move(3, far, left, 0),
+            lambda: self.move(4, far, right, TOK // 2),
+            lambda: self.move(5, other_side(left), left),
+            lambda: self.move(6, other_side(right), right),
+            lambda: self.move(7, other_side(far), across, 0),
+            lambda: self.move(8, other_side(far), across, TOK // 2),
+        )[channel]()
+
+    def start(self, *channels):
+        for channel in channels:
+            self.outgoing(channel).start()
+
+    def arrived(self, *channels):
+        for channel in channels:
+            self.incoming(channel).wait_recv()
+
+    def sent(self):
+        for channel in range(9):
+            self.outgoing(channel).wait_send()
+
+
+def own_heads(vector, me):
+    pick = (iota2((HEADS, 128), 0) == iota2((HEADS, 128), 1) + me * OWN) & (
+        iota2((HEADS, 128), 1) < OWN
+    )
+    wide = jnp.broadcast_to(vector, (8, HEADS))
+    return mm_right(wide, pick.astype(BF), 3)[0:1]
+
+
+def own_channels(vector, me):
+    pick = iota2((HEADS, CH), 0) == iota2((HEADS, CH), 1) // HEAD_DIM + me * OWN
+    wide = jnp.broadcast_to(vector, (8, HEADS))
+    return mm_right(wide, pick.astype(BF), 3)[0:1]
+
+
+def own_slices(me, conv_weight, conv_bias):
+    own = pl.ds(pl.multiple_of(me * CH, 128), CH)
+    taps = jnp.concatenate([conv_weight[:, INNER:], conv_weight[:, own]], axis=1)
+    shift = jnp.concatenate([conv_bias[:, INNER:], conv_bias[:, own]], axis=1)
+    return taps, shift
+
+
+def front_kernel(
+    first_ref, resid, cotangent, w_in, narrow, w_out, norm_gain, conv_weight, conv_bias, dt_bias,
+    a_log, skip, gate_gain, x_out, low_out, w_all_out, proj_out, y_out, states_out, normed_out, sums_out,
+    x_all, low_all, w_all, proj, y, states, d_normed, sums, carry, stage, taps, shift,
+    x_send, x_recv, low_send, low_recv, piece_send, piece_recv, y_send, y_recv, core_send, core_recv,
+    sum_send, sum_recv, here,
 ):
+    rep, me, left, right, far, across = place_of()
+    core = lax.rem(rep, 2)
+    along_y = rep // 4
     first_len = first_ref[0]
+    load_resid = pltpu.make_async_copy(resid, stage.at[0], here.at[0])
+    load_cot = pltpu.make_async_copy(cotangent, stage.at[1], here.at[1])
+    load_resid.start()
+    load_cot.start()
+    enter(rep, me)
+
+    own_rows = pl.ds(pl.multiple_of(along_y * PIECE, 16), PIECE)
+
+    def landing(block):
+        return pl.ds(pl.multiple_of(block * 192 + along_y * PIECE, 16), PIECE)
+
+    def weight_pieces(to, make):
+        wide = pl.ds(pl.multiple_of(core * INNER + to * CH, 128), CH)
+        half = pl.ds(pl.multiple_of(core * BC, 128), BC)
+        make(w_in.at[own_rows, wide], w_all.at[core, landing(me), pl.ds(0, CH)])
+        make(narrow.at[own_rows, half], w_all.at[core, landing(me), pl.ds(CH, BC)])
+
+    for o in range(1, SHARDS):
+        to = lax.rem(me + o, SHARDS)
+        weight_pieces(
+            to,
+            lambda src, dst: pltpu.make_async_remote_copy(
+                src_ref=src, dst_ref=dst, send_sem=piece_send.at[o], recv_sem=piece_recv.at[o],
+                device_id=(rep, to), device_id_type=MESH,
+            ).start(),
+        )
+    weight_pieces(me, lambda src, dst: pltpu.make_async_copy(src, dst, here.at[2]).start())
+
+    load_resid.wait()
+    rows = stage[0]
+    scale = lax.rsqrt(jnp.mean(rows * rows, axis=1, keepdims=True) + epsilon)
+    x_all[me] = (rows * scale * norm_gain[...]).astype(BF)
+    gather_x = Gather(x_all, x_send, x_recv)
+    gather_x.start(0, 1, 2)
+    load_cot.wait()
+    low_all[me] = stage[1].astype(BF)
+    gather_low = Gather(low_all, low_send, low_recv)
+
+    taps_now, shift_now = own_slices(me, conv_weight, conv_bias)
+    taps[...] = taps_now
+    shift[...] = shift_now
+    proj[pl.ds(0, HALO), :] = jnp.zeros((HALO, COLS), BF)
     carry[...] = jnp.zeros_like(carry)
 
-    def block(b, unused):
-        r0 = pl.multiple_of(b * L, L)
-        rows = proj[pl.ds(r0, HALO + L), :]
-        gate, xbc, conv, raw, step, log_decay, cum = block_front(
-            rows, r0, first_len, taps[...], shift[...], step_bias[...], rate_log[...]
+    pltpu.make_async_copy(
+        w_all.at[core, landing(me)], w_all.at[core, landing(me)], here.at[2]
+    ).wait()
+    for o in range(1, SHARDS):
+        source = lax.rem(me + SHARDS - o, SHARDS)
+        piece = w_all.at[core, landing(source)]
+        pltpu.make_async_remote_copy(
+            src_ref=piece, dst_ref=piece, send_sem=piece_send.at[o], recv_sem=piece_recv.at[o],
+            device_id=(rep, source), device_id_type=MESH,
+        ).wait()
+    for o in range(1, 4):
+        for block in range(SHARDS):
+            piece = w_all.at[core, landing(block)]
+            pltpu.make_async_remote_copy(
+                src_ref=piece, dst_ref=piece, send_sem=y_send.at[o], recv_sem=y_recv.at[o],
+                device_id=(lax.rem(rep + 4 * o, 16), me), device_id_type=MESH,
+            ).start()
+    gather_x.arrived(0)
+    gather_x.start(3)
+    gather_x.arrived(1)
+    gather_x.start(4)
+    gather_x.arrived(2)
+    gather_x.start(5, 6)
+    gather_x.arrived(3)
+    gather_x.start(7)
+    gather_x.arrived(4)
+    gather_x.start(8)
+    gather_low.start(0, 1, 2)
+    for o in range(1, 4):
+        quarter = w_all.at[core, pl.ds(0, SHARDS * PIECE)]
+        pltpu.make_async_remote_copy(
+            src_ref=quarter, dst_ref=quarter, send_sem=y_send.at[o], recv_sem=y_recv.at[o],
+            device_id=(lax.rem(rep + 4 * o, 16), me), device_id_type=MESH,
+        ).wait()
+
+    def halves(which):
+        return pltpu.make_async_remote_copy(
+            src_ref=w_all.at[which], dst_ref=w_all.at[which], send_sem=core_send.at[0],
+            recv_sem=core_recv.at[0], device_id=(rep + 1 - 2 * core, me), device_id_type=MESH,
         )
-        act = conv * sigmoid(conv)
-        x = act[:, :CH]
-        b_low = act[:, CH : CH + STATE].astype(BF)
-        c_low = act[:, CH + STATE :].astype(BF)
-        cum_rows = jnp.transpose(cum)
-        scores = mm(c_low, b_low, ((1,), (1,)))
-        scaled = x * spread(step)
-        scaled_low = scaled.astype(BF)
-        weights = [(w * scores).astype(BF) for w in decay_weights(cum, cum_rows)]
-        state = carry[...]
-        states[b] = state
-        y = pair_mix(weights, scaled_low)
-        y = y + jnp.exp(spread(cum)) * mm(c_low, state.astype(BF), ((1,), (1,)))
-        tail = jnp.exp(spread(cum[L - 1 : L] - cum))
-        carry[...] = head_rows(cum_rows, L - 1) * state + mm(
-            (tail * scaled).astype(BF), b_low, ((0,), (0,))
+
+    halves(core).start()
+    halves(1 - core).wait_recv()
+    halves(core).wait_send()
+    pick = (iota2((128, 128), 0) == iota2((128, 128), 1) + me * OWN) & (iota2((128, 128), 1) < OWN)
+    w_all[1, :, CH : CH + 128] = mm(w_all[1, :, CH : CH + 128], pick.astype(BF)).astype(BF)
+
+    side = (me // 4) * 4
+
+    def project(at, unused):
+        rows = x_all[at]
+        begin = pl.multiple_of(HALO + at * TOK, 16)
+        proj[pl.ds(begin, TOK), :HALF] = mm(rows, w_all[0]).astype(BF)
+        proj[pl.ds(begin, TOK), HALF:] = mm(rows, w_all[1, :, : CH + 128]).astype(BF)
+        return unused
+
+    lax.fori_loop(side, side + 4, project, 0)
+    gather_low.arrived(0)
+    gather_low.start(3)
+    gather_low.arrived(1)
+    gather_low.start(4)
+    gather_x.arrived(5, 6, 7, 8)
+    lax.fori_loop(4 - side, 8 - side, project, 0)
+    gather_low.arrived(2)
+    gather_low.start(5, 6)
+
+    step_bias = own_heads(dt_bias[...], me)
+    rate_log = own_heads(a_log[...], me)
+    skip_wide = own_channels(skip[...], me)
+
+    def scan(b, unused):
+        @pl.when(b == 6)
+        def relay_a():
+            gather_low.arrived(3)
+            gather_low.start(7)
+
+        @pl.when(b == 8)
+        def relay_b():
+            gather_low.arrived(4)
+            gather_low.start(8)
+
+        forward_block(
+            b, first_len, proj, taps[...], shift[...], step_bias, rate_log, skip_wide, y, states,
+            sums.at[me, 0], carry,
         )
-        y = y + skip[...] * x
-        y_out[pl.ds(r0, L), :] = y
-        gated = y * (gate * sigmoid(gate))
-        normed = gain[...] * d_normed[pl.ds(r0, L), :]
-        sums[0, pl.ds(b, 1), :] = to_row(jnp.sum(gated * gated, axis=1, keepdims=True))
-        sums[1, pl.ds(b, 1), :] = to_row(jnp.sum(gated * normed, axis=1, keepdims=True))
         return unused
 
-    lax.fori_loop(0, NB, block, 0)
+    lax.fori_loop(0, NB, scan, 0)
     states[NB] = carry[...]
+
+    gain = gate_gain[:, pl.ds(pl.multiple_of(me * CH, 128), CH)]
+
+    def normed(at, unused):
+        begin = pl.multiple_of(at * TOK, TOK)
+        dn = mm(low_all[at], w_out[...], ((1,), (1,)))
+        d_normed[pl.ds(begin, TOK), :] = dn
+        gate = proj[pl.ds(HALO + begin, TOK), :CH].astype(F32)
+        gated = y[pl.ds(begin, TOK), :] * (gate * sigmoid(gate))
+        both = jnp.sum(gated * gain * dn, axis=1, keepdims=True)
+        sums[me, 1, pl.ds(2 * at, 1), :] = to_row(both[:L])
+        sums[me, 1, pl.ds(2 * at + 1, 1), :] = to_row(both[L:])
+        return unused
+
+    lax.fori_loop(side, side + 4, normed, 0)
+    gather_low.arrived(5, 6, 7, 8)
+    lax.fori_loop(4 - side, 8 - side, normed, 0)
+
+    def sum_copy(o, slot, to):
+        return pltpu.make_async_remote_copy(
+            src_ref=sums.at[slot], dst_ref=sums.at[slot], send_sem=sum_send.at[o],
+            recv_sem=sum_recv.at[o], device_id=(rep, to), device_id_type=MESH,
+        )
+
+    for o in range(1, SHARDS):
+        sum_copy(o, me, lax.rem(me + o, SHARDS)).start()
+    for o in range(1, SHARDS):
+        source = lax.rem(me + SHARDS - o, SHARDS)
+        sum_copy(o, source, source).wait_recv()
+    for o in range(1, SHARDS):
+        sum_copy(o, me, lax.rem(me + o, SHARDS)).wait_send()
+    total = sums[0]
+    for slot in range(1, SHARDS):
+        total = total + sums[slot]
+    sums_out[...] = total
+    gather_x.sent()
+    gather_low.sent()
+    keep = (
+        (x_all, x_out), (low_all, low_out), (w_all, w_all_out), (proj, proj_out), (y, y_out),
+        (states, states_out), (d_normed, normed_out),
+    )
+    for at, (src, dst) in enumerate(keep):
+        pltpu.make_async_copy(src, dst, here.at[3 + at]).start()
+    for at, (src, dst) in enumerate(keep):
+        pltpu.make_async_copy(src, dst, here.at[3 + at]).wait()
 
 
 def backward_kernel(
@@ -213,9 +498,9 @@
         )
         sig = sigmoid(conv)
         act = conv * sig
-        x = act[:, :CH]
-        b_low = act[:, CH : CH + STATE].astype(BF)
-        c_low = act[:, CH + STATE :].astype(BF)
+        x = act[:, BC:]
+        b_low = act[:, :STATE].astype(BF)
+        c_low = act[:, STATE:BC].astype(BF)
         cum_rows = jnp.transpose(cum)
         scores = mm(c_low, b_low, ((1,), (1,)))
         step_wide = spread(step)
@@ -282,7 +567,7 @@
 
         carry[...] = head_rows(cum_rows, L - 1) * d_state + mm(enter_dy, c_low, ((0,), (0,)))
 
-        d_act = jnp.concatenate([d_x, d_b, d_c], axis=1)
+        d_act = jnp.concatenate([d_b, d_c, d_x], axis=1)
         d_conv = d_act * (sig + act * (1.0 - sig))
         row = r0 + iota2((L + 8, 1), 0)
         longer = jnp.concatenate([d_conv, late[...]], axis=0)
@@ -310,6 +595,7 @@
 
 VM = pl.BlockSpec(memory_space=pltpu.VMEM)
 SM = pl.BlockSpec(memory_space=pltpu.SMEM)
+ANY = pl.BlockSpec(memory_space=pl.ANY)
 LIMIT = 56 << 20
 
 
@@ -340,51 +626,51 @@
     me = lax.axis_index("shard")
     w = in_weight[0]
     rows = w.shape[0]
-    normed_in = rms_scale(resid, norm_gain[0]).astype(BF)
-    out_low = cotangent.astype(BF)
-    wide = jnp.concatenate(
-        [w[:, :INNER].reshape(rows, SHARDS, CH), w[:, INNER : 2 * INNER].reshape(rows, SHARDS, CH)],
-        axis=2,
-    ).transpose(1, 0, 2)
-    wide = lax.all_to_all(wide, "shard", 0, 0).reshape(MODEL, 2 * CH)
-    narrow = lax.all_gather(w[:, 2 * INNER :], "shard", axis=0, tiled=True)
-    w_step = lax.dynamic_slice(narrow, (0, 2 * STATE + me * OWN), (MODEL, OWN))
-    w_in = jnp.concatenate(
-        [wide, narrow[:, : 2 * STATE], jnp.pad(w_step, ((0, 0), (0, 128 - OWN)))], axis=1
-    )
+    narrow = jnp.pad(w[:, 2 * INNER :], ((0, 0), (0, 4 * 128 - BC - HEADS)))
     w_out = out_weight[0]
-    all_in = lax.all_gather(normed_in, "shard", axis=0, tiled=True)
-    all_low = lax.all_gather(out_low, "shard", axis=0, tiled=True)
-    proj = jnp.dot(all_in, w_in, preferred_element_type=F32).astype(BF)
-    proj = jnp.pad(proj, ((HALO, 0), (0, 0)))
-    d_normed = mm(all_low, w_out, ((1,), (1,)))
-
+    shapes = (
+        ((SHARDS, TOK, MODEL), BF), ((SHARDS, TOK, MODEL), BF), ((2, MODEL, HALF), BF),
+        ((HALO + GROUP, COLS), BF), ((GROUP, CH), F32), ((NB + 1, CH, STATE), F32), ((GROUP, CH), F32),
+    )
+    dma = pltpu.SemaphoreType.DMA
+    x_all, low_all, w_all, proj, y, states, d_normed, sums = pl.pallas_call(
+        front_kernel,
+        out_shape=tuple(jax.ShapeDtypeStruct(*shape) for shape in shapes)
+        + (jax.ShapeDtypeStruct((2, NB, L), F32),),
+        in_specs=[SM, ANY, ANY, ANY, ANY] + [VM] * 8,
+        out_specs=(ANY,) * 7 + (VM,),
+        scratch_shapes=[pltpu.VMEM(*shape) for shape in shapes]
+        + [
+            pltpu.VMEM((SHARDS, 2, NB, L), F32),
+            pltpu.VMEM((CH, STATE), F32),
+            pltpu.VMEM((2, TOK, MODEL), F32),
+            pltpu.VMEM((CONV, XBC), F32),
+            pltpu.VMEM((1, XBC), F32),
+        ]
+        + [dma((9,))] * 4 + [dma((SHARDS,))] * 2 + [dma((4,))] * 2 + [dma((1,))] * 2
+        + [dma((SHARDS,))] * 2 + [dma((10,))],
+        compiler_params=pltpu.CompilerParams(
+            vmem_limit_bytes=LIMIT, collective_id=0, has_side_effects=True
+        ),
+    )(
+        first_length, resid, cotangent, w, narrow, w_out, norm_gain, conv_weight[0], conv_bias, dt_bias,
+        a_log, skip, gate_gain,
+    )
+    all_in = x_all.reshape(GROUP, MODEL)
+    all_low = low_all.reshape(GROUP, MODEL)
+    w_in = jnp.concatenate([w_all[0], w_all[1][:, : CH + 128]], axis=1)
     taps = jnp.concatenate(
-        [lax.dynamic_slice(conv_weight[0], (0, me * CH), (CONV, CH)), conv_weight[0][:, INNER:]],
+        [conv_weight[0][:, INNER:], lax.dynamic_slice(conv_weight[0], (0, me * CH), (CONV, CH))],
         axis=1,
     )
     shift = jnp.concatenate(
-        [lax.dynamic_slice(conv_bias[0], (me * CH,), (CH,)), conv_bias[0][INNER:]]
+        [conv_bias[0][INNER:], lax.dynamic_slice(conv_bias[0], (me * CH,), (CH,))]
     )[None]
     step_bias = own_lanes(dt_bias[0], me * OWN, OWN, 128)
     rate_log = own_lanes(a_log[0], me * OWN, OWN, 128)
     skip_wide = jnp.repeat(lax.dynamic_slice(skip[0], (me * OWN,), (OWN,)), HEAD_DIM)[None]
     gain = lax.dynamic_slice(gate_gain[0], (me * CH,), (CH,))[None]
     params = (taps, shift, step_bias, rate_log, skip_wide, gain)
-
-    y, states, sums = pl.pallas_call(
-        forward_kernel,
-        out_shape=(
-            jax.ShapeDtypeStruct((GROUP, CH), F32),
-            jax.ShapeDtypeStruct((NB + 1, CH, STATE), F32),
-            jax.ShapeDtypeStruct((2, NB, L), F32),
-        ),
-        in_specs=[SM] + [VM] * 8,
-        out_specs=(VM,) * 3,
-        scratch_shapes=[pltpu.VMEM((CH, STATE), F32)],
-        compiler_params=pltpu.CompilerParams(vmem_limit_bytes=LIMIT),
-    )(first_length, proj, d_normed, *params)
-    sums = lax.psum(sums, "shard")
 
     inv = lax.rsqrt(sums[0].reshape(GROUP, 1) * (1.0 / INNER) + epsilon)
     normed_out = (y * jax.nn.silu(proj[HALO:, :CH].astype(F32)) * inv * gain).astype(BF)
@@ -412,12 +698,13 @@
     d_stream, d_norm_gain = norm_pull(d_in)
     grad = cotangent + d_stream
 
-    wide_part = in_part[:, : 2 * CH].astype(BF).reshape(SHARDS, rows, 2 * CH)
+    wide_part = jnp.concatenate([in_part[:, :CH], in_part[:, HALF : HALF + CH]], axis=1)
+    wide_part = wide_part.astype(BF).reshape(SHARDS, rows, 2 * CH)
     wide_sum = lax.all_to_all(wide_part, "shard", 0, 0).transpose(1, 0, 2)
     narrow_part = jnp.zeros((MODEL, 2 * STATE + HEADS), F32)
-    narrow_part = narrow_part.at[:, : 2 * STATE].set(in_part[:, 2 * CH : 2 * CH + 2 * STATE])
+    narrow_part = narrow_part.at[:, : 2 * STATE].set(in_part[:, CH : CH + BC])
     narrow_part = lax.dynamic_update_slice(
-        narrow_part, in_part[:, 2 * CH + 2 * STATE :][:, :OWN], (0, 2 * STATE + me * OWN)
+        narrow_part, in_part[:, HALF + CH :][:, :OWN], (0, 2 * STATE + me * OWN)
     ).astype(BF)
     narrow_sum = lax.psum_scatter(narrow_part, "shard", scatter_dimension=0, tiled=True)
     in_share = jnp.concatenate(
@@ -431,7 +718,7 @@
         full = lax.dynamic_update_slice(full, own, (0, me * own.shape[1]))
         return full if rest is None else full.at[:, total - rest.shape[1] :].set(rest)
 
-    conv_parts = place(small[:5, :CH], small[:5, CH:], CONVCH)
+    conv_parts = place(small[:5, BC:], small[:5, :BC], CONVCH)
     skip_part = jnp.sum(small[5, :CH].reshape(OWN, HEAD_DIM), axis=1)[None]
     per_head = place(jnp.concatenate([heads[:2, :OWN], skip_part], axis=0), None, HEADS)
     gain_part = place(small[6:7, :CH], None, INNER)

time: 923 us -> 632 us (0.68)
  waiting for transfers between devices: 538 us -> 288 us
  blocking collectives: 171 us -> 68.3 us
  Pallas kernels: 67.3 us -> 168 us
  matrix products: 59.6 us -> 37.9 us
    all_gather x2 -> x0, waiting for transfers between devices: 106 us -> none  [the longest x1 73.9 us: local(): all_low = lax.all_gather(out_low, 'shard', axis=0, tiled=True)]
    pallas_call x1, Pallas kernels: 23.2 us -> 124 us  [local(): pl.pallas_call(front_kernel, out_shape=tuple((jax.ShapeDtypeStruct(*shape...]
    reduce_scatter x1, waiting for transfers between devices: 96.8 us -> 0.01 us  [local(): lax.psum_scatter(d_in_part, 'shard', scatter_dimension=0, tiled=True)]
    all_gather x1 -> x0, blocking collectives: 66.7 us -> none  [local(): narrow = lax.all_gather(w[:, 2 * INNER:], 'shard', axis=0, tiled=True)]
    psum x1, waiting for transfers between devices: 116 us -> 55 us  [local(): lax.psum((conv_parts, per_head, gain_part, d_norm_gain[None]), ('rep', 's...]
    psum x1, waiting for transfers between devices: 129 us -> 168 us  [local(): in_grad, out_grad = lax.psum((in_share, out_part.astype(BF)), 'rep')]
    psum x1 -> x0, blocking collectives: 30.6 us -> none  [local(): sums = lax.psum(sums, 'shard')]
    reduce_scatter x1, waiting for transfers between devices: 26.2 us -> 0.01 us  [local(): lax.psum_scatter(mixed_part, 'shard', scatter_dimension=0, tiled=True)]
  transfers between devices with their start and end apart: 9 -> 6, of which waited for: 8 -> 4; matrix products, arithmetic and copies ran while one was open for 9% -> 8% of each run, Pallas kernels for 0% -> 0%
where the time goes in v2:
time: 632 us; the launch traced here: 631 us
  waiting for transfers between devices  288 us (46%)
  Pallas kernels  168 us (27%)
  blocking collectives  68.3 us (11%)
  matrix products  37.9 us (6%)
  local copies, waits for them, and re-layouts  27.3 us (4%)
  other arithmetic  17.8 us (3%)
  between operations  16.1 us (3%)
  starting transfers between devices  6.9 us (1%)
    psum x1, waiting for transfers between devices, local(): in_grad, out_grad = lax.psum((in_share, out_part.astype(BF)), 'rep')  168 us
    pallas_call x1, Pallas kernels, local(): pl.pallas_call(front_kernel, out_shape=tuple((jax.ShapeDtypeStruct(*shape...  124 us
    psum x1, blocking collectives, local(): lax.psum((conv_parts, per_head, gain_part, d_norm_gain[None]), ('rep', 's...  68.3 us
    psum x1, waiting for transfers between devices, local(): lax.psum((conv_parts, per_head, gain_part, d_norm_gain[None]), ('rep', 's...  55 us
    pallas_call x1, Pallas kernels, local(): pl.pallas_call(backward_kernel, out_shape=(jax.ShapeDtypeStruct((GROUP, C...  44.1 us
    reduce_scatter x1, waiting for transfers between devices, local(): lax.psum_scatter(narrow_part, 'shard', scatter_dimension=0, tiled=True)  41.6 us
    dot_general x4, matrix products, mm(): return lax.dot_general(a, b, (dims, ((), ())), preferred_element_type=F32)  37.9 us
    all_to_all x1, waiting for transfers between devices, local(): wide_sum = lax.all_to_all(wide_part, 'shard', 0, 0).transpose(1, 0, 2)  23.4 us
  transfers between devices with their start and end apart: 6, of which 4 were waited for; matrix products, arithmetic and copies ran while one was open for 8% of the time, Pallas kernels for 0%

profile of v2, /device:TPU:1, one launch (start us, length us, event | category | flops | bytes accessed | tf_op | source)
XLA Modules:
  0.0 630.6 jit_solution(16293845882459636945)
XLA Ops:
  12.0 0.7 fusion.18
  13.8 0.7 fusion.20
  15.3 0.9 slice.137
  17.4 1.2 fusion.25
  19.4 123.7 %shard_map.203 = (bf16[8,256,1536]{2,1,0:T(8,128)(2,1)}, bf16[8,256,1536]{2,1,0:T(8,128)(2,1)}, bf16[2,1536,640]{2,1,0:T(8,128)(2,1)}, bf16[2064,1152]{1,0:T(8,1...) custom-call(s32[1]{0:T(128)S(6)} %copy.35.first_ref, ...), custom_call_target="tpu_custom_call" | custom-call | tf_op jit(solution)/shard_map/pallas_call | solution.py:636
  143.1 44.1 %shard_map.204 = (bf16[2048,1152]{1,0:T(8,128)(2,1)}, f32[8,640]{1,0:T(8,128)}, f32[8,128]{1,0:T(8,128)}) custom-call(s32[1]{0:T(128)S(6)} %copy.35.first_ref, bf16[2064,1152]{1,0:T(8,128)(2,1)} %get-tuple-element.47.proj, f32[2048,384]{1,0:T(8,128)} %get-tuple-element.49.d_normed, f32[4,640]{1,0:T(4,128)} %pad_maximum_fusion.1.taps, ...), custom_call_target="tpu_custom_call" | custom-call | tf_op jit(solution)/shard_map/pallas_call | solution.py:681
  187.2 11.1 %fusion.28 = bf16[1536,1152]{1,0:T(8,128)(2,1)S(1)} fusion(bf16[2048,1536]{1,0:T(8,128)(2,1)S(1)} %bitcast.59, bf16[2048,1152]{1,0:T(8,128)(2,1)} %get-tuple-element.51), kind=kOutput, calls=%fused_computation.63 | convolution fusion | flops 7247757312 | bytes 14548992 | tf_op jit(solution)/shard_map/dot_general | solution.py:37
  198.3 1.7 copy-done.3
  200.0 0.8 slice_select_fusion
  200.9 1.5 dynamic_update_slice.12
  202.4 1.0 copy-done.2
  203.5 1.9 fusion.26
  205.4 1.6 pad_maximum_fusion
  207.0 6.5 %all-to-all-start = ((bf16[8,192,768]{2,1,0:T(8,128)(2,1)}), bf16[8,192,768]{2,1,0:T(8,128)(2,1)S(1)}, u32[]{:S(2)}, u32[]{:S(2)}) async-start(bf16[8,192,768]{2,1,0:T(8,128)(2,1)} %pad_maximum_fusion), calls=%async_computation.2 | async-start | bytes 4718592 | tf_op jit(solution)/shard_map/all_to_all | solution.py:703
  214.5 8.1 %fusion.10 = bf16[1,384,1536]{2,1,0:T(8,128)(2,1)} fusion(bf16[2048,1536]{1,0:T(8,128)(2,1)} %bitcast.58, f32[2048,384]{1,0:T(8,128)} %get-tuple-element.46.y_in, f32[384]{0:T(512)S(1)} %get-tuple-element.64, f32[2048]{0:T(1024)S(1)} %rsqrt_bitcast_fusion, bf16[2064,1152]{1,0:T(8,128)(2,1)} %get-tuple-element.47.proj), kind=kOutput, calls=%fused_computation.15 | convolution fusion | flops 2423586816 | bytes 12199424 | tf_op jit(solution)/shard_map/dot_general | solution.py:37
  222.6 23.4 %all-to-all-done = bf16[8,192,768]{2,1,0:T(8,128)(2,1)S(1)} async-done(((bf16[8,192,768]{2,1,0:T(8,128)(2,1)}), bf16[8,192,768]{2,1,0:T(8,128)(2,1)S(1)}, u32[]{:S(2)}, u32[]{:S(2)}) %all-to-all-start) | async-done | bytes 2359328 | tf_op jit(solution)/shard_map/all_to_all | solution.py:703
  246.8 41.6 %reduce-scatter.8.cloned.1.call-done = bf16[192,304]{1,0:T(8,128)(2,1)} async-done(((bf16[1536,304]{1,0:T(8,128)(2,1)}), bf16[192,304]{1,0:T(8,128)(2,1)}) %reduce-scatter.8.cloned.1.call-update) | async-done | bytes 116752 | tf_op jit(solution)/shard_map/reduce_scatter | solution.py:709
  288.5 2.6 maximum_bitcast_fusion
  291.1 2.6 slice_bitcast_fusion.1
  294.6 10.3 %convolution_convert_fusion = bf16[2048,1536]{1,0:T(8,128)(2,1)} fusion(bf16[2048,1152]{1,0:T(8,128)(2,1)S(1)} %bitcast.61, bf16[1536,512]{1,0:T(8,128)(2,1)S(1)} %slice.139, bf16[1536,640]{1,0:T(8,128)(2,1)S(1)} %get-tuple-element.66), kind=kOutput, calls=%fused_computation | convolution fusion | flops 7257980928 | bytes 14548992 | tf_op jit(solution)/shard_map/dot_general | solution.py:37
  305.0 1.8 copy-done.4
  306.8 8.5 %convolution_convert_fusion.1 = bf16[2048,1536]{1,0:T(8,128)(2,1)} fusion(bf16[1,384,1536]{2,1,0:T(8,128)(2,1)} %param.27, f32[2048,384]{1,0:T(8,128)S(1)} %copy-done.4, f32[384]{0:T(512)S(1)} %get-tuple-element.64, f32[2048]{0:T(1024)S(1)} %rsqrt_bitcast_fusion, bf16[2064,1152]{1,0:T(8,128)(2,1)} %get-tuple-element.47.proj), kind=kOutput, calls=%fused_computation.1 | convolution fusion | flops 2426142720 | bytes 12199424 | tf_op jit(solution)/shard_map/dot_general | solution.py:37
  315.6 0.9 slice.131
  317.0 55.0 %all-reduce.9.cloned.1.call-done = f32[5,3328]{1,0:T(8,128)} async-done(((f32[5,3328]{1,0:T(8,128)}), f32[5,3328]{1,0:T(8,128)}) %all-reduce.9.cloned.1.call-update) | async-done | bytes 66576 | tf_op jit(solution)/shard_map/psum | solution.py:725
  372.0 1.5 slice.147
  373.5 1.5 slice_bitcast_fusion.4
  375.1 168.3 %all-reduce.11.cloned.1.call-done = (bf16[1,192,6448]{2,1,0:T(8,128)(2,1)}, bf16[1,384,1536]{2,1,0:T(8,128)(2,1)}) async-done(((bf16[1,192,6448]{2,1,0:T(8,128)(2,1)}, bf16[1,384,1536]{2,1,0:T(8,128)(2,1)}), (bf16[1,192,6448]{2,1,0:T(8,128)(2,1)}, bf16[1,384,1536]{2,1,0:T(8,128)(2,1)})) %all-reduce.11.cloned.1.call-update) | async-done | bytes 3655696 | tf_op jit(solution)/shard_map/psum | solution.py:714
  543.4 4.4 broadcast_in_dim.52
  547.8 1.7 broadcast_in_dim.59
  549.5 1.6 fusion.14
  551.1 68.3 %all-reduce.4 = (f32[1,1536]{1,0:T(1,128)}, f32[3,48]{1,0:T(4,128)S(1)}, f32[1,3072]{1,0:T(1,128)}) all-reduce(f32[1,1536]{1,0:T(1,128)S(1)} %reshape.133, f32[3,48]{1,0:T(4,128)S(1)} %dynamic_update_slice.14, f32[1,3072]{1,0:T(1,128)S(1)} %get-tuple-element.74), channel_id=1, replica_groups=mesh['rep'=16,'shard'=8] {'rep','shard'}, use_global_device_ids=true, to_apply=%region_5.6 | all-reduce | flops 4752 | bytes 38016 | tf_op jit(solution)/shard_map/psum | solution.py:725
  620.0 3.5 fusion.15
  (72 shorter events, 11.2 us)
Async XLA Ops:
  8.0 280.4 %reduce-scatter.8.cloned.1.call-start = ((), (), s32[]{:S(2)}) async-start(), calls=%async_computation.6 | async-start | bytes 1327104 | tf_op jit(solution)/shard_map/reduce_scatter | solution.py:709
  143.1 44.1 %copy-start.10 = (bf16[8,256,1536]{2,1,0:T(8,128)(2,1)S(1)}, bf16[8,256,1536]{2,1,0:T(8,128)(2,1)}, u32[]{:S(2)}) copy-start(bf16[8,256,1536]{2,1,0:T(8,128)(2,1)} %get-tuple-element.53) | copy-start | bytes 18874372
  198.2 1.8 copy-start.3
  202.4 1.0 copy-start.2
  207.0 6.5 %copy-start.8 = (f32[8,640]{1,0:T(8,128)S(1)}, f32[8,640]{1,0:T(8,128)}, u32[]{:S(2)}) copy-start(f32[8,640]{1,0:T(8,128)} %get-tuple-element.54) | copy-start | bytes 61444
  207.0 7.5 %copy-start.7 = (f32[2,16,128]{2,1,0:T(8,128)S(1)}, f32[2,16,128]{2,1,0:T(8,128)}, u32[]{:S(2)}) copy-start(f32[2,16,128]{2,1,0:T(8,128)} %get-tuple-element.48.sums) | copy-start | bytes 49156
  207.0 39.1 %all-to-all-start = ((bf16[8,192,768]{2,1,0:T(8,128)(2,1)}), bf16[8,192,768]{2,1,0:T(8,128)(2,1)S(1)}, u32[]{:S(2)}, u32[]{:S(2)}) async-start(bf16[8,192,768]{2,1,0:T(8,128)(2,1)} %pad_maximum_fusion), calls=%async_computation.2 | async-start | bytes 4718592 | tf_op jit(solution)/shard_map/all_to_all | solution.py:703
  213.4 158.6 %all-reduce.9.cloned.1.call-start = ((), (), s32[]{:S(2)}) async-start(), calls=%async_computation.7 | async-start | bytes 212992 | tf_op jit(solution)/shard_map/psum | solution.py:725
  213.5 0.6 copy-start.6
  214.2 329.2 %all-reduce.11.cloned.1.call-start = ((), (), s32[]{:S(2)}) async-start(), calls=%async_computation.8 | async-start | bytes 7372800 | tf_op jit(solution)/shard_map/psum | solution.py:714
  291.0 2.9 slice-start
  291.1 258.4 %reduce-scatter.6.cloned.1.call-start = ((), (), s32[]{:S(2)}) async-start(), calls=%async_computation.5 | async-start | bytes 7077888 | tf_op jit(solution)/shard_map/reduce_scatter | solution.py:696
  291.1 3.5 slice-start.1
  304.9 1.9 copy-start.4
  304.9 315.1 %reduce-scatter.4.cloned.1.call-start = ((), (), s32[]{:S(2)}) async-start(), calls=%async_computation.4 | async-start | bytes 7077888 | tf_op jit(solution)/shard_map/reduce_scatter | solution.py:678
  315.3 1.2 copy-start.9
  315.3 1.5 copy-start
  543.4 4.4 copy-start.5
  547.8 72.2 %copy-start.1 = (f32[256,1536]{1,0:T(8,128)S(1)}, f32[256,1536]{1,0:T(8,128)}, u32[]{:S(2)}) copy-start(f32[256,1536]{1,0:T(8,128)} %cotangent.1) | copy-start | bytes 4718596
Sparse Core Ops, SparseCore 0:
  203.6 84.8 reduce-scatter.7
  305.0 98.7 reduce-scatter.5
  407.7 105.4 reduce-scatter.3
Sparse Core Ops, SparseCore 1:
  218.6 153.3 all-reduce.8
  375.3 168.1 all-reduce.10

commit v3 on v2

v3 whole, which is shorter than its diff:
```python
import jax
import jax.numpy as jnp
from jax import lax
from jax.experimental import pallas as pl
from jax.experimental.pallas import tpu as pltpu
from jax.sharding import PartitionSpec as P

HEADS = 48
HEAD_DIM = 64
STATE = 128
CONV = 4
INNER = 3072
CONVCH = 3328
MODEL = 1536
SHARDS = 8
OWN = HEADS // SHARDS
CH = OWN * HEAD_DIM
XBC = CH + 2 * STATE
HALF = 640
COLS = 2 * CH + 2 * STATE + 128
BC = 2 * STATE
TOK = 256
GROUP = TOK * SHARDS
L = 128
NB = GROUP // L
HALO = 16
PIECE = 48
MESH = pl.DeviceIdType.MESH
ROWS = MODEL // SHARDS
QUARTER = SHARDS * PIECE
TAIL = 8 * 256 + 128
CHUNK = 16
HALF_OUT = MODEL // 2
WIDE = 512
OUT_PART = pl.ds(MODEL, CH)
RESET = -200.0

epsilon = 1e-05
F32 = jnp.float32
BF = jnp.bfloat16


def mm(a, b, dims=((1,), (0,))):
    return lax.dot_general(a, b, (dims, ((), ())), preferred_element_type=F32)


def split(v, parts):
    out = []
    for _ in range(parts):
        piece = v.astype(BF)
        out.append(piece)
        v = v - piece.astype(F32)
    return out


def mm_left(ones, v, parts):
    return sum(mm(ones, piece) for piece in split(v, parts))


def mm_right(v, ones, parts):
    return sum(mm(piece, ones) for piece in split(v, parts))


def iota2(shape, dim):
    return lax.broadcasted_iota(jnp.int32, shape, dim)


def head_columns():
    return (iota2((CH, 128), 0) // HEAD_DIM == iota2((CH, 128), 1)).astype(BF)


def spread(per_head):
    lane = iota2((per_head.shape[0], 128), 1)
    tiles = []
    for pair in range(OWN // 2):
        left = per_head[:, 2 * pair : 2 * pair + 1]
        right = per_head[:, 2 * pair + 1 : 2 * pair + 2]
        tiles.append(jnp.where(lane < HEAD_DIM, left, right))
    return jnp.concatenate(tiles, axis=1)


def head_rows(cum_rows, at):
    pieces = [
        jnp.broadcast_to(cum_rows[h : h + 1, at : at + 1], (HEAD_DIM, 1)) for h in range(OWN)
    ]
    return jnp.exp(jnp.concatenate(pieces, axis=0))


def tap_mask(row, first_len, back):
    past = row - first_len
    return jnp.where((past >= 0) & (past < back), 0.0, 1.0)


def block_front(rows, r0, first_len, taps, shift, step_bias, rate_log):
    xbc = rows[:, CH : CH + XBC].astype(F32)
    row = r0 + iota2((L, 1), 0)
    conv = jnp.broadcast_to(shift, (L, XBC))
    for k in range(CONV):
        back = CONV - 1 - k
        term = taps[k : k + 1] * xbc[HALO - back : HALO - back + L]
        if back:
            term = term * tap_mask(row, first_len, back)
        conv = conv + term
    gate = rows[HALO:, :CH].astype(F32)
    raw = rows[HALO:, CH + XBC :].astype(F32) + step_bias
    step = jnp.maximum(raw, 0.0) + jnp.log1p(jnp.exp(-jnp.abs(raw)))
    log_decay = -step * jnp.exp(rate_log)
    with_reset = log_decay + jnp.where(row == first_len, RESET, 0.0)
    lower = (iota2((L, L), 0) >= iota2((L, L), 1)).astype(BF)
    cum = mm_left(lower, with_reset, 3)
    return gate, xbc, conv, raw, step, log_decay, cum


def sigmoid(v):
    return 1.0 / (1.0 + jnp.exp(-v))


def pair_mix(weights, value, dims=((1,), (0,))):
    lane = iota2((L, 128), 1)
    tiles = []
    for pair in range(OWN // 2):
        part = value[:, 128 * pair : 128 * pair + 128]
        tiles.append(
            jnp.where(
                lane < HEAD_DIM,
                mm(weights[2 * pair], part, dims),
                mm(weights[2 * pair + 1], part, dims),
            )
        )
    return jnp.concatenate(tiles, axis=1)


def decay_weights(cum, cum_rows):
    causal = iota2((L, L), 0) >= iota2((L, L), 1)
    out = []
    for h in range(OWN):
        gap = cum[:, h : h + 1] - cum_rows[h : h + 1, :]
        out.append(jnp.exp(jnp.where(causal, gap, -1e30)))
    return out


def to_row(column):
    return jnp.transpose(jnp.broadcast_to(column, (L, L)))[0:1]


def to_column(row):
    return jnp.transpose(jnp.broadcast_to(row, (L, L)))


def forward_block(b, first_len, proj, taps, shift, step_bias, rate_log, skip, y_out, states, sums, carry):
    r0 = pl.multiple_of(b * L, L)
    rows = proj[pl.ds(r0, HALO + L), :]
    gate, xbc, conv, raw, step, log_decay, cum = block_front(
        rows, r0, first_len, taps, shift, step_bias, rate_log
    )
    act = conv * sigmoid(conv)
    x = act[:, BC:]
    b_low = act[:, :STATE].astype(BF)
    c_low = act[:, STATE:BC].astype(BF)
    cum_rows = jnp.transpose(cum)
    scores = mm(c_low, b_low, ((1,), (1,)))
    scaled = x * spread(step)
    scaled_low = scaled.astype(BF)
    weights = [(w * scores).astype(BF) for w in decay_weights(cum, cum_rows)]
    state = carry[...]
    states[b] = state
    y = pair_mix(weights, scaled_low)
    y = y + jnp.exp(spread(cum)) * mm(c_low, state.astype(BF), ((1,), (1,)))
    tail = jnp.exp(spread(cum[L - 1 : L] - cum))
    carry[...] = head_rows(cum_rows, L - 1) * state + mm(
        (tail * scaled).astype(BF), b_low, ((0,), (0,))
    )
    y = y + skip * x
    y_out[pl.ds(r0, L), :] = y
    gated = y * (gate * sigmoid(gate))
    sums[pl.ds(b, 1), :] = to_row(jnp.sum(gated * gated, axis=1, keepdims=True))


def place_of():
    rep, me = lax.axis_index("rep"), lax.axis_index("shard")
    hi, z = me // 4, lax.rem(me, 4)
    left = hi * 4 + lax.rem(z + 3, 4)
    right = hi * 4 + lax.rem(z + 1, 4)
    far = hi * 4 + lax.rem(z + 2, 4)
    across = lax.rem(me + 4, 8)
    return rep, me, left, right, far, across


def sibling(rep, me):
    return rep + 1 - 2 * lax.rem(rep, 2), me


def beside(rep, me):
    return rep + 2 - 4 * lax.rem(rep // 2, 2), me


def other_side(block):
    return lax.rem(block + 4, 8)


def enter(rep, me):
    barrier = pltpu.get_barrier_semaphore()
    peers = [(rep, lax.rem(me + o, SHARDS)) for o in range(1, SHARDS)]
    peers += [(lax.rem(rep + o, 16), me) for o in range(1, 16)]
    for peer in peers:
        pl.semaphore_signal(barrier, inc=1, device_id=peer, device_id_type=MESH)
    return lambda: pl.semaphore_wait(barrier, len(peers))


def block_rows(block, half=None):
    if half is None:
        return pl.ds(pl.multiple_of(block * TOK, TOK), TOK)
    return pl.ds(pl.multiple_of(block * TOK + half, TOK // 2), TOK // 2)


class Gather:
    def __init__(self, blocks, send, recv):
        self.blocks, self.send, self.recv = blocks, send, recv
        self.rep, self.me, self.left, self.right, self.far, self.across = place_of()

    def move(self, channel, block, to, rows=None):
        ref = self.blocks.at[block_rows(block, rows)]
        return pltpu.make_async_remote_copy(
            src_ref=ref,
            dst_ref=ref,
            send_sem=self.send.at[channel],
            recv_sem=self.recv.at[channel],
            device_id=(self.rep, to),
            device_id_type=MESH,
        )

    def outgoing(self, channel):
        me, left, right, across = self.me, self.left, self.right, self.across
        return (
            lambda: self.move(0, me, right),
            lambda: self.move(1, me, left),
            lambda: self.move(2, me, across),
            lambda: self.move(3, left, right, 0),
            lambda: self.move(4, right, left, TOK // 2),
            lambda: self.move(5, across, right),
            lambda: self.move(6, across, left),
            lambda: self.move(7, self.far, across, 0),
            lambda: self.move(8, self.far, across, TOK // 2),
        )[channel]()

    def incoming(self, channel):
        left, right, far, across = self.left, self.right, self.far, self.across
        return (
            lambda: self.move(0, left, left),
            lambda: self.move(1, right, right),
            lambda: self.move(2, across, across),
            lambda: self.move(3, far, left, 0),
            lambda: self.move(4, far, right, TOK // 2),
            lambda: self.move(5, other_side(left), left),
            lambda: self.move(6, other_side(right), right),
            lambda: self.move(7, other_side(far), across, 0),
            lambda: self.move(8, other_side(far), across, TOK // 2),
        )[channel]()

    def start(self, *channels):
        for channel in channels:
            self.outgoing(channel).start()

    def arrived(self, *channels):
        for channel in channels:
            self.incoming(channel).wait_recv()

    def sent(self):
        for channel in range(9):
            self.outgoing(channel).wait_send()


class Scatter:
    SLOTS = ((0, None), (1, None), (2, None), (3, 0), (3, TOK // 2), (4, None), (5, None), (6, None))

    def __init__(self, part, out, into, send, recv):
        self.part, self.out, self.into, self.send, self.recv = part, out, into, send, recv
        self.rep, self.me, self.left, self.right, self.far, self.across = place_of()
        self.to = (
            self.across, self.left, self.right, self.left, self.right, self.right, self.left, self.across,
        )

    def copy(self, channel):
        slot, rows = self.SLOTS[channel]
        at = (slot,) if rows is None else (slot, pl.ds(rows, TOK // 2))
        return pltpu.make_async_remote_copy(
            src_ref=self.out.at[at],
            dst_ref=self.into.at[at],
            send_sem=self.send.at[channel],
            recv_sem=self.recv.at[channel],
            device_id=(self.rep, self.to[channel]),
            device_id_type=MESH,
        )

    def arrived(self, *channels):
        for channel in channels:
            self.copy(channel).wait_recv()

    def fill(self, slot, block, *arrived):
        for at in range(0, MODEL, WIDE):
            lanes = slice(at, at + WIDE)
            value = self.part(block, lanes)
            for other in arrived:
                value = value + self.into[other, :, lanes].astype(F32)
            self.out[slot, :, lanes] = value.astype(BF)

    def leaf(self, slot):
        self.fill(slot, other_side((self.far, self.left, self.right)[slot]))
        self.copy(slot).start()

    def middle(self):
        self.arrived(0)
        self.fill(3, self.far, 0)
        self.copy(3).start()
        self.copy(4).start()
        self.arrived(1, 2)
        self.fill(6, self.across, 1, 2)
        self.copy(7).start()

    def last(self):
        half = TOK // 2
        self.fill(4, self.right)
        self.fill(5, self.left)
        self.arrived(3, 4)
        for slot, rows in ((4, slice(half, TOK)), (5, slice(0, half))):
            value = self.out[slot, rows].astype(F32) + self.into[3, rows].astype(F32)
            self.out[slot, rows] = value.astype(BF)
            self.copy(1 + slot).start()

    def total(self, lanes):
        value = self.part(self.me, lanes)
        for slot in (4, 5, 6):
            value = value + self.into[slot, :, lanes].astype(F32)
        return value

    def sent(self):
        for channel in range(8):
            self.copy(channel).wait_send()


def own_heads(vector, me):
    pick = (iota2((HEADS, 128), 0) == iota2((HEADS, 128), 1) + me * OWN) & (
        iota2((HEADS, 128), 1) < OWN
    )
    wide = jnp.broadcast_to(vector, (8, HEADS))
    return mm_right(wide, pick.astype(BF), 3)[0:1]


def own_channels(vector, me):
    pick = iota2((HEADS, CH), 0) == iota2((HEADS, CH), 1) // HEAD_DIM + me * OWN
    wide = jnp.broadcast_to(vector, (8, HEADS))
    return mm_right(wide, pick.astype(BF), 3)[0:1]


def own_slices(me, conv_weight, conv_bias):
    own = pl.ds(pl.multiple_of(me * CH, 128), CH)
    taps = jnp.concatenate([conv_weight[:, INNER:], conv_weight[:, own]], axis=1)
    shift = jnp.concatenate([conv_bias[:, INNER:], conv_bias[:, own]], axis=1)
    return taps, shift


def layer_kernel(
    first_ref, resid, cotangent, w_in, narrow, w_out, norm_gain, conv_weight, conv_bias, dt_bias,
    a_log, skip, gate_gain,
    mixed_out, grad_out, gates_out, tail_out, outs_out, small_out, norm_out,
    x_all, low_all, w_all, proj, y, states, d_normed, sums, carry, stage, taps, shift,
    totals, normed_out, gain_sum, norm_sum, small, heads, late, scatter_out, scatter_in,
    near_y, core_out, core_gate, near_out, near_gate, part_out, part_gate, side_out, side_gate,
    quarter, gates, outs,
    tail_swap, tail_pieces, tail,
    packed, packed_in, packed_y, packed_all, norm_parts, norm_all,
    x_send, x_recv, low_send, low_recv, piece_send, piece_recv, y_send, y_recv, core_send, core_recv,
    sum_send, sum_recv, here, mix_send, mix_recv, grad_send, grad_recv, g_send, g_recv, norm_send, norm_recv, owner_send, owner_recv, free, core_free,
):
    rep, me, left, right, far, across = place_of()
    core = lax.rem(rep, 2)
    along_y = rep // 4
    first_len = first_ref[0]
    load_resid = pltpu.make_async_copy(resid, stage.at[0], here.at[0])
    load_cot = pltpu.make_async_copy(cotangent, stage.at[1], here.at[1])
    load_resid.start()
    load_cot.start()
    all_entered = enter(rep, me)

    load_resid.wait()

    def norm_rows(at, unused):
        rows = stage[0, pl.ds(pl.multiple_of(at * CHUNK, CHUNK), CHUNK), :]
        scale = lax.rsqrt(jnp.mean(rows * rows, axis=1, keepdims=True) + epsilon)
        own = pl.ds(pl.multiple_of(me * TOK + at * CHUNK, CHUNK), CHUNK)
        x_all[own, :] = (rows * scale * norm_gain[...]).astype(BF)
        return unused

    lax.fori_loop(0, TOK // CHUNK, norm_rows, 0)
    all_entered()
    gather_x = Gather(x_all, x_send, x_recv)
    gather_x.start(0, 1, 2)

    own_rows = pl.ds(pl.multiple_of(along_y * PIECE, 16), PIECE)

    def landing(block):
        return pl.ds(pl.multiple_of(block * 192 + along_y * PIECE, 16), PIECE)

    def weight_pieces(to, make):
        wide = pl.ds(pl.multiple_of(core * INNER + to * CH, 128), CH)
        half = pl.ds(pl.multiple_of(core * BC, 128), BC)
        make(w_in.at[own_rows, wide], w_all.at[core, landing(me), pl.ds(0, CH)])
        make(narrow.at[own_rows, half], w_all.at[core, landing(me), pl.ds(CH, BC)])

    for o in range(1, SHARDS):
        to = lax.rem(me + o, SHARDS)
        weight_pieces(
            to,
            lambda src, dst: pltpu.make_async_remote_copy(
                src_ref=src, dst_ref=dst, send_sem=piece_send.at[o], recv_sem=piece_recv.at[o],
                device_id=(rep, to), device_id_type=MESH,
            ).start(),
        )
    weight_pieces(me, lambda src, dst: pltpu.make_async_copy(src, dst, here.at[2]).start())

    load_cot.wait()
    low_all[block_rows(me), :] = stage[1].astype(BF)
    gather_low = Gather(low_all, low_send, low_recv)

    taps_now, shift_now = own_slices(me, conv_weight, conv_bias)
    taps[...] = taps_now
    shift[...] = shift_now
    proj[pl.ds(0, HALO), :] = jnp.zeros((HALO, COLS), BF)
    carry[...] = jnp.zeros_like(carry)

    pltpu.make_async_copy(
        w_all.at[core, landing(me)], w_all.at[core, landing(me)], here.at[2]
    ).wait()
    for o in range(1, SHARDS):
        source = lax.rem(me + SHARDS - o, SHARDS)
        piece = w_all.at[core, landing(source)]
        pltpu.make_async_remote_copy(
            src_ref=piece, dst_ref=piece, send_sem=piece_send.at[o], recv_sem=piece_recv.at[o],
            device_id=(rep, source), device_id_type=MESH,
        ).wait()
    for o in range(1, 4):
        for block in range(SHARDS):
            piece = w_all.at[core, landing(block)]
            pltpu.make_async_remote_copy(
                src_ref=piece, dst_ref=piece, send_sem=y_send.at[o], recv_sem=y_recv.at[o],
                device_id=(lax.rem(rep + 4 * o, 16), me), device_id_type=MESH,
            ).start()
    gather_x.arrived(0)
    gather_x.start(3)
    gather_x.arrived(1)
    gather_x.start(4)
    gather_x.arrived(2)
    gather_x.start(5, 6)
    gather_x.arrived(3)
    gather_x.start(7)
    gather_x.arrived(4)
    gather_x.start(8)
    gather_low.start(0, 1, 2)
    for o in range(1, 4):
        landed = w_all.at[core, pl.ds(0, QUARTER)]
        pltpu.make_async_remote_copy(
            src_ref=landed, dst_ref=landed, send_sem=y_send.at[o], recv_sem=y_recv.at[o],
            device_id=(lax.rem(rep + 4 * o, 16), me), device_id_type=MESH,
        ).wait()

    def halves(which):
        return pltpu.make_async_remote_copy(
            src_ref=w_all.at[which], dst_ref=w_all.at[which], send_sem=core_send.at[0],
            recv_sem=core_recv.at[0], device_id=(rep + 1 - 2 * core, me), device_id_type=MESH,
        )

    halves(core).start()
    halves(1 - core).wait_recv()
    halves(core).wait_send()
    pick = (iota2((128, 128), 0) == iota2((128, 128), 1) + me * OWN) & (iota2((128, 128), 1) < OWN)
    w_all[1, :, CH : CH + 128] = mm(w_all[1, :, CH : CH + 128], pick.astype(BF)).astype(BF)

    side = (me // 4) * 4

    def project(at, unused):
        rows = x_all[block_rows(at), :]
        begin = pl.multiple_of(HALO + at * TOK, 16)
        proj[pl.ds(begin, TOK), :HALF] = mm(rows, w_all[0]).astype(BF)
        proj[pl.ds(begin, TOK), HALF:] = mm(rows, w_all[1, :, : CH + 128]).astype(BF)
        return unused

    lax.fori_loop(side, side + 4, project, 0)
    gather_low.arrived(0)
    gather_low.start(3)
    gather_low.arrived(1)
    gather_low.start(4)
    gather_x.arrived(5, 6, 7, 8)
    lax.fori_loop(4 - side, 8 - side, project, 0)

    step_bias = own_heads(dt_bias[...], me)
    rate_log = own_heads(a_log[...], me)
    skip_wide = own_channels(skip[...], me)

    def scan(b, unused):
        @pl.when(b == 6)
        def relay():
            gather_low.arrived(3, 4, 2)
            gather_low.start(7, 8, 5, 6)

        forward_block(
            b, first_len, proj, taps[...], shift[...], step_bias, rate_log, skip_wide, y, states,
            sums.at[me, 0], carry,
        )
        return unused

    lax.fori_loop(0, NB, scan, 0)
    states[NB] = carry[...]

    gain = gate_gain[:, pl.ds(pl.multiple_of(me * CH, 128), CH)]

    def normed(at, unused):
        begin = pl.multiple_of(at * TOK, TOK)
        dn = mm(low_all[block_rows(at), :], w_out[...], ((1,), (1,)))
        d_normed[pl.ds(begin, TOK), :] = dn.astype(BF)
        gate = proj[pl.ds(HALO + begin, TOK), :CH].astype(F32)
        gated = y[pl.ds(begin, TOK), :] * (gate * sigmoid(gate))
        both = jnp.sum(gated * gain * dn, axis=1, keepdims=True)
        sums[me, 1, pl.ds(2 * at, 1), :] = to_row(both[:L])
        sums[me, 1, pl.ds(2 * at + 1, 1), :] = to_row(both[L:])
        return unused

    lax.fori_loop(side, side + 4, normed, 0)
    gather_low.arrived(5, 6)

    def normed_near(at, unused):
        return normed(other_side(side + lax.rem(me + at, 4)), unused)

    lax.fori_loop(3, 6, normed_near, 0)
    gather_low.arrived(7, 8)
    lax.fori_loop(6, 7, normed_near, 0)

    def sum_copy(o, slot, to):
        return pltpu.make_async_remote_copy(
            src_ref=sums.at[slot], dst_ref=sums.at[slot], send_sem=sum_send.at[o],
            recv_sem=sum_recv.at[o], device_id=(rep, to), device_id_type=MESH,
        )

    for o in range(1, SHARDS):
        sum_copy(o, me, lax.rem(me + o, SHARDS)).start()
    for o in range(1, SHARDS):
        source = lax.rem(me + SHARDS - o, SHARDS)
        sum_copy(o, source, source).wait_recv()
    for o in range(1, SHARDS):
        sum_copy(o, me, lax.rem(me + o, SHARDS)).wait_send()
    total = sums[0]
    for slot in range(1, SHARDS):
        total = total + sums[slot]
    totals[...] = total

    def send(index, src, dst, to):
        return pltpu.make_async_remote_copy(
            src_ref=src, dst_ref=dst, send_sem=g_send.at[index], recv_sem=g_recv.at[index],
            device_id=to, device_id_type=MESH,
        )

    def y_peer(o):
        return lax.rem(rep + 4 * o, 16), me

    def y_of(o):
        return lax.rem(along_y + o, 4)

    gain_sum[...] = jnp.zeros_like(gain_sum)
    small[...] = jnp.zeros_like(small)
    heads[...] = jnp.zeros_like(heads)
    late[...] = jnp.zeros_like(late)
    carry[...] = jnp.zeros_like(carry)

    def prepare(b, unused):
        prepare_block(b, proj, y, d_normed, totals, gain, normed_out, gain_sum)
        return unused

    def mixed_part(block, lanes):
        return mm(normed_out[block_rows(block), :], w_out[:, lanes])

    mix = Scatter(mixed_part, scatter_out, scatter_in, mix_send, mix_recv)
    def prepare_two(block):
        lax.fori_loop(2 * block, 2 * block + 2, prepare, 0)

    for slot, block in enumerate((far, left, right)):
        prepare_two(other_side(block))
        mix.leaf(slot)
    prepare_two(across)
    lax.fori_loop(2 * side, 2 * side + 8, prepare, 0)

    gather_low.sent()
    def out_tile(at, unused):
        lanes = pl.ds(pl.multiple_of(at * 256, 256), 256)
        low = low_all[:, lanes]
        low_all[OUT_PART, lanes] = mm(normed_out[...], low, ((0,), (0,))).astype(BF)
        return unused

    def gate_tile(at, unused):
        lanes = pl.ds(pl.multiple_of(at * 256, 256), 256)
        rows = x_all[:, lanes]
        low_all[lanes, :CH] = mm(rows, proj[HALO:, :CH], ((0,), (0,))).astype(BF)
        return unused

    def y_rows(block, y_at):
        return pl.ds(pl.multiple_of(block * ROWS + y_at * PIECE, 16), PIECE)

    def out_rows(y_at, base=0):
        return pl.ds(pl.multiple_of(base + y_at * 96, 16), 96)

    def part_columns(which):
        return pl.ds(pl.multiple_of(which * CH, 128), CH)

    def out_half(which):
        return pl.ds(pl.multiple_of(which * HALF_OUT, 128), HALF_OUT)

    def gate_half(which):
        return pl.ds(pl.multiple_of(which * HALF_OUT, 128), HALF_OUT)

    core_copies = (
        send(1, low_all.at[OUT_PART, out_half(1 - core)], core_out, sibling(rep, me)),
        send(2, low_all.at[gate_half(1 - core), pl.ds(0, CH)], core_gate, sibling(rep, me)),
    )
    lax.fori_loop(0, MODEL // 256, out_tile, 0)
    core_copies[0].start()
    lax.fori_loop(0, MODEL // 256, gate_tile, 0)
    core_copies[1].start()

    def gate_piece(block, y_at):
        return pl.ds(pl.multiple_of(core * HALF_OUT + block * ROWS + y_at * PIECE, 16), PIECE)

    def out_to_y(o):
        src = low_all.at[out_rows(y_of(o), MODEL), out_half(core)]
        return send(2 + o, src, near_out.at[o - 1], y_peer(o))

    def gate_to_y(o, block):
        dst = near_gate.at[o - 1, pl.ds(block * PIECE, PIECE)]
        return send(5 + o, low_all.at[gate_piece(block, y_of(o)), pl.ds(0, CH)], dst, y_peer(o))

    def core_sum():
        for copy in core_copies:
            copy.wait()
        mine = out_half(core)
        both = low_all[OUT_PART, mine].astype(F32) + core_out[...].astype(F32)
        low_all[OUT_PART, mine] = both.astype(BF)
        both = low_all[gate_half(core), :CH].astype(F32) + core_gate[...].astype(F32)
        low_all[gate_half(core), :CH] = both.astype(BF)
        for o in range(1, 4):
            out_to_y(o).start()
            for block in range(SHARDS // 2):
                gate_to_y(o, block).start()

    side_copies = (
        send(9, part_gate, side_gate, beside(rep, me)),
        send(10, part_out, side_out, beside(rep, me)),
    )

    def y_sum():
        for o in range(1, 4):
            out_to_y(o).wait()
            landed = low_all.at[pl.ds(0, HALF_OUT // 4), pl.ds(0, CH)]
            send(5 + o, landed, near_gate.at[o - 1], y_peer(o)).wait()
        total = low_all[out_rows(along_y, MODEL), out_half(core)].astype(F32)
        for o in range(3):
            total = total + near_out[o].astype(F32)
        part_out[...] = total.astype(BF)
        for block in range(SHARDS // 2):
            rows = slice(block * PIECE, (block + 1) * PIECE)
            total = low_all[gate_piece(block, along_y), :CH].astype(F32)
            for o in range(3):
                total = total + near_gate[o, rows].astype(F32)
            part_gate[rows] = total.astype(BF)
        for copy in side_copies:
            copy.start()
        pl.semaphore_signal(
            core_free, inc=1, device_id=sibling(rep, me), device_id_type=MESH
        )

    own_piece = pl.ds(pl.multiple_of(along_y * PIECE, 16), PIECE)

    def gate_columns(block):
        return pl.ds(pl.multiple_of(block * CH, 128), CH)

    def own_quarter(block):
        return pl.ds(pl.multiple_of(block * PIECE, 16), PIECE)

    owner_here = core == me // 4

    def from_shard(o):
        source = lax.rem(me + SHARDS - o, SHARDS)
        dst = gates.at[own_piece, gate_columns(source)]
        return pltpu.make_async_remote_copy(
            src_ref=dst, dst_ref=dst, send_sem=owner_send.at[me], recv_sem=owner_recv.at[source],
            device_id=(rep, source), device_id_type=MESH,
        )

    def owner_copy(block):
        to = core * (SHARDS // 2) + block
        return pltpu.make_async_remote_copy(
            src_ref=part_gate.at[pl.ds(block * PIECE, PIECE)], dst_ref=gates.at[own_piece, gate_columns(me)],
            send_sem=owner_send.at[block], recv_sem=owner_recv.at[me], device_id=(rep, to),
            device_id_type=MESH,
        )

    def each_owner(act):
        for block in range(SHARDS // 2):

            @pl.when(core * (SHARDS // 2) + block != me)
            def other():
                act(owner_copy(block))

    def own_outs(y_at):
        return outs.at[out_rows(y_at), out_half(core)]

    def side_sum():
        for copy in side_copies:
            copy.wait()
        part_gate[...] = (part_gate[...].astype(F32) + side_gate[...].astype(F32)).astype(BF)
        total = part_out[...].astype(F32) + side_out[...].astype(F32)
        outs[out_rows(along_y), out_half(core)] = total.astype(BF)
        each_owner(lambda copy: copy.start())

        @pl.when(owner_here)
        def keep():
            own = pl.ds(pl.multiple_of(lax.rem(me, 4) * PIECE, 16), PIECE)
            gates[own_piece, gate_columns(me)] = part_gate[own, :]

        for o in range(1, 4):
            send(14 + o, own_outs(along_y), own_outs(along_y), y_peer(o)).start()

    def share_gates():
        each_owner(lambda copy: copy.wait_send())

        @pl.when(owner_here)
        def collect():
            for o in range(1, SHARDS):
                from_shard(o).wait_recv()
            for o in range(1, 4):
                src = gates.at[own_piece]
                send(18 + o, src, src, y_peer(o)).start()

    def to_sibling():
        for o in range(1, 4):
            src = own_outs(y_of(4 - o))
            send(14 + o, src, src, y_peer(o)).wait()
        send(22, outs.at[:, out_half(core)], outs.at[:, out_half(core)], sibling(rep, me)).start()

        @pl.when(owner_here)
        def share():
            for o in range(1, 4):
                src = gates.at[pl.ds(pl.multiple_of(y_of(4 - o) * PIECE, 16), PIECE)]
                send(18 + o, src, src, y_peer(o)).wait()
            send(23, gates, gates, sibling(rep, me)).start()

    def early_done():
        send(22, outs.at[:, out_half(core)], outs.at[:, out_half(core)], sibling(rep, me)).wait_send()
        theirs = outs.at[:, out_half(1 - core)]
        send(22, theirs, theirs, sibling(rep, me)).wait_recv()

        @pl.when(owner_here)
        def sent():
            send(23, gates, gates, sibling(rep, me)).wait_send()

        @pl.when(jnp.logical_not(owner_here))
        def got():
            send(23, gates, gates, sibling(rep, me)).wait_recv()

        pltpu.make_async_copy(gates, gates_out, here.at[3]).start()
        pltpu.make_async_copy(outs, outs_out, here.at[10]).start()

    def backward(at, unused):
        @pl.when(at == 1)
        def hook_a():
            core_sum()

        @pl.when(at == 4)
        def hook_b():
            mix.middle()

        @pl.when(at == 10)
        def hook_c():
            y_sum()

        @pl.when(at == 9)
        def hook_d():
            mix.last()

        @pl.when(at == 13)
        def hook_e():
            side_sum()

        backward_block(
            NB - 1 - at, first_len, proj, d_normed, taps[...], shift[...], step_bias, rate_log, skip_wide,
            y, states, small, heads, carry, late,
        )
        return unused

    lax.fori_loop(0, NB, backward, 0)

    def d_in_part(block, lanes):
        begin = pl.multiple_of(HALO + block * TOK, 16)
        return mm(proj[pl.ds(begin, TOK), :HALF], w_all[0, lanes, :], ((1,), (1,))) + mm(
            proj[pl.ds(begin, TOK), HALF:], w_all[1, lanes, : CH + 128], ((1,), (1,))
        )

    mix.arrived(5, 6, 7)
    for at in range(0, MODEL, WIDE):
        lanes = slice(at, at + WIDE)
        stage[1, :, lanes] = stage[0, :, lanes] + mix.total(lanes)
    store_mixed = pltpu.make_async_copy(stage.at[1], mixed_out, here.at[5])
    store_mixed.start()
    mix.sent()
    for peer in (left, right, across):
        pl.semaphore_signal(free, inc=1, device_id=(rep, peer), device_id_type=MESH)
    pl.semaphore_wait(free, 3)
    d_in = Scatter(d_in_part, scatter_out, scatter_in, grad_send, grad_recv)
    for slot in range(3):
        d_in.leaf(slot)
    store_mixed.wait()
    load_again = pltpu.make_async_copy(cotangent, stage.at[1], here.at[6])
    load_again.start()

    def small_copy(which):
        peer = (sibling, beside)[which](rep, me)
        return send(44 + which, packed.at[which], packed_in.at[which], peer)

    def small_first():
        small_copy(0).wait()
        packed[1] = packed[0] + packed_in[0]
        small_copy(1).start()

    def small_second():
        small_copy(1).wait()
        packed_y[along_y] = packed[1] + packed_in[1]
        for o in range(1, 4):
            send(46 + o, packed_y.at[along_y], packed_y.at[along_y], y_peer(o)).start()

    def small_third():
        for o in range(1, 4):
            src = packed_y.at[y_of(4 - o)]
            send(46 + o, src, src, y_peer(o)).wait()
        packed_all[me] = packed_y[0] + packed_y[1] + packed_y[2] + packed_y[3]
        for o in range(1, SHARDS):
            to = rep, lax.rem(me + o, SHARDS)
            send(50 + o, packed_all.at[me], packed_all.at[me], to).start()

    def small_last():
        for o in range(1, SHARDS):
            source = lax.rem(me + SHARDS - o, SHARDS)
            send(50 + o, packed_all.at[source], packed_all.at[source], (rep, source)).wait()
        pltpu.make_async_copy(packed_all, small_out, here.at[9]).start()

    def norm_copy(index, ref, to):
        return pltpu.make_async_remote_copy(
            src_ref=ref, dst_ref=ref, send_sem=norm_send.at[index], recv_sem=norm_recv.at[index],
            device_id=to, device_id_type=MESH,
        )

    packed[0] = jnp.zeros_like(packed[0])
    packed[0, :5, :XBC] = small[:5]
    packed[0, 5:6, :CH] = small[5:6, :CH]
    packed[0, 5:6, CH : 2 * CH] = gain_sum[...]
    packed[0, 5:6, 2 * CH : 2 * CH + 128] = heads[0:1]
    packed[0, 5:6, 2 * CH + 128 : 2 * CH + 256] = heads[1:2]
    small_copy(0).start()

    def tail_tiles(which):
        def tile(at, unused):
            lanes = pl.ds(pl.multiple_of(at * 256, 256), 256)
            part = mm(x_all[:, lanes], proj[HALO:, part_columns(1 + which)], ((0,), (0,)))
            low_all[lanes, part_columns(1 + which)] = part.astype(BF)
            return unused

        lax.fori_loop(0, MODEL // 256, tile, 0)

    mine = part_columns(1 + core)
    share_gates()
    tail_tiles(1 - core)
    received = low_all.at[pl.ds(0, MODEL), part_columns(0)]
    core_copy = send(28, low_all.at[pl.ds(0, MODEL), part_columns(2 - core)], received, sibling(rep, me))
    pl.semaphore_wait(core_free, 1)
    core_copy.start()
    tail_tiles(core)
    core_copy.wait()

    def add_core(at, unused):
        rows = block_rows(at)
        both = low_all[rows, mine].astype(F32) + low_all[rows, :CH].astype(F32)
        low_all[rows, mine] = both.astype(BF)
        return unused

    lax.fori_loop(0, MODEL // TOK, add_core, 0)
    for o in range(1, 4):
        for block in range(SHARDS):
            src = low_all.at[y_rows(block, y_of(o)), mine]
            send(28 + o, src, near_y.at[o - 1, pl.ds(block * PIECE, PIECE)], y_peer(o)).start()
    small_first()
    d_in.middle()
    to_sibling()
    for o in range(1, 4):
        send(28 + o, low_all.at[pl.ds(0, QUARTER), mine], near_y.at[o - 1], y_peer(o)).wait()
    for block in range(SHARDS):
        rows = slice(block * PIECE, (block + 1) * PIECE)
        total = low_all[y_rows(block, along_y), mine].astype(F32)
        for o in range(3):
            total = total + near_y[o, rows].astype(F32)
        quarter[rows] = total.astype(BF)
    side_copy = send(32, quarter, tail_swap, beside(rep, me))
    side_copy.start()
    small_second()
    d_in.last()
    side_copy.wait()
    quarter[...] = (quarter[...].astype(F32) + tail_swap[...].astype(F32)).astype(BF)
    for o in range(1, SHARDS):
        to = lax.rem(me + o, SHARDS)
        send(32 + o, quarter.at[own_quarter(to)], tail_pieces.at[me], (rep, to)).start()
    tail_pieces[me] = quarter[own_quarter(me), :]
    small_third()
    early_done()
    for o in range(1, SHARDS):
        source = lax.rem(me + SHARDS - o, SHARDS)
        send(32 + o, quarter.at[own_quarter(source)], tail_pieces.at[source], (rep, source)).wait()

    @pl.when(core == 0)
    def assemble_first():
        total = tail_pieces[0, :, :BC].astype(F32)
        for block in range(1, SHARDS):
            total = total + tail_pieces[block, :, :BC].astype(F32)
        tail[0, own_piece, :BC] = total.astype(BF)
        for block in range(SHARDS):
            tail[0, own_piece, BC + 128 * block : BC + 128 * block + 128] = tail_pieces[block, :, BC:]
        tail[0, own_piece, BC + 1024 :] = jnp.zeros((PIECE, TAIL - BC - 1024), BF)

    @pl.when(core == 1)
    def assemble_second():
        total = jnp.zeros((PIECE, 128), F32)
        for block in range(SHARDS):
            tail[1, own_piece, 256 * block : 256 * block + 256] = tail_pieces[block, :, :256]
            put = (iota2((128, 128), 1) == iota2((128, 128), 0) + block * OWN) & (
                iota2((128, 128), 0) < OWN
            )
            total = total + mm(tail_pieces[block, :, 256:], put.astype(BF))
        tail[1, own_piece, 2048:] = total.astype(BF)

    for o in range(1, 4):
        src = tail.at[core, own_piece]
        send(40 + o, src, src, y_peer(o)).start()

    small_last()
    d_in.arrived(5, 6, 7)
    for at in range(MODEL // CH):
        y[at * TOK : (at + 1) * TOK, :] = d_in.total(slice(at * CH, (at + 1) * CH))
    load_again.wait()
    norm_sum[...] = jnp.zeros_like(norm_sum)

    def norm_back(at, unused):
        chunk = pl.ds(pl.multiple_of(at * CHUNK, CHUNK), CHUNK)
        rows = stage[0, chunk, :]
        pieces = [
            y[pl.ds(pl.multiple_of(k * TOK + at * CHUNK, CHUNK), CHUNK), :] for k in range(MODEL // CH)
        ]
        d_rows = jnp.concatenate(pieces, axis=1)
        scale = lax.rsqrt(jnp.mean(rows * rows, axis=1, keepdims=True) + epsilon)
        unit = rows * scale
        d_unit = d_rows * norm_gain[...]
        norm_sum[...] += jnp.sum((d_rows * unit).reshape(CHUNK // 8, 8, MODEL), axis=0)
        stage[1, chunk, :] += scale * (d_unit - unit * jnp.mean(d_unit * unit, axis=1, keepdims=True))
        return unused

    lax.fori_loop(0, TOK // CHUNK, norm_back, 0)
    store_grad = pltpu.make_async_copy(stage.at[1], grad_out, here.at[7])
    store_grad.start()

    for at in range(MODEL // 128):
        norm_parts[rep, at : at + 1, :] = jnp.sum(
            norm_sum[:, 128 * at : 128 * at + 128], axis=0, keepdims=True
        )
    norm_parts[rep, MODEL // 128 :, :] = jnp.zeros((16 - MODEL // 128, 128), F32)
    for o in range(1, 16):
        to = lax.rem(rep + o, 16), me
        norm_copy(o, norm_parts.at[rep], to).start()
    for o in range(1, 16):
        source = lax.rem(rep + 16 - o, 16)
        norm_copy(o, norm_parts.at[source], (source, me)).wait()
    total = norm_parts[0]
    for at in range(1, 16):
        total = total + norm_parts[at]
    norm_all[me] = total
    for o in range(1, SHARDS):
        norm_copy(15 + o, norm_all.at[me], (rep, lax.rem(me + o, SHARDS))).start()

    for o in range(1, 4):
        src = tail.at[core, pl.ds(pl.multiple_of(y_of(4 - o) * PIECE, 16), PIECE)]
        send(40 + o, src, src, y_peer(o)).wait()
    last_copy = send(58, tail.at[core], tail.at[core], sibling(rep, me))
    last_copy.start()
    send(58, tail.at[1 - core], tail.at[1 - core], sibling(rep, me)).wait_recv()
    last_copy.wait_send()
    store_tail = pltpu.make_async_copy(tail, tail_out, here.at[8])
    store_tail.start()
    for o in range(1, SHARDS):
        source = lax.rem(me + SHARDS - o, SHARDS)
        norm_copy(15 + o, norm_all.at[source], (rep, source)).wait()
    store_norm = pltpu.make_async_copy(norm_all, norm_out, here.at[4])
    store_norm.start()
    d_in.sent()
    gather_x.sent()
    pltpu.make_async_copy(gates, gates_out, here.at[3]).wait()
    pltpu.make_async_copy(outs, outs_out, here.at[10]).wait()
    store_grad.wait()
    store_tail.wait()
    pltpu.make_async_copy(packed_all, small_out, here.at[9]).wait()
    store_norm.wait()


def prepare_block(b, proj, y, d_normed, totals, gain, normed_out, gain_sum):
    r0 = pl.multiple_of(b * L, L)
    here = pl.ds(pl.multiple_of(HALO + b * L, 16), L)
    gate = proj[here, :CH].astype(F32)
    mixer = y[pl.ds(r0, L), :]
    sig = sigmoid(gate)
    silu = gate * sig
    gated = mixer * silu
    inv = lax.rsqrt(totals[0, pl.ds(b, 1), :] * (1.0 / INNER) + epsilon)
    back = inv * inv * inv * totals[1, pl.ds(b, 1), :] * (1.0 / INNER)
    inv = jnp.concatenate([to_column(inv)] * (CH // 128), axis=1)
    back = jnp.concatenate([to_column(back)] * (CH // 128), axis=1)
    dn = d_normed[pl.ds(r0, L), :].astype(F32)
    scaled = gated * inv
    normed_out[pl.ds(r0, L), :] = (scaled * gain).astype(BF)
    gain_sum[...] += jnp.sum(dn * scaled, axis=0, keepdims=True)
    d_gated = inv * gain * dn - gated * back
    d_normed[pl.ds(r0, L), :] = (d_gated * silu).astype(BF)
    proj[here, :CH] = (d_gated * mixer * (sig + silu * (1.0 - sig))).astype(BF)


def backward_block(
    b, first_len, proj, d_out, taps, shift, step_bias, rate_log, skip, y_in, states, small, heads,
    carry, late,
):
    upper = (iota2((L, L), 1) >= iota2((L, L), 0)).astype(BF)
    columns = head_columns()
    r0 = pl.multiple_of(b * L, L)
    rows = proj[pl.ds(r0, HALO + L), :]
    gate, xbc, conv, raw, step, log_decay, cum = block_front(
        rows, r0, first_len, taps, shift, step_bias, rate_log
    )
    sig = sigmoid(conv)
    act = conv * sig
    x = act[:, BC:]
    b_low = act[:, :STATE].astype(BF)
    c_low = act[:, STATE:BC].astype(BF)
    cum_rows = jnp.transpose(cum)
    scores = mm(c_low, b_low, ((1,), (1,)))
    step_wide = spread(step)
    scaled = x * step_wide
    scaled_low = scaled.astype(BF)
    decays = decay_weights(cum, cum_rows)

    y = y_in[pl.ds(r0, L), :]
    dy_low = d_out[pl.ds(r0, L), :]
    dy = dy_low.astype(F32)

    state = states[b]
    end_state = states[b + 1]
    d_state = carry[...]
    state_low = state.astype(BF)
    d_state_low = d_state.astype(BF)
    enter = jnp.exp(spread(cum))
    tail = jnp.exp(spread(cum[L - 1 : L] - cum))
    lane = iota2((L, 128), 1)
    d_scores = jnp.zeros((L, L), F32)
    weights = []
    for h in range(OWN):
        part = slice(128 * (h // 2), 128 * (h // 2) + 128)
        mine = (lane < HEAD_DIM) if h % 2 == 0 else (lane >= HEAD_DIM)
        d_weight = mm(
            dy_low[:, part],
            jnp.where(mine, scaled[:, part], 0.0).astype(BF),
            ((1,), (1,)),
        )
        d_scores = d_scores + d_weight * decays[h]
        weights.append((decays[h] * scores).astype(BF))
    d_scores_low = d_scores.astype(BF)
    d_scaled = pair_mix(weights, dy_low, ((0,), (0,)))
    d_scaled = d_scaled + tail * mm(b_low, d_state_low, ((1,), (1,)))
    enter_dy = (enter * dy).astype(BF)
    d_c = mm(d_scores_low, b_low) + mm(enter_dy, state_low)
    d_b = mm(d_scores_low, c_low, ((0,), (0,))) + mm((tail * scaled).astype(BF), d_state_low)

    ssm = y - skip * x
    d_cum = mm_right(
        dy_low.astype(F32) * ssm - scaled_low.astype(F32) * d_scaled, columns, 3
    )
    through = jnp.zeros((1, 128), F32)
    for piece in split(end_state * d_state, 3):
        through = through + jnp.sum(
            mm(piece, columns, ((0,), (0,))), axis=0, keepdims=True
        )
    d_cum = d_cum + jnp.where(iota2((L, 1), 0) == L - 1, through, 0.0)
    d_log = mm_left(upper, d_cum, 3)
    rate = jnp.exp(rate_log)
    d_step = mm_right(d_scaled * x, columns, 3) - rate * d_log
    d_raw = d_step * sigmoid(raw)
    d_x = d_scaled * step_wide + skip * dy

    carry[...] = head_rows(cum_rows, L - 1) * d_state + mm(enter_dy, c_low, ((0,), (0,)))

    d_act = jnp.concatenate([d_b, d_c, d_x], axis=1)
    d_conv = d_act * (sig + act * (1.0 - sig))
    row = r0 + iota2((L + 8, 1), 0)
    longer = jnp.concatenate([d_conv, late[...]], axis=0)
    late[...] = d_conv[:8]
    d_xbc = jnp.zeros((L, XBC), F32)
    for k in range(CONV):
        ahead = CONV - 1 - k
        masked = longer
        if ahead:
            masked = longer * tap_mask(row, first_len, ahead)
        d_xbc = d_xbc + taps[k : k + 1] * masked[ahead : ahead + L]
        small[k : k + 1, :] += jnp.sum(
            masked[:L] * xbc[HALO - ahead : HALO - ahead + L], axis=0, keepdims=True
        )
    small[4:5, :] += jnp.sum(d_conv, axis=0, keepdims=True)
    small[5:6, :CH] += jnp.sum(dy * x, axis=0, keepdims=True)
    heads[0:1, :] += jnp.sum(d_raw, axis=0, keepdims=True)
    heads[1:2, :] += jnp.sum(d_log * log_decay, axis=0, keepdims=True)
    proj[pl.ds(pl.multiple_of(HALO + b * L, 16), L), CH:] = jnp.concatenate(
        [d_xbc, d_raw], axis=1
    ).astype(BF)


def finish_kernel(
    mixed_in, grad_in, gates, tail, outs, packed, norm, mixed, grad, norm_grad, in_grad, conv_grad, bias_grad,
    dt_grad, rate_grad, skip_grad, gain_grad, out_grad, moved,
):
    copies = (
        pltpu.make_async_copy(mixed_in, mixed, moved.at[0]),
        pltpu.make_async_copy(grad_in, grad, moved.at[1]),
    )
    for copy in copies:
        copy.start()
    out_grad[0] = outs[...].astype(F32)
    in_grad[0, :, :INNER] = gates[...].astype(F32)
    for s in range(SHARDS):
        begin = INNER + CH * s
        in_grad[0, :, begin : begin + 128] = tail[0, :, BC + 128 * s : BC + 128 * s + 128].astype(F32)
        in_grad[0, :, begin + 128 : begin + CH] = tail[1, :, 256 * s : 256 * s + 256].astype(F32)
    in_grad[0, :, 2 * INNER : 2 * INNER + BC] = tail[0, :, :BC].astype(F32)
    in_grad[0, :, 2 * INNER + BC :] = tail[1, :, 2048 : 2048 + HEADS].astype(F32)
    parts = [packed[s] for s in range(SHARDS)]
    both = parts[0][:, :BC]
    for s in range(1, SHARDS):
        both = both + parts[s][:, :BC]
    conv_grad[0, :, INNER:] = both[:CONV]
    bias_grad[:, INNER:] = both[CONV : CONV + 1]
    heads = [jnp.zeros((8, 128), F32)] * 3
    for s in range(SHARDS):
        own = slice(CH * s, CH * s + CH)
        conv_grad[0, :, own] = parts[s][:CONV, BC:XBC]
        bias_grad[:, own] = parts[s][CONV : CONV + 1, BC:XBC]
        gain_grad[:, own] = parts[s][5:6, CH : 2 * CH]
        put = (iota2((128, 128), 1) == iota2((128, 128), 0) + s * OWN) & (iota2((128, 128), 0) < OWN)
        put_wide = iota2((CH, 128), 1) == iota2((CH, 128), 0) // HEAD_DIM + s * OWN
        rows = (
            (parts[s][5:6, 2 * CH : 2 * CH + 128], put),
            (parts[s][5:6, 2 * CH + 128 : 2 * CH + 256], put),
            (parts[s][5:6, :CH], put_wide),
        )
        for at, (row, to) in enumerate(rows):
            wide = jnp.broadcast_to(row, (8, row.shape[1]))
            heads[at] = heads[at] + mm_right(wide, to.astype(BF), 3)
    for at, ref in enumerate((dt_grad, rate_grad, skip_grad)):
        ref[...] = heads[at][0:1, :HEADS]
    total = norm[0]
    for s in range(1, SHARDS):
        total = total + norm[s]
    for at in range(MODEL // 128):
        norm_grad[:, 128 * at : 128 * at + 128] = total[at : at + 1]
    for copy in copies:
        copy.wait()


VM = pl.BlockSpec(memory_space=pltpu.VMEM)
SM = pl.BlockSpec(memory_space=pltpu.SMEM)
ANY = pl.BlockSpec(memory_space=pl.ANY)
LIMIT = 61 << 20


def local(
    resid,
    cotangent,
    first_length,
    norm_gain,
    in_weight,
    conv_weight,
    conv_bias,
    dt_bias,
    a_log,
    skip,
    gate_gain,
    out_weight,
):
    w = in_weight[0]
    narrow = jnp.pad(w[:, 2 * INNER :], ((0, 0), (0, 4 * 128 - BC - HEADS)))
    dma = pltpu.SemaphoreType.DMA
    outs = (
        ((TOK, MODEL), F32), ((TOK, MODEL), F32), ((ROWS, INNER), BF), ((2, ROWS, TAIL), BF),
        ((CH, MODEL), BF), ((SHARDS, 8, MODEL), F32), ((SHARDS, 16, 128), F32),
    )
    scratch = (
        ((GROUP, MODEL), BF), ((GROUP, MODEL), BF), ((2, MODEL, HALF), BF),
        ((HALO + GROUP, COLS), BF), ((GROUP, CH), F32), ((NB + 1, CH, STATE), F32), ((GROUP, CH), BF),
        ((SHARDS, 2, NB, L), F32), ((CH, STATE), F32), ((2, TOK, MODEL), F32), ((CONV, XBC), F32),
        ((1, XBC), F32),
        ((2, NB, L), F32), ((GROUP, CH), BF), ((1, CH), F32), ((8, MODEL), F32), ((8, XBC), F32),
        ((8, 128), F32),
        ((8, XBC), F32), ((7, TOK, MODEL), BF), ((7, TOK, MODEL), BF),
        ((3, QUARTER, CH), BF), ((CH, HALF_OUT), BF), ((HALF_OUT, CH), BF), ((3, 96, HALF_OUT), BF),
        ((3, QUARTER // 2, CH), BF), ((96, HALF_OUT), BF), ((QUARTER // 2, CH), BF),
        ((96, HALF_OUT), BF), ((QUARTER // 2, CH), BF),
        ((QUARTER, CH), BF),
        ((ROWS, INNER), BF), ((CH, MODEL), BF),
        ((QUARTER, CH), BF),
        ((SHARDS, PIECE, CH), BF), ((2, ROWS, TAIL), BF),
        ((2, 8, MODEL), F32), ((2, 8, MODEL), F32), ((4, 8, MODEL), F32), ((SHARDS, 8, MODEL), F32),
        ((16, 16, 128), F32), ((SHARDS, 16, 128), F32),
    )
    mixed, grad, gates, tail, out_grad, packed, norm = pl.pallas_call(
        layer_kernel,
        out_shape=tuple(jax.ShapeDtypeStruct(*shape) for shape in outs),
        in_specs=[SM, ANY, ANY, ANY, ANY] + [VM] * 8,
        out_specs=(ANY,) * 7,
        scratch_shapes=[pltpu.VMEM(*shape) for shape in scratch]
        + [dma((9,))] * 4 + [dma((SHARDS,))] * 2 + [dma((4,))] * 2 + [dma((1,))] * 2
        + [dma((SHARDS,))] * 2 + [dma((11,))] + [dma((8,))] * 4 + [dma((60,))] * 2 + [dma((23,))] * 2 + [dma((SHARDS,))] * 2
        + [pltpu.SemaphoreType.REGULAR] * 2,
        compiler_params=pltpu.CompilerParams(
            vmem_limit_bytes=LIMIT, collective_id=0, has_side_effects=True
        ),
    )(
        first_length, resid, cotangent, w, narrow, out_weight[0], norm_gain, conv_weight[0], conv_bias,
        dt_bias, a_log, skip, gate_gain,
    )
    wide = CONVCH
    shapes = (
        (TOK, MODEL), (TOK, MODEL), (1, MODEL), (1, ROWS, 2 * INNER + BC + HEADS), (1, CONV, wide), (1, wide),
        (1, HEADS), (1, HEADS), (1, HEADS), (1, INNER), (1, CH, MODEL),
    )
    return pl.pallas_call(
        finish_kernel,
        out_shape=tuple(jax.ShapeDtypeStruct(shape, F32) for shape in shapes),
        in_specs=[VM] * 7,
        out_specs=(ANY, ANY) + (VM,) * 9,
        scratch_shapes=[dma((2,))],
        compiler_params=pltpu.CompilerParams(vmem_limit_bytes=LIMIT),
    )(mixed, grad, gates, tail, out_grad, packed, norm)


def solution(mesh):
    rows = P(("rep", "shard"), None)
    weight = P(None, "shard", None)
    return jax.shard_map(
        local,
        mesh=mesh,
        in_specs=(rows, rows, P("rep"), P(), weight, P(), P(), P(), P(), P(), P(), weight),
        out_specs=(rows, rows, P(), weight, P(), P(), P(), P(), P(), P(), weight),
        check_vma=False,
    )
```

time: 632 us -> 258 us (0.41)
  waiting for transfers between devices: 288 us -> 0 us
  Pallas kernels: 168 us -> 255 us
  blocking collectives: 68.3 us -> 0 us
  matrix products: 37.9 us -> 0 us
  local copies, waits for them, and re-layouts: 27.3 us -> 1.63 us
  other arithmetic: 17.8 us -> 0 us
  between operations: 16.1 us -> 1.48 us
  starting transfers between devices: 6.9 us -> 0 us
    psum x2 -> x0, waiting for transfers between devices: 223 us -> none  [the longest x1 168 us: local(): in_grad, out_grad = lax.psum((in_share, out_part.astype(BF)), 'rep')]
    pallas_call x2, Pallas kernels: 168 us -> 255 us  [the longest x1 247 us: local(): pl.pallas_call(layer_kernel, out_shape=tuple((jax.ShapeDtypeStruct(*shape...]
    psum x1 -> x0, blocking collectives: 68.3 us -> none  [local(): lax.psum((conv_parts, per_head, gain_part, d_norm_gain[None]), ('rep', 's...]
    reduce_scatter x3 -> x0, waiting for transfers between devices: 41.6 us -> none  [the longest x1 41.6 us: local(): lax.psum_scatter(narrow_part, 'shard', scatter_dimension=0, tiled=True)]
    dot_general x4 -> x0, matrix products: 37.9 us -> none  [mm(): return lax.dot_general(a, b, (dims, ((), ())), preferred_element_type=F32)]
    all_to_all x1 -> x0, waiting for transfers between devices: 23.4 us -> none  [local(): wide_sum = lax.all_to_all(wide_part, 'shard', 0, 0).transpose(1, 0, 2)]
    broadcast_in_dim x3 -> x0, other arithmetic: 8.68 us -> none  [the longest x2 6.99 us: local(): in_grad.astype(F32)[None]]
    all_to_all x1 -> x0, starting transfers between devices: 6.47 us -> none  [local(): wide_sum = lax.all_to_all(wide_part, 'shard', 0, 0).transpose(1, 0, 2)]
  transfers between devices with their start and end apart: 6 -> 0, of which waited for: 4 -> 0; matrix products, arithmetic and copies ran while one was open for 8% -> 0% of each run, Pallas kernels for 0% -> 0%
where the time goes in v3:
time: 258 us
  Pallas kernels  255 us (99%)
    pallas_call x1, Pallas kernels, local(): pl.pallas_call(layer_kernel, out_shape=tuple((jax.ShapeDtypeStruct(*shape...  247 us
    pallas_call x1, Pallas kernels, local(): pl.pallas_call(finish_kernel, out_shape=tuple((jax.ShapeDtypeStruct(shape...  7.99 us

profile of v3, /device:TPU:1, one launch (start us, length us, event | category | flops | bytes accessed | tf_op | source)
XLA Modules:
  0.0 257.8 jit_solution(16721625700391091660)
XLA Ops:
  1.3 0.9 slice.4
  2.2 0.7 pad.4.narrow
  2.9 246.7 %shard_map.203 = (f32[256,1536]{1,0:T(8,128)}, f32[256,1536]{1,0:T(8,128)}, bf16[192,3072]{1,0:T(8,128)(2,1)}, bf16[2,192,2176]{2,1,0:T(8,128)(2,1)}, bf16[384,1...) custom-call(s32[1]{0:T(128)S(6)} %copy.23.first_ref, f32[256,1536]{1,0:T(8,128)} %resid.1, ...), custom_call_target="tpu_custom_call" | custom-call | tf_op jit(solution)/shard_map/pallas_call | solution.py:1227
  249.7 8.0 %shard_map.204 = (f32[256,1536]{1,0:T(8,128)}, f32[256,1536]{1,0:T(8,128)}, f32[1,1536]{1,0:T(1,128)}, f32[1,192,6448]{2,1,0:T(8,128)}, f32[1,4,3328]{2,1,0:T(4,...) custom-call(f32[256,1536]{1,0:T(8,128)} %get-tuple-element.18.mixed_, ...), custom_call_target="tpu_custom_call" | custom-call | tf_op jit(solution)/shard_map/pallas_call | solution.py:1248

commit v4 on v3

--- a/solution.py
+++ b/solution.py
@@ -29,7 +29,8 @@
 ROWS = MODEL // SHARDS
 QUARTER = SHARDS * PIECE
 TAIL = 8 * 256 + 128
-CHUNK = 16
+FRONT = 64
+CHUNK = 32
 HALF_OUT = MODEL // 2
 WIDE = 512
 OUT_PART = pl.ds(MODEL, CH)
@@ -201,16 +202,21 @@
 def enter(rep, me):
     barrier = pltpu.get_barrier_semaphore()
     peers = [(rep, lax.rem(me + o, SHARDS)) for o in range(1, SHARDS)]
-    peers += [(lax.rem(rep + o, 16), me) for o in range(1, 16)]
+    peers += [(lax.rem(rep + 4 * o, 16), me) for o in range(1, 4)]
+    peers += [sibling(rep, me), beside(rep, me)]
     for peer in peers:
         pl.semaphore_signal(barrier, inc=1, device_id=peer, device_id_type=MESH)
     return lambda: pl.semaphore_wait(barrier, len(peers))
 
 
-def block_rows(block, half=None):
-    if half is None:
-        return pl.ds(pl.multiple_of(block * TOK, TOK), TOK)
-    return pl.ds(pl.multiple_of(block * TOK + half, TOK // 2), TOK // 2)
+def block_rows(block, part=(0, TOK)):
+    begin, end = part
+    return pl.ds(pl.multiple_of(block * TOK + begin, 16), end - begin)
+
+
+FIRST, SECOND = (0, TOK // 2), (TOK // 2, TOK)
+EDGE = 48
+TOP, REST = (0, EDGE), (EDGE, TOK)
 
 
 class Gather:
@@ -218,7 +224,7 @@
         self.blocks, self.send, self.recv = blocks, send, recv
         self.rep, self.me, self.left, self.right, self.far, self.across = place_of()
 
-    def move(self, channel, block, to, rows=None):
+    def move(self, channel, block, to, rows=(0, TOK)):
         ref = self.blocks.at[block_rows(block, rows)]
         return pltpu.make_async_remote_copy(
             src_ref=ref,
@@ -235,12 +241,14 @@
             lambda: self.move(0, me, right),
             lambda: self.move(1, me, left),
             lambda: self.move(2, me, across),
-            lambda: self.move(3, left, right, 0),
-            lambda: self.move(4, right, left, TOK // 2),
-            lambda: self.move(5, across, right),
-            lambda: self.move(6, across, left),
-            lambda: self.move(7, self.far, across, 0),
-            lambda: self.move(8, self.far, across, TOK // 2),
+            lambda: self.move(3, left, right, FIRST),
+            lambda: self.move(4, right, left, SECOND),
+            lambda: self.move(5, across, right, REST),
+            lambda: self.move(6, across, left, REST),
+            lambda: self.move(7, self.far, across, FIRST),
+            lambda: self.move(8, self.far, across, SECOND),
+            lambda: self.move(9, left, across, TOP),
+            lambda: self.move(10, right, across, TOP),
         )[channel]()
 
     def incoming(self, channel):
@@ -249,12 +257,14 @@
             lambda: self.move(0, left, left),
             lambda: self.move(1, right, right),
             lambda: self.move(2, across, across),
-            lambda: self.move(3, far, left, 0),
-            lambda: self.move(4, far, right, TOK // 2),
-            lambda: self.move(5, other_side(left), left),
-            lambda: self.move(6, other_side(right), right),
-            lambda: self.move(7, other_side(far), across, 0),
-            lambda: self.move(8, other_side(far), across, TOK // 2),
+            lambda: self.move(3, far, left, FIRST),
+            lambda: self.move(4, far, right, SECOND),
+            lambda: self.move(5, other_side(left), left, REST),
+            lambda: self.move(6, other_side(right), right, REST),
+            lambda: self.move(7, other_side(far), across, FIRST),
+            lambda: self.move(8, other_side(far), across, SECOND),
+            lambda: self.move(9, other_side(left), across, TOP),
+            lambda: self.move(10, other_side(right), across, TOP),
         )[channel]()
 
     def start(self, *channels):
@@ -266,23 +276,27 @@
             self.incoming(channel).wait_recv()
 
     def sent(self):
-        for channel in range(9):
+        for channel in range(11):
             self.outgoing(channel).wait_send()
 
 
 class Scatter:
-    SLOTS = ((0, None), (1, None), (2, None), (3, 0), (3, TOK // 2), (4, None), (5, None), (6, None))
+    SLOTS = (
+        (0, (0, TOK)), (1, REST), (2, REST), (3, FIRST), (3, SECOND), (4, (0, TOK)), (5, (0, TOK)),
+        (6, (0, TOK)), (1, TOP), (2, TOP),
+    )
 
     def __init__(self, part, out, into, send, recv):
         self.part, self.out, self.into, self.send, self.recv = part, out, into, send, recv
         self.rep, self.me, self.left, self.right, self.far, self.across = place_of()
         self.to = (
             self.across, self.left, self.right, self.left, self.right, self.right, self.left, self.across,
+            self.across, self.across,
         )
 
     def copy(self, channel):
         slot, rows = self.SLOTS[channel]
-        at = (slot,) if rows is None else (slot, pl.ds(rows, TOK // 2))
+        at = (slot, pl.ds(rows[0], rows[1] - rows[0]))
         return pltpu.make_async_remote_copy(
             src_ref=self.out.at[at],
             dst_ref=self.into.at[at],
@@ -304,28 +318,44 @@
                 value = value + self.into[other, :, lanes].astype(F32)
             self.out[slot, :, lanes] = value.astype(BF)
 
+    def add(self, slot, into, rows):
+        rows = slice(*rows)
+        value = self.out[slot, rows].astype(F32)
+        for other in into:
+            value = value + self.into[other, rows].astype(F32)
+        self.out[slot, rows] = value.astype(BF)
+
     def leaf(self, slot):
         self.fill(slot, other_side((self.far, self.left, self.right)[slot]))
         self.copy(slot).start()
+        if slot:
+            self.copy(7 + slot).start()
 
     def middle(self):
         self.arrived(0)
         self.fill(3, self.far, 0)
         self.copy(3).start()
         self.copy(4).start()
+        self.fill(6, self.across)
         self.arrived(1, 2)
-        self.fill(6, self.across, 1, 2)
+        self.add(6, (1, 2), REST)
+
+    def cross(self):
         self.copy(7).start()
 
-    def last(self):
-        half = TOK // 2
+    def near(self):
         self.fill(4, self.right)
         self.fill(5, self.left)
+
+    def last(self):
+        self.arrived(8, 9)
+        self.add(4, (2,), TOP)
+        self.add(5, (1,), TOP)
         self.arrived(3, 4)
-        for slot, rows in ((4, slice(half, TOK)), (5, slice(0, half))):
-            value = self.out[slot, rows].astype(F32) + self.into[3, rows].astype(F32)
-            self.out[slot, rows] = value.astype(BF)
-            self.copy(1 + slot).start()
+        self.add(4, (3,), SECOND)
+        self.copy(5).start()
+        self.add(5, (3,), FIRST)
+        self.copy(6).start()
 
     def total(self, lanes):
         value = self.part(self.me, lanes)
@@ -334,7 +364,7 @@
         return value
 
     def sent(self):
-        for channel in range(8):
+        for channel in range(10):
             self.copy(channel).wait_send()
 
 
@@ -362,15 +392,15 @@
 def layer_kernel(
     first_ref, resid, cotangent, w_in, narrow, w_out, norm_gain, conv_weight, conv_bias, dt_bias,
     a_log, skip, gate_gain,
-    mixed_out, grad_out, gates_out, tail_out, outs_out, small_out, norm_out,
+    mixed_out, grad_out, gates_out, tail_out, outs_out, small_out,
     x_all, low_all, w_all, proj, y, states, d_normed, sums, carry, stage, taps, shift,
     totals, normed_out, gain_sum, norm_sum, small, heads, late, scatter_out, scatter_in,
     near_y, core_out, core_gate, near_out, near_gate, part_out, part_gate, side_out, side_gate,
     quarter, gates, outs,
     tail_swap, tail_pieces, tail,
-    packed, packed_in, packed_y, packed_all, norm_parts, norm_all,
+    packed, packed_in, packed_y, packed_all,
     x_send, x_recv, low_send, low_recv, piece_send, piece_recv, y_send, y_recv, core_send, core_recv,
-    sum_send, sum_recv, here, mix_send, mix_recv, grad_send, grad_recv, g_send, g_recv, norm_send, norm_recv, owner_send, owner_recv, free, core_free,
+    sum_send, sum_recv, here, mix_send, mix_recv, grad_send, grad_recv, g_send, g_recv, owner_send, owner_recv, free, core_free,
 ):
     rep, me, left, right, far, across = place_of()
     core = lax.rem(rep, 2)
@@ -385,13 +415,13 @@
     load_resid.wait()
 
     def norm_rows(at, unused):
-        rows = stage[0, pl.ds(pl.multiple_of(at * CHUNK, CHUNK), CHUNK), :]
+        rows = stage[0, pl.ds(pl.multiple_of(at * FRONT, FRONT), FRONT), :]
         scale = lax.rsqrt(jnp.mean(rows * rows, axis=1, keepdims=True) + epsilon)
-        own = pl.ds(pl.multiple_of(me * TOK + at * CHUNK, CHUNK), CHUNK)
+        own = pl.ds(pl.multiple_of(me * TOK + at * FRONT, FRONT), FRONT)
         x_all[own, :] = (rows * scale * norm_gain[...]).astype(BF)
         return unused
 
-    lax.fori_loop(0, TOK // CHUNK, norm_rows, 0)
+    lax.fori_loop(0, TOK // FRONT, norm_rows, 0)
     all_entered()
     gather_x = Gather(x_all, x_send, x_recv)
     gather_x.start(0, 1, 2)
@@ -446,9 +476,9 @@
                 device_id=(lax.rem(rep + 4 * o, 16), me), device_id_type=MESH,
             ).start()
     gather_x.arrived(0)
-    gather_x.start(3)
+    gather_x.start(3, 9)
     gather_x.arrived(1)
-    gather_x.start(4)
+    gather_x.start(4, 10)
     gather_x.arrived(2)
     gather_x.start(5, 6)
     gather_x.arrived(3)
@@ -486,10 +516,10 @@
 
     lax.fori_loop(side, side + 4, project, 0)
     gather_low.arrived(0)
-    gather_low.start(3)
+    gather_low.start(3, 9)
     gather_low.arrived(1)
-    gather_low.start(4)
-    gather_x.arrived(5, 6, 7, 8)
+    gather_low.start(4, 10)
+    gather_x.arrived(5, 6, 7, 8, 9, 10)
     lax.fori_loop(4 - side, 8 - side, project, 0)
 
     step_bias = own_heads(dt_bias[...], me)
@@ -524,8 +554,41 @@
         sums[me, 1, pl.ds(2 * at + 1, 1), :] = to_row(both[L:])
         return unused
 
+    def sum_copy(kind, o, slot, to):
+        ref = sums.at[slot, kind]
+        return pltpu.make_async_remote_copy(
+            src_ref=ref, dst_ref=ref, send_sem=sum_send.at[SHARDS * kind + o],
+            recv_sem=sum_recv.at[SHARDS * kind + o], device_id=(rep, to), device_id_type=MESH,
+        )
+
+    def start_sum(kind):
+        for o in range(1, SHARDS):
+            sum_copy(kind, o, me, lax.rem(me + o, SHARDS)).start()
+
+    def end_sum(kind):
+        for o in range(1, SHARDS):
+            source = lax.rem(me + SHARDS - o, SHARDS)
+            sum_copy(kind, o, source, source).wait_recv()
+        total = sums[0, kind]
+        for slot in range(1, SHARDS):
+            total = total + sums[slot, kind]
+        totals[kind] = total
+        for o in range(1, SHARDS):
+            sum_copy(kind, o, me, lax.rem(me + o, SHARDS)).wait_send()
+
+    def scale_out(b, unused):
+        scale_block(b, proj, y, totals, gain, normed_out)
+        return unused
+
+    def mixed_part(block, lanes):
+        return mm(normed_out[block_rows(block), :], w_out[:, lanes])
+
+    mix = Scatter(mixed_part, scatter_out, scatter_in, mix_send, mix_recv)
+    start_sum(0)
     lax.fori_loop(side, side + 4, normed, 0)
-    gather_low.arrived(5, 6)
+    end_sum(0)
+    lax.fori_loop(0, NB, scale_out, 0)
+    gather_low.arrived(5, 6, 9, 10)
 
     def normed_near(at, unused):
         return normed(other_side(side + lax.rem(me + at, 4)), unused)
@@ -533,24 +596,7 @@
     lax.fori_loop(3, 6, normed_near, 0)
     gather_low.arrived(7, 8)
     lax.fori_loop(6, 7, normed_near, 0)
-
-    def sum_copy(o, slot, to):
-        return pltpu.make_async_remote_copy(
-            src_ref=sums.at[slot], dst_ref=sums.at[slot], send_sem=sum_send.at[o],
-            recv_sem=sum_recv.at[o], device_id=(rep, to), device_id_type=MESH,
-        )
-
-    for o in range(1, SHARDS):
-        sum_copy(o, me, lax.rem(me + o, SHARDS)).start()
-    for o in range(1, SHARDS):
-        source = lax.rem(me + SHARDS - o, SHARDS)
-        sum_copy(o, source, source).wait_recv()
-    for o in range(1, SHARDS):
-        sum_copy(o, me, lax.rem(me + o, SHARDS)).wait_send()
-    total = sums[0]
-    for slot in range(1, SHARDS):
-        total = total + sums[slot]
-    totals[...] = total
+    start_sum(1)
 
     def send(index, src, dst, to):
         return pltpu.make_async_remote_copy(
@@ -571,23 +617,20 @@
     carry[...] = jnp.zeros_like(carry)
 
     def prepare(b, unused):
-        prepare_block(b, proj, y, d_normed, totals, gain, normed_out, gain_sum)
+        prepare_block(b, proj, y, d_normed, totals, gain, gain_sum)
         return unused
 
-    def mixed_part(block, lanes):
-        return mm(normed_out[block_rows(block), :], w_out[:, lanes])
-
-    mix = Scatter(mixed_part, scatter_out, scatter_in, mix_send, mix_recv)
-    def prepare_two(block):
-        lax.fori_loop(2 * block, 2 * block + 2, prepare, 0)
-
-    for slot, block in enumerate((far, left, right)):
-        prepare_two(other_side(block))
+    for slot in range(3):
         mix.leaf(slot)
-    prepare_two(across)
-    lax.fori_loop(2 * side, 2 * side + 8, prepare, 0)
-
     gather_low.sent()
+    def row_dots(at, part, weight):
+        dots = jnp.sum(part * weight.astype(F32), axis=1, keepdims=True)
+        for half in range(2):
+            lanes = pl.ds(pl.multiple_of(at * 256 + half * L, L), L)
+            norm_sum[0:1, lanes] += to_row(dots[half * L : half * L + L])
+
+    norm_sum[...] = jnp.zeros_like(norm_sum)
+
     def out_tile(at, unused):
         lanes = pl.ds(pl.multiple_of(at * 256, 256), 256)
         low = low_all[:, lanes]
@@ -597,7 +640,9 @@
     def gate_tile(at, unused):
         lanes = pl.ds(pl.multiple_of(at * 256, 256), 256)
         rows = x_all[:, lanes]
-        low_all[lanes, :CH] = mm(rows, proj[HALO:, :CH], ((0,), (0,))).astype(BF)
+        part = mm(rows, proj[HALO:, :CH], ((0,), (0,)))
+        low_all[lanes, :CH] = part.astype(BF)
+        row_dots(at, part, w_all[0, lanes, :CH])
         return unused
 
     def y_rows(block, y_at):
@@ -621,6 +666,8 @@
     )
     lax.fori_loop(0, MODEL // 256, out_tile, 0)
     core_copies[0].start()
+    end_sum(1)
+    lax.fori_loop(0, NB, prepare, 0)
     lax.fori_loop(0, MODEL // 256, gate_tile, 0)
     core_copies[1].start()
 
@@ -774,6 +821,7 @@
         @pl.when(at == 4)
         def hook_b():
             mix.middle()
+            mix.cross()
 
         @pl.when(at == 10)
         def hook_c():
@@ -781,6 +829,7 @@
 
         @pl.when(at == 9)
         def hook_d():
+            mix.near()
             mix.last()
 
         @pl.when(at == 13)
@@ -848,25 +897,14 @@
             send(50 + o, packed_all.at[source], packed_all.at[source], (rep, source)).wait()
         pltpu.make_async_copy(packed_all, small_out, here.at[9]).start()
 
-    def norm_copy(index, ref, to):
-        return pltpu.make_async_remote_copy(
-            src_ref=ref, dst_ref=ref, send_sem=norm_send.at[index], recv_sem=norm_recv.at[index],
-            device_id=to, device_id_type=MESH,
-        )
-
-    packed[0] = jnp.zeros_like(packed[0])
-    packed[0, :5, :XBC] = small[:5]
-    packed[0, 5:6, :CH] = small[5:6, :CH]
-    packed[0, 5:6, CH : 2 * CH] = gain_sum[...]
-    packed[0, 5:6, 2 * CH : 2 * CH + 128] = heads[0:1]
-    packed[0, 5:6, 2 * CH + 128 : 2 * CH + 256] = heads[1:2]
-    small_copy(0).start()
-
     def tail_tiles(which):
         def tile(at, unused):
             lanes = pl.ds(pl.multiple_of(at * 256, 256), 256)
             part = mm(x_all[:, lanes], proj[HALO:, part_columns(1 + which)], ((0,), (0,)))
             low_all[lanes, part_columns(1 + which)] = part.astype(BF)
+            first = jnp.concatenate([w_all[0, lanes, CH:], w_all[1, lanes, :128]], axis=1).astype(F32)
+            second = w_all[1, lanes, 128 : CH + 128].astype(F32)
+            row_dots(at, part, jnp.where(which == 0, first, second))
             return unused
 
         lax.fori_loop(0, MODEL // 256, tile, 0)
@@ -879,6 +917,14 @@
     pl.semaphore_wait(core_free, 1)
     core_copy.start()
     tail_tiles(core)
+    packed[0] = jnp.zeros_like(packed[0])
+    packed[0, :5, :XBC] = small[:5]
+    packed[0, 5:6, :CH] = small[5:6, :CH]
+    packed[0, 5:6, CH : 2 * CH] = gain_sum[...]
+    packed[0, 5:6, 2 * CH : 2 * CH + 128] = heads[0:1]
+    packed[0, 5:6, 2 * CH + 128 : 2 * CH + 256] = heads[1:2]
+    packed[0, 6:7, :] = norm_sum[0:1, :] / norm_gain[...]
+    small_copy(0).start()
     core_copy.wait()
 
     def add_core(at, unused):
@@ -894,7 +940,6 @@
             send(28 + o, src, near_y.at[o - 1, pl.ds(block * PIECE, PIECE)], y_peer(o)).start()
     small_first()
     d_in.middle()
-    to_sibling()
     for o in range(1, 4):
         send(28 + o, low_all.at[pl.ds(0, QUARTER), mine], near_y.at[o - 1], y_peer(o)).wait()
     for block in range(SHARDS):
@@ -906,13 +951,16 @@
     side_copy = send(32, quarter, tail_swap, beside(rep, me))
     side_copy.start()
     small_second()
-    d_in.last()
+    to_sibling()
+    d_in.near()
     side_copy.wait()
     quarter[...] = (quarter[...].astype(F32) + tail_swap[...].astype(F32)).astype(BF)
     for o in range(1, SHARDS):
         to = lax.rem(me + o, SHARDS)
         send(32 + o, quarter.at[own_quarter(to)], tail_pieces.at[me], (rep, to)).start()
     tail_pieces[me] = quarter[own_quarter(me), :]
+    d_in.cross()
+    d_in.last()
     small_third()
     early_done()
     for o in range(1, SHARDS):
@@ -944,13 +992,16 @@
         src = tail.at[core, own_piece]
         send(40 + o, src, src, y_peer(o)).start()
 
+    for o in range(1, 4):
+        src = tail.at[core, pl.ds(pl.multiple_of(y_of(4 - o) * PIECE, 16), PIECE)]
+        send(40 + o, src, src, y_peer(o)).wait()
+    last_copy = send(58, tail.at[core], tail.at[core], sibling(rep, me))
+    last_copy.start()
     small_last()
     d_in.arrived(5, 6, 7)
     for at in range(MODEL // CH):
         y[at * TOK : (at + 1) * TOK, :] = d_in.total(slice(at * CH, (at + 1) * CH))
     load_again.wait()
-    norm_sum[...] = jnp.zeros_like(norm_sum)
-
     def norm_back(at, unused):
         chunk = pl.ds(pl.multiple_of(at * CHUNK, CHUNK), CHUNK)
         rows = stage[0, chunk, :]
@@ -961,7 +1012,6 @@
         scale = lax.rsqrt(jnp.mean(rows * rows, axis=1, keepdims=True) + epsilon)
         unit = rows * scale
         d_unit = d_rows * norm_gain[...]
-        norm_sum[...] += jnp.sum((d_rows * unit).reshape(CHUNK // 8, 8, MODEL), axis=0)
         stage[1, chunk, :] += scale * (d_unit - unit * jnp.mean(d_unit * unit, axis=1, keepdims=True))
         return unused
 
@@ -969,38 +1019,10 @@
     store_grad = pltpu.make_async_copy(stage.at[1], grad_out, here.at[7])
     store_grad.start()
 
-    for at in range(MODEL // 128):
-        norm_parts[rep, at : at + 1, :] = jnp.sum(
-            norm_sum[:, 128 * at : 128 * at + 128], axis=0, keepdims=True
-        )
-    norm_parts[rep, MODEL // 128 :, :] = jnp.zeros((16 - MODEL // 128, 128), F32)
-    for o in range(1, 16):
-        to = lax.rem(rep + o, 16), me
-        norm_copy(o, norm_parts.at[rep], to).start()
-    for o in range(1, 16):
-        source = lax.rem(rep + 16 - o, 16)
-        norm_copy(o, norm_parts.at[source], (source, me)).wait()
-    total = norm_parts[0]
-    for at in range(1, 16):
-        total = total + norm_parts[at]
-    norm_all[me] = total
-    for o in range(1, SHARDS):
-        norm_copy(15 + o, norm_all.at[me], (rep, lax.rem(me + o, SHARDS))).start()
-
-    for o in range(1, 4):
-        src = tail.at[core, pl.ds(pl.multiple_of(y_of(4 - o) * PIECE, 16), PIECE)]
-        send(40 + o, src, src, y_peer(o)).wait()
-    last_copy = send(58, tail.at[core], tail.at[core], sibling(rep, me))
-    last_copy.start()
     send(58, tail.at[1 - core], tail.at[1 - core], sibling(rep, me)).wait_recv()
     last_copy.wait_send()
     store_tail = pltpu.make_async_copy(tail, tail_out, here.at[8])
     store_tail.start()
-    for o in range(1, SHARDS):
-        source = lax.rem(me + SHARDS - o, SHARDS)
-        norm_copy(15 + o, norm_all.at[source], (rep, source)).wait()
-    store_norm = pltpu.make_async_copy(norm_all, norm_out, here.at[4])
-    store_norm.start()
     d_in.sent()
     gather_x.sent()
     pltpu.make_async_copy(gates, gates_out, here.at[3]).wait()
@@ -1008,10 +1030,18 @@
     store_grad.wait()
     store_tail.wait()
     pltpu.make_async_copy(packed_all, small_out, here.at[9]).wait()
-    store_norm.wait()
-
-
-def prepare_block(b, proj, y, d_normed, totals, gain, normed_out, gain_sum):
+
+
+def scale_block(b, proj, y, totals, gain, normed_out):
+    r0 = pl.multiple_of(b * L, L)
+    gate = proj[pl.ds(pl.multiple_of(HALO + b * L, 16), L), :CH].astype(F32)
+    inv = to_column(lax.rsqrt(totals[0, pl.ds(b, 1), :] * (1.0 / INNER) + epsilon))
+    inv = jnp.concatenate([inv] * (CH // 128), axis=1)
+    gated = y[pl.ds(r0, L), :] * (gate * sigmoid(gate))
+    normed_out[pl.ds(r0, L), :] = (gated * inv * gain).astype(BF)
+
+
+def prepare_block(b, proj, y, d_normed, totals, gain, gain_sum):
     r0 = pl.multiple_of(b * L, L)
     here = pl.ds(pl.multiple_of(HALO + b * L, 16), L)
     gate = proj[here, :CH].astype(F32)
@@ -1025,7 +1055,6 @@
     back = jnp.concatenate([to_column(back)] * (CH // 128), axis=1)
     dn = d_normed[pl.ds(r0, L), :].astype(F32)
     scaled = gated * inv
-    normed_out[pl.ds(r0, L), :] = (scaled * gain).astype(BF)
     gain_sum[...] += jnp.sum(dn * scaled, axis=0, keepdims=True)
     d_gated = inv * gain * dn - gated * back
     d_normed[pl.ds(r0, L), :] = (d_gated * silu).astype(BF)
@@ -1129,7 +1158,7 @@
 
 
 def finish_kernel(
-    mixed_in, grad_in, gates, tail, outs, packed, norm, mixed, grad, norm_grad, in_grad, conv_grad, bias_grad,
+    mixed_in, grad_in, gates, tail, outs, packed, mixed, grad, norm_grad, in_grad, conv_grad, bias_grad,
     dt_grad, rate_grad, skip_grad, gain_grad, out_grad, moved,
 ):
     copies = (
@@ -1170,11 +1199,10 @@
             heads[at] = heads[at] + mm_right(wide, to.astype(BF), 3)
     for at, ref in enumerate((dt_grad, rate_grad, skip_grad)):
         ref[...] = heads[at][0:1, :HEADS]
-    total = norm[0]
+    total = parts[0][6:7]
     for s in range(1, SHARDS):
-        total = total + norm[s]
-    for at in range(MODEL // 128):
-        norm_grad[:, 128 * at : 128 * at + 128] = total[at : at + 1]
+        total = total + parts[s][6:7]
+    norm_grad[...] = total
     for copy in copies:
         copy.wait()
 
@@ -1204,7 +1232,7 @@
     dma = pltpu.SemaphoreType.DMA
     outs = (
         ((TOK, MODEL), F32), ((TOK, MODEL), F32), ((ROWS, INNER), BF), ((2, ROWS, TAIL), BF),
-        ((CH, MODEL), BF), ((SHARDS, 8, MODEL), F32), ((SHARDS, 16, 128), F32),
+        ((CH, MODEL), BF), ((SHARDS, 8, MODEL), F32),
     )
     scratch = (
         ((GROUP, MODEL), BF), ((GROUP, MODEL), BF), ((2, MODEL, HALF), BF),
@@ -1222,16 +1250,15 @@
         ((QUARTER, CH), BF),
         ((SHARDS, PIECE, CH), BF), ((2, ROWS, TAIL), BF),
         ((2, 8, MODEL), F32), ((2, 8, MODEL), F32), ((4, 8, MODEL), F32), ((SHARDS, 8, MODEL), F32),
-        ((16, 16, 128), F32), ((SHARDS, 16, 128), F32),
-    )
-    mixed, grad, gates, tail, out_grad, packed, norm = pl.pallas_call(
+    )
+    mixed, grad, gates, tail, out_grad, packed = pl.pallas_call(
         layer_kernel,
         out_shape=tuple(jax.ShapeDtypeStruct(*shape) for shape in outs),
         in_specs=[SM, ANY, ANY, ANY, ANY] + [VM] * 8,
-        out_specs=(ANY,) * 7,
+        out_specs=(ANY,) * 6,
         scratch_shapes=[pltpu.VMEM(*shape) for shape in scratch]
-        + [dma((9,))] * 4 + [dma((SHARDS,))] * 2 + [dma((4,))] * 2 + [dma((1,))] * 2
-        + [dma((SHARDS,))] * 2 + [dma((11,))] + [dma((8,))] * 4 + [dma((60,))] * 2 + [dma((23,))] * 2 + [dma((SHARDS,))] * 2
+        + [dma((11,))] * 4 + [dma((SHARDS,))] * 2 + [dma((4,))] * 2 + [dma((1,))] * 2
+        + [dma((2 * SHARDS,))] * 2 + [dma((11,))] + [dma((10,))] * 4 + [dma((60,))] * 2 + [dma((SHARDS,))] * 2
         + [pltpu.SemaphoreType.REGULAR] * 2,
         compiler_params=pltpu.CompilerParams(
             vmem_limit_bytes=LIMIT, collective_id=0, has_side_effects=True
@@ -1248,11 +1275,11 @@
     return pl.pallas_call(
         finish_kernel,
         out_shape=tuple(jax.ShapeDtypeStruct(shape, F32) for shape in shapes),
-        in_specs=[VM] * 7,
+        in_specs=[VM] * 6,
         out_specs=(ANY, ANY) + (VM,) * 9,
         scratch_shapes=[dma((2,))],
         compiler_params=pltpu.CompilerParams(vmem_limit_bytes=LIMIT),
-    )(mixed, grad, gates, tail, out_grad, packed, norm)
+    )(mixed, grad, gates, tail, out_grad, packed)
 
 
 def solution(mesh):

time: 258 us -> 249 us (0.965); the launches traced: 258 us -> 244 us
  Pallas kernels: 255 us -> 241 us
    pallas_call x1, Pallas kernels: 247 us -> 233 us  [local(): pl.pallas_call(layer_kernel, out_shape=tuple((jax.ShapeDtypeStruct(*shape...]
where the time goes in v4:
time: 249 us; the launch traced here: 244 us
  Pallas kernels  241 us (97%)
    pallas_call x1, Pallas kernels, local(): pl.pallas_call(layer_kernel, out_shape=tuple((jax.ShapeDtypeStruct(*shape...  233 us
    pallas_call x1, Pallas kernels, local(): pl.pallas_call(finish_kernel, out_shape=tuple((jax.ShapeDtypeStruct(shape...  7.9 us

profile of v4, /device:TPU:1, one launch (start us, length us, event | category | flops | bytes accessed | tf_op | source)
XLA Modules:
  0.0 244.1 jit_solution(15913937432063540430)
XLA Ops:
  1.3 0.9 slice.4
  2.2 0.7 pad.4.narrow
  2.9 233.1 %shard_map.203 = (f32[256,1536]{1,0:T(8,128)}, f32[256,1536]{1,0:T(8,128)}, bf16[192,3072]{1,0:T(8,128)(2,1)}, bf16[2,192,2176]{2,1,0:T(8,128)(2,1)}, bf16[384,1536]{1,0:T(8,128)(2,1)}, /*index=5*/f32[8,8,1536]{2,1,0:T(8,128)}) custom-call(s32[1]{0:T(128)S(6)} %copy.23.first_ref, f32[256,1536]{1,0:T(8,128)} %resid.1, f32[256,1536]{1,0:T(8,128)} %cotangent.1, ...), custom_call_target="tpu_custom_call" | custom-call | tf_op jit(solution)/shard_map/pallas_call | solution.py:1254
  236.1 7.9 %shard_map.204 = (f32[256,1536]{1,0:T(8,128)}, f32[256,1536]{1,0:T(8,128)}, f32[1,1536]{1,0:T(1,128)}, f32[1,192,6448]{2,1,0:T(8,128)}, f32[1,4,3328]{2,1,0:T(4,...) custom-call(f32[256,1536]{1,0:T(8,128)} %get-tuple-element.17.mixed_, ...), custom_call_target="tpu_custom_call" | custom-call | tf_op jit(solution)/shard_map/pallas_call | solution.py:1275

commit v5 on v4

--- a/solution.py
+++ b/solution.py
@@ -28,7 +28,8 @@
 MESH = pl.DeviceIdType.MESH
 ROWS = MODEL // SHARDS
 QUARTER = SHARDS * PIECE
-TAIL = 8 * 256 + 128
+TAIL_WIDTH = (2 * 128 + 8 * 128, 8 * 256 + 128)
+TAIL = max(TAIL_WIDTH)
 FRONT = 64
 CHUNK = 32
 HALF_OUT = MODEL // 2
@@ -113,7 +114,7 @@
 
 
 def sigmoid(v):
-    return 1.0 / (1.0 + jnp.exp(-v))
+    return 0.5 * jnp.tanh(0.5 * v) + 0.5
 
 
 def pair_mix(weights, value, dims=((1,), (0,))):
@@ -166,8 +167,8 @@
     state = carry[...]
     states[b] = state
     y = pair_mix(weights, scaled_low)
-    y = y + jnp.exp(spread(cum)) * mm(c_low, state.astype(BF), ((1,), (1,)))
-    tail = jnp.exp(spread(cum[L - 1 : L] - cum))
+    y = y + spread(jnp.exp(cum)) * mm(c_low, state.astype(BF), ((1,), (1,)))
+    tail = spread(jnp.exp(cum[L - 1 : L] - cum))
     carry[...] = head_rows(cum_rows, L - 1) * state + mm(
         (tail * scaled).astype(BF), b_low, ((0,), (0,))
     )
@@ -818,7 +819,7 @@
         def hook_a():
             core_sum()
 
-        @pl.when(at == 4)
+        @pl.when(at == 3)
         def hook_b():
             mix.middle()
             mix.cross()
@@ -827,7 +828,7 @@
         def hook_c():
             y_sum()
 
-        @pl.when(at == 9)
+        @pl.when(at == 8)
         def hook_d():
             mix.near()
             mix.last()
@@ -861,8 +862,7 @@
         pl.semaphore_signal(free, inc=1, device_id=(rep, peer), device_id_type=MESH)
     pl.semaphore_wait(free, 3)
     d_in = Scatter(d_in_part, scatter_out, scatter_in, grad_send, grad_recv)
-    for slot in range(3):
-        d_in.leaf(slot)
+    d_in.leaf(0)
     store_mixed.wait()
     load_again = pltpu.make_async_copy(cotangent, stage.at[1], here.at[6])
     load_again.start()
@@ -916,6 +916,8 @@
     core_copy = send(28, low_all.at[pl.ds(0, MODEL), part_columns(2 - core)], received, sibling(rep, me))
     pl.semaphore_wait(core_free, 1)
     core_copy.start()
+    d_in.leaf(1)
+    d_in.leaf(2)
     tail_tiles(core)
     packed[0] = jnp.zeros_like(packed[0])
     packed[0, :5, :XBC] = small[:5]
@@ -940,6 +942,7 @@
             send(28 + o, src, near_y.at[o - 1, pl.ds(block * PIECE, PIECE)], y_peer(o)).start()
     small_first()
     d_in.middle()
+    d_in.near()
     for o in range(1, 4):
         send(28 + o, low_all.at[pl.ds(0, QUARTER), mine], near_y.at[o - 1], y_peer(o)).wait()
     for block in range(SHARDS):
@@ -952,7 +955,6 @@
     side_copy.start()
     small_second()
     to_sibling()
-    d_in.near()
     side_copy.wait()
     quarter[...] = (quarter[...].astype(F32) + tail_swap[...].astype(F32)).astype(BF)
     for o in range(1, SHARDS):
@@ -975,7 +977,6 @@
         tail[0, own_piece, :BC] = total.astype(BF)
         for block in range(SHARDS):
             tail[0, own_piece, BC + 128 * block : BC + 128 * block + 128] = tail_pieces[block, :, BC:]
-        tail[0, own_piece, BC + 1024 :] = jnp.zeros((PIECE, TAIL - BC - 1024), BF)
 
     @pl.when(core == 1)
     def assemble_second():
@@ -988,19 +989,43 @@
             total = total + mm(tail_pieces[block, :, 256:], put.astype(BF))
         tail[1, own_piece, 2048:] = total.astype(BF)
 
-    for o in range(1, 4):
-        src = tail.at[core, own_piece]
-        send(40 + o, src, src, y_peer(o)).start()
-
-    for o in range(1, 4):
-        src = tail.at[core, pl.ds(pl.multiple_of(y_of(4 - o) * PIECE, 16), PIECE)]
-        send(40 + o, src, src, y_peer(o)).wait()
-    last_copy = send(58, tail.at[core], tail.at[core], sibling(rep, me))
-    last_copy.start()
+    def tail_piece(which, y_at):
+        rows = pl.ds(pl.multiple_of(y_at * PIECE, 16), PIECE)
+        return tail.at[which, rows, pl.ds(0, TAIL_WIDTH[which])]
+
+    def tail_half(which):
+        return tail.at[which, :, pl.ds(0, TAIL_WIDTH[which])]
+
+    def each_core(act):
+        for which in range(2):
+
+            @pl.when(core == which)
+            def mine_only():
+                act(which)
+
+    def spread_tail(which):
+        for o in range(1, 4):
+            src = tail_piece(which, along_y)
+            send(40 + o, src, src, y_peer(o)).start()
+
+    def swap_tail(which):
+        for o in range(1, 4):
+            src = tail_piece(which, y_of(4 - o))
+            send(40 + o, src, tail_piece(which, along_y), y_peer(o)).wait()
+        send(58, tail_half(which), tail_half(which), sibling(rep, me)).start()
+
+    def end_tail(which):
+        other = tail_half(1 - which)
+        send(58, other, other, sibling(rep, me)).wait_recv()
+        send(58, tail_half(which), tail_half(which), sibling(rep, me)).wait_send()
+
+    each_core(spread_tail)
+    for at in range(MODEL // CH):
+        y[at * TOK : (at + 1) * TOK, :] = d_in.part(me, slice(at * CH, (at + 1) * CH))
+
+    each_core(swap_tail)
     small_last()
     d_in.arrived(5, 6, 7)
-    for at in range(MODEL // CH):
-        y[at * TOK : (at + 1) * TOK, :] = d_in.total(slice(at * CH, (at + 1) * CH))
     load_again.wait()
     def norm_back(at, unused):
         chunk = pl.ds(pl.multiple_of(at * CHUNK, CHUNK), CHUNK)
@@ -1009,6 +1034,8 @@
             y[pl.ds(pl.multiple_of(k * TOK + at * CHUNK, CHUNK), CHUNK), :] for k in range(MODEL // CH)
         ]
         d_rows = jnp.concatenate(pieces, axis=1)
+        for slot in (4, 5, 6):
+            d_rows = d_rows + scatter_in[slot, chunk, :].astype(F32)
         scale = lax.rsqrt(jnp.mean(rows * rows, axis=1, keepdims=True) + epsilon)
         unit = rows * scale
         d_unit = d_rows * norm_gain[...]
@@ -1019,8 +1046,7 @@
     store_grad = pltpu.make_async_copy(stage.at[1], grad_out, here.at[7])
     store_grad.start()
 
-    send(58, tail.at[1 - core], tail.at[1 - core], sibling(rep, me)).wait_recv()
-    last_copy.wait_send()
+    each_core(end_tail)
     store_tail = pltpu.make_async_copy(tail, tail_out, here.at[8])
     store_tail.start()
     d_in.sent()
@@ -1093,8 +1119,8 @@
     d_state = carry[...]
     state_low = state.astype(BF)
     d_state_low = d_state.astype(BF)
-    enter = jnp.exp(spread(cum))
-    tail = jnp.exp(spread(cum[L - 1 : L] - cum))
+    enter = spread(jnp.exp(cum))
+    tail = spread(jnp.exp(cum[L - 1 : L] - cum))
     lane = iota2((L, 128), 1)
     d_scores = jnp.zeros((L, L), F32)
     weights = []
@@ -1116,18 +1142,20 @@
     d_b = mm(d_scores_low, c_low, ((0,), (0,))) + mm((tail * scaled).astype(BF), d_state_low)
 
     ssm = y - skip * x
-    d_cum = mm_right(
-        dy_low.astype(F32) * ssm - scaled_low.astype(F32) * d_scaled, columns, 3
-    )
+    pieces = split(dy_low.astype(F32) * ssm - scaled_low.astype(F32) * d_scaled, 2)
+    pieces += split(d_scaled * x, 2)
+    sums = mm(jnp.concatenate(pieces, axis=0), columns)
+    d_cum = sums[:L] + sums[L : 2 * L]
+    inner = end_state * d_state
+    heads_lane = iota2((1, 128), 1)
     through = jnp.zeros((1, 128), F32)
-    for piece in split(end_state * d_state, 3):
-        through = through + jnp.sum(
-            mm(piece, columns, ((0,), (0,))), axis=0, keepdims=True
-        )
+    for h in range(OWN):
+        total = jnp.sum(inner[HEAD_DIM * h : HEAD_DIM * h + HEAD_DIM], axis=0, keepdims=True)
+        total = jnp.sum(total, axis=1, keepdims=True)
+        through = through + jnp.where(heads_lane == h, total, 0.0)
     d_cum = d_cum + jnp.where(iota2((L, 1), 0) == L - 1, through, 0.0)
-    d_log = mm_left(upper, d_cum, 3)
-    rate = jnp.exp(rate_log)
-    d_step = mm_right(d_scaled * x, columns, 3) - rate * d_log
+    d_log = mm_left(upper, d_cum, 2)
+    d_step = sums[2 * L : 3 * L] + sums[3 * L :] - jnp.exp(rate_log) * d_log
     d_raw = d_step * sigmoid(raw)
     d_x = d_scaled * step_wide + skip * dy
 
@@ -1158,23 +1186,43 @@
 
 
 def finish_kernel(
-    mixed_in, grad_in, gates, tail, outs, packed, mixed, grad, norm_grad, in_grad, conv_grad, bias_grad,
-    dt_grad, rate_grad, skip_grad, gain_grad, out_grad, moved,
+    mixed_in, grad_in, gates_in, tail_in, outs_in, packed, mixed, grad, norm_grad, in_grad, conv_grad, bias_grad,
+    dt_grad, rate_grad, skip_grad, gain_grad, out_grad,
+    mixed_here, grad_here, gates, tail, outs, in_here, out_here, into, out,
 ):
-    copies = (
-        pltpu.make_async_copy(mixed_in, mixed, moved.at[0]),
-        pltpu.make_async_copy(grad_in, grad, moved.at[1]),
-    )
-    for copy in copies:
-        copy.start()
-    out_grad[0] = outs[...].astype(F32)
-    in_grad[0, :, :INNER] = gates[...].astype(F32)
-    for s in range(SHARDS):
-        begin = INNER + CH * s
-        in_grad[0, :, begin : begin + 128] = tail[0, :, BC + 128 * s : BC + 128 * s + 128].astype(F32)
-        in_grad[0, :, begin + 128 : begin + CH] = tail[1, :, 256 * s : 256 * s + 256].astype(F32)
-    in_grad[0, :, 2 * INNER : 2 * INNER + BC] = tail[0, :, :BC].astype(F32)
-    in_grad[0, :, 2 * INNER + BC :] = tail[1, :, 2048 : 2048 + HEADS].astype(F32)
+    loads = [
+        pltpu.make_async_copy(src, dst, into.at[at])
+        for at, (src, dst) in enumerate(
+            ((outs_in, outs), (gates_in, gates), (tail_in, tail), (mixed_in, mixed_here), (grad_in, grad_here))
+        )
+    ]
+    for load in loads:
+        load.start()
+    stores = []
+
+    def store(src, dst):
+        stores.append(pltpu.make_async_copy(src, dst, out.at[len(stores)]))
+        stores[-1].start()
+
+    loads[0].wait()
+    out_here[...] = outs[...].astype(F32)
+    store(out_here, out_grad.at[0])
+    loads[1].wait()
+    loads[2].wait()
+    for chunk in range(0, ROWS, PIECE):
+        rows = slice(chunk, chunk + PIECE)
+        in_here[rows, :INNER] = gates[rows, :].astype(F32)
+        for s in range(SHARDS):
+            begin = INNER + CH * s
+            in_here[rows, begin : begin + 128] = tail[0, rows, BC + 128 * s : BC + 128 * s + 128].astype(F32)
+            in_here[rows, begin + 128 : begin + CH] = tail[1, rows, 256 * s : 256 * s + 256].astype(F32)
+        in_here[rows, 2 * INNER : 2 * INNER + BC] = tail[0, rows, :BC].astype(F32)
+        in_here[rows, 2 * INNER + BC :] = tail[1, rows, 2048 : 2048 + HEADS].astype(F32)
+        store(in_here.at[pl.ds(chunk, PIECE)], in_grad.at[0, pl.ds(chunk, PIECE)])
+    loads[3].wait()
+    store(mixed_here, mixed)
+    loads[4].wait()
+    store(grad_here, grad)
     parts = [packed[s] for s in range(SHARDS)]
     both = parts[0][:, :BC]
     for s in range(1, SHARDS):
@@ -1203,7 +1251,7 @@
     for s in range(1, SHARDS):
         total = total + parts[s][6:7]
     norm_grad[...] = total
-    for copy in copies:
+    for copy in stores:
         copy.wait()
 
 
@@ -1275,9 +1323,13 @@
     return pl.pallas_call(
         finish_kernel,
         out_shape=tuple(jax.ShapeDtypeStruct(shape, F32) for shape in shapes),
-        in_specs=[VM] * 6,
-        out_specs=(ANY, ANY) + (VM,) * 9,
-        scratch_shapes=[dma((2,))],
+        in_specs=[ANY] * 5 + [VM],
+        out_specs=(ANY, ANY, VM, ANY) + (VM,) * 6 + (ANY,),
+        scratch_shapes=[
+            pltpu.VMEM((TOK, MODEL), F32), pltpu.VMEM((TOK, MODEL), F32), pltpu.VMEM((ROWS, INNER), BF),
+            pltpu.VMEM((2, ROWS, TAIL), BF), pltpu.VMEM((CH, MODEL), BF),
+            pltpu.VMEM((ROWS, 2 * INNER + BC + HEADS), F32), pltpu.VMEM((CH, MODEL), F32), dma((5,)), dma((7,)),
+        ],
         compiler_params=pltpu.CompilerParams(vmem_limit_bytes=LIMIT),
     )(mixed, grad, gates, tail, out_grad, packed)
 

time: 249 us -> 244 us (0.980)
  Pallas kernels: 241 us -> 237 us
    pallas_call x1, Pallas kernels: 233 us -> 229 us  [local(): pl.pallas_call(layer_kernel, out_shape=tuple((jax.ShapeDtypeStruct(*shape...]
where the time goes in v5:
time: 244 us; the launch traced here: 240 us
  Pallas kernels  237 us (97%)
    pallas_call x1, Pallas kernels, local(): pl.pallas_call(layer_kernel, out_shape=tuple((jax.ShapeDtypeStruct(*shape...  229 us
    pallas_call x1, Pallas kernels, local(): pl.pallas_call(finish_kernel, out_shape=tuple((jax.ShapeDtypeStruct(shape...  7.68 us

profile of v5, /device:TPU:1, one launch (start us, length us, event | category | flops | bytes accessed | tf_op | source)
XLA Modules:
  0.0 240.2 jit_solution(14639778789222329211)
XLA Ops:
  1.3 0.9 slice.4
  2.2 0.7 pad.4.narrow
  2.9 229.4 %shard_map.203 = (f32[256,1536]{1,0:T(8,128)}, f32[256,1536]{1,0:T(8,128)}, bf16[192,3072]{1,0:T(8,128)(2,1)}, bf16[2,192,2176]{2,1,0:T(8,128)(2,1)}, bf16[384,1536]{1,0:T(8,128)(2,1)}, /*index=5*/f32[8,8,1536]{2,1,0:T(8,128)}) custom-call(s32[1]{0:T(128)S(6)} %copy.23.first_ref, f32[256,1536]{1,0:T(8,128)} %resid.1, f32[256,1536]{1,0:T(8,128)} %cotangent.1, ...), custom_call_target="tpu_custom_call" | custom-call | tf_op jit(solution)/shard_map/pallas_call | solution.py:1302
  232.3 7.7 %shard_map.204 = (f32[256,1536]{1,0:T(8,128)}, f32[256,1536]{1,0:T(8,128)}, f32[1,1536]{1,0:T(1,128)}, f32[1,192,6448]{2,1,0:T(8,128)}, f32[1,4,3328]{2,1,0:T(4,...) custom-call(f32[256,1536]{1,0:T(8,128)} %get-tuple-element.17.mixed_, ...), custom_call_target="tpu_custom_call" | custom-call | tf_op jit(solution)/shard_map/pallas_call | solution.py:1323

commit v6 on v5

--- a/solution.py
+++ b/solution.py
@@ -862,7 +862,8 @@
         pl.semaphore_signal(free, inc=1, device_id=(rep, peer), device_id_type=MESH)
     pl.semaphore_wait(free, 3)
     d_in = Scatter(d_in_part, scatter_out, scatter_in, grad_send, grad_recv)
-    d_in.leaf(0)
+    for slot in range(3):
+        d_in.leaf(slot)
     store_mixed.wait()
     load_again = pltpu.make_async_copy(cotangent, stage.at[1], here.at[6])
     load_again.start()
@@ -916,8 +917,6 @@
     core_copy = send(28, low_all.at[pl.ds(0, MODEL), part_columns(2 - core)], received, sibling(rep, me))
     pl.semaphore_wait(core_free, 1)
     core_copy.start()
-    d_in.leaf(1)
-    d_in.leaf(2)
     tail_tiles(core)
     packed[0] = jnp.zeros_like(packed[0])
     packed[0, :5, :XBC] = small[:5]
@@ -1276,7 +1275,7 @@
     out_weight,
 ):
     w = in_weight[0]
-    narrow = jnp.pad(w[:, 2 * INNER :], ((0, 0), (0, 4 * 128 - BC - HEADS)))
+    narrow = lax.pad(w, jnp.zeros((), BF), ((0, 0, 0), (-2 * INNER, 4 * 128 - BC - HEADS, 0)))
     dma = pltpu.SemaphoreType.DMA
     outs = (
         ((TOK, MODEL), F32), ((TOK, MODEL), F32), ((ROWS, INNER), BF), ((2, ROWS, TAIL), BF),

time: 244 us -> 244 us (level)
  no operation moved by 1% of the time
where the time goes in v6:
time: 244 us; the launch traced here: 240 us
  Pallas kernels  237 us (97%)
    pallas_call x1, Pallas kernels, local(): pl.pallas_call(layer_kernel, out_shape=tuple((jax.ShapeDtypeStruct(*shape...  229 us
    pallas_call x1, Pallas kernels, local(): pl.pallas_call(finish_kernel, out_shape=tuple((jax.ShapeDtypeStruct(shape...  7.68 us

profile of v6, /device:TPU:1, one launch (start us, length us, event | category | flops | bytes accessed | tf_op | source)
XLA Modules:
  0.0 240.0 jit_solution(4151025197148489454)
XLA Ops:
  1.3 1.6 pad_slice_fusion.narrow
  2.9 229.2 %shard_map.203 = (f32[256,1536]{1,0:T(8,128)}, f32[256,1536]{1,0:T(8,128)}, bf16[192,3072]{1,0:T(8,128)(2,1)}, bf16[2,192,2176]{2,1,0:T(8,128)(2,1)}, bf16[384,1536]{1,0:T(8,128)(2,1)}, /*index=5*/f32[8,8,1536]{2,1,0:T(8,128)}) custom-call(s32[1]{0:T(128)S(6)} %copy.23.first_ref, f32[256,1536]{1,0:T(8,128)} %resid.1, f32[256,1536]{1,0:T(8,128)} %cotangent.1, ...), custom_call_target="tpu_custom_call" | custom-call | tf_op jit(solution)/shard_map/pallas_call | solution.py:1301
  232.1 7.7 %shard_map.204 = (f32[256,1536]{1,0:T(8,128)}, f32[256,1536]{1,0:T(8,128)}, f32[1,1536]{1,0:T(1,128)}, f32[1,192,6448]{2,1,0:T(8,128)}, f32[1,4,3328]{2,1,0:T(4,...) custom-call(f32[256,1536]{1,0:T(8,128)} %get-tuple-element.17.mixed_, ...), custom_call_target="tpu_custom_call" | custom-call | tf_op jit(solution)/shard_map/pallas_call | solution.py:1322
